TPU v7x, 512 devices: a whole 4x4x16 slice. The times are simulated.
512 devices in a mesh: tm: 64 (over y, z), space: 8 (over x, core).
Axes of the slice: x: 4, y: 4, z: 16, core: 2. Of those that a mesh axis runs over, the one named last changes fastest.
Arguments:
- initial: float32 [4, 65536], P(None, 'space'), may hold values from -6 to 6
- guess: float32 [64, 4, 65536], P('tm', None, 'space'), may hold values from -6 to 6
- speeds: float32 [65536], P('space'), may hold values from 0.02 to 0.5
- flags: int32 [65536], P('space'), may hold values 0 or 1
Outputs:
- corrected: float32 [64, 4, 65536], P('tm', None, 'space')
All inputs are finite; a program needn't handle non-finite values. No bound on the sum of `flags` on one device may be relied on, other than what follows from the above.
Results may differ from a plain program's by a relative error of at most 0.0003.
Values sent between devices are 32-bit elements; how exact they have to be, the bound alone decides.
No kernel may reach another device: no remote copies, remote signals or barrier semaphores. Data moves between devices by JAX's collectives and lax.ppermute only.
A program may use at most 128 MiB of HBM per device.

v0:
```python
import jax
import jax.numpy as jnp
import numpy as np
from jax import lax
from jax.sharding import PartitionSpec as P

STEPS = 8


viscosity = 0.02
penalty = 10.0
step_size = 0.015625
jacobian = 8.0


def passed_along(block, axis, distance):
    devices = range(lax.axis_size(axis))
    route = [(i - distance, i) for i in devices if i - distance in devices]
    return lax.ppermute(block, axis, route)


def with_halo(cells, sides, width):
    for axis, dim in sides:
        count = lax.axis_size(axis)
        ends = count - 1
        head = lax.slice_in_dim(cells, 0, width, axis=dim)
        tail = lax.slice_in_dim(cells, cells.shape[dim] - width, cells.shape[dim], axis=dim)
        cells = jnp.concatenate(
            [
                lax.ppermute(tail, axis, [(i, (i + 1) % count) for i in range(ends)]),
                cells,
                lax.ppermute(head, axis, [((i + 1) % count, i) for i in range(ends)]),
            ],
            axis=dim,
        )
    return cells


def basis_tables(count):
    order = np.arange(count)
    right_vals = np.ones(count)
    left_vals = (-1.0) ** order
    right_slope = order * (order + 1) / 2.0
    left_slope = -left_vals * right_slope
    inv_mass = (2.0 * order + 1.0) / 2.0
    row_index = order[:, None]
    col_index = order[None, :]
    odd_sum = (row_index + col_index) % 2
    advect = np.where((row_index > col_index) & (odd_sum == 1), 2.0, 0.0)
    lesser = np.minimum(row_index, col_index)
    stiffness = np.where(odd_sum == 0, lesser * (lesser + 1.0), 0.0)
    return (right_vals, left_vals, right_slope, left_slope, inv_mass, advect, stiffness)


def column(values, dtype):
    return jnp.asarray(values, dtype)[:, None]


def multiply(table, field):
    return jnp.einsum(
        "ij,je->ie", jnp.asarray(table, field.dtype), field, precision=lax.Precision.HIGHEST
    )


def spatial_rhs(padded, speed_pad, open_pad):
    dtype = padded.dtype
    right_vals, left_vals, right_slope, left_slope, inv_mass, advect, stiffness = basis_tables(
        padded.shape[0]
    )
    trace_r = jnp.sum(column(right_vals, dtype) * padded, 0)
    trace_l = jnp.sum(column(left_vals, dtype) * padded, 0)
    slope_r = jnp.sum(column(right_slope, dtype) * padded, 0)
    slope_l = jnp.sum(column(left_slope, dtype) * padded, 0)
    jumps = trace_r[:-1] - trace_l[1:]
    means = 0.5 * (slope_r[:-1] + slope_l[1:])
    gates = open_pad[1:]
    inflow = speed_pad[:-1] * trace_r[:-1] * gates
    center = padded[:, 1:-1]
    speeds = speed_pad[1:-1]
    volume = speeds * multiply(advect, center) - column(right_vals, dtype) * (
        speeds * trace_r[1:-1]
    )
    volume = (
        volume - viscosity * multiply(stiffness, center) + column(left_vals, dtype) * inflow[:-1]
    )
    right_terms = gates[1:] * (
        means[1:] * column(right_vals, dtype)
        + 0.5 * jumps[1:] * column(right_slope, dtype)
        - penalty * jumps[1:] * column(right_vals, dtype)
    )
    left_terms = gates[:-1] * (
        -means[:-1] * column(left_vals, dtype)
        + 0.5 * jumps[:-1] * column(left_slope, dtype)
        + penalty * jumps[:-1] * column(left_vals, dtype)
    )
    return jacobian * column(inv_mass, dtype) * (volume + viscosity * (right_terms + left_terms))


def local_rhs(state, speeds):
    dtype = state.dtype
    right_vals, left_vals, right_slope, left_slope, inv_mass, advect, stiffness = basis_tables(
        state.shape[0]
    )
    trace_r = jnp.sum(column(right_vals, dtype) * state, 0)
    volume = speeds * multiply(advect, state) - column(right_vals, dtype) * (speeds * trace_r)
    volume = volume - viscosity * multiply(stiffness, state)
    return jacobian * column(inv_mass, dtype) * volume


def runge_kutta(state, tendency, delta):
    section_one = state + delta * tendency(state)
    section_two = 0.75 * state + 0.25 * (section_one + delta * tendency(section_one))
    return state / 3.0 + 2.0 / 3.0 * (section_two + delta * tendency(section_two))


def coarse_matrices(speeds, count):
    units = jnp.eye(count, dtype=speeds.dtype)[:, :, None] * jnp.ones_like(speeds)[None, None, :]
    columns = jax.vmap(
        lambda unit: runge_kutta(unit, lambda s: local_rhs(s, speeds), STEPS * step_size)
    )(units)
    return jnp.transpose(columns, (1, 0, 2))


def apply_map(matrices, field):
    return jnp.sum(matrices * field[None, :, :], axis=1)


def body(initial, guess, speeds, flags):
    dtype = initial.dtype
    count = initial.shape[1]
    modes = initial.shape[0]
    place = lax.axis_index("space") * count + lax.iota(jnp.int32, count)
    open_faces = (1 - flags).astype(dtype) * (place > 0).astype(dtype)
    coefs = jnp.stack([speeds, open_faces])
    previous = passed_along(guess[0], "tm", 1)
    start = jnp.where(lax.axis_index("tm") == 0, initial, previous)
    rims = with_halo(coefs, (("space", 1),), 1)

    def tendency(state):
        padded = with_halo(state, (("space", 1),), 1)
        return spatial_rhs(padded, rims[0], rims[1])

    def advance(counter, state):
        return runge_kutta(state, tendency, step_size)

    final = lax.fori_loop(0, STEPS, advance, start)
    residual = final - guess[0]
    matrices = coarse_matrices(speeds, modes)
    gathered = lax.all_gather(residual[None], "tm", axis=0, tiled=True)
    my_slab = lax.axis_index("tm")

    def relay(counter, carry):
        term = lax.dynamic_index_in_dim(gathered, counter, 0, keepdims=False)
        return jnp.where(counter < my_slab, apply_map(matrices, carry) + term, carry)

    incoming = lax.fori_loop(0, lax.axis_size("tm"), relay, jnp.zeros_like(residual))
    correction = apply_map(matrices, incoming) + residual
    return (guess[0] + correction)[None]


def solution(mesh):
    return jax.shard_map(
        body,
        mesh=mesh,
        in_specs=(P(None, "space"), P("tm", None, "space"), P("space"), P("space")),
        out_specs=P("tm", None, "space"),
        check_vma=False,
    )
```

profile of v0, /device:TPU:2, one launch (start us, length us, event | category | flops | bytes accessed | tf_op | source)
XLA Modules:
  0.0 542.1 jit_solution(15068488024693112194)
XLA Ops:
  8.0 1.9 collective-permute-start.7
  10.0 3.6 collective-permute-start.8
  13.6 3.8 collective-permute-start.6
  18.5 2.0 collective-permute-done.6
  21.5 253.0 %while.26 = (s32[]{:T(128)}, f32[4,8192]{1,0:T(4,128)S(1)}, f32[2,8194]{1,0:T(2,128)S(1)}, s32[]{:T(128)}, f32[4,4]{1,0:T(4,128)}, /*index=5*/f32[4,4]{1,0:T(4,1...) while((s32[]{:T(128)}, f32[4,8192]{1,0:T(4,128)S(1)}, ...), condition=%wide.region_16.17_spmd.clone.clone, body=%wide.region_3.16_spmd.sunk.clone.clone.sunk | while | flops 12656795 | bytes 7572181 | solution.py:146
  21.7 1.9 collective-permute-start
  23.6 3.6 collective-permute-start.1
  32.9 2.9 collective-permute-start.2
  35.8 2.6 collective-permute-start.3
  41.5 1.3 fusion.149
  43.9 3.2 collective-permute-start.4
  47.1 2.4 collective-permute-start.5
  53.3 3.2 collective-permute-start
  56.5 2.4 collective-permute-start.1
  64.5 2.9 collective-permute-start.2
  67.4 2.6 collective-permute-start.3
  73.1 1.3 fusion.149
  75.5 3.2 collective-permute-start.4
  78.7 2.4 collective-permute-start.5
  84.9 3.2 collective-permute-start
  88.1 2.4 collective-permute-start.1
  96.1 2.9 collective-permute-start.2
  99.1 2.6 collective-permute-start.3
  104.7 1.3 fusion.149
  107.2 3.2 collective-permute-start.4
  110.4 2.4 collective-permute-start.5
  116.6 3.2 collective-permute-start
  119.8 2.4 collective-permute-start.1
  127.8 2.9 collective-permute-start.2
  130.7 2.6 collective-permute-start.3
  136.4 1.3 fusion.149
  138.8 3.2 collective-permute-start.4
  142.0 2.4 collective-permute-start.5
  148.2 3.2 collective-permute-start
  151.4 2.4 collective-permute-start.1
  159.4 2.9 collective-permute-start.2
  162.3 2.6 collective-permute-start.3
  168.0 1.3 fusion.149
  170.4 3.2 collective-permute-start.4
  173.6 2.4 collective-permute-start.5
  179.8 3.2 collective-permute-start
  183.0 2.4 collective-permute-start.1
  191.0 2.9 collective-permute-start.2
  194.0 2.6 collective-permute-start.3
  199.6 1.3 fusion.149
  202.1 3.2 collective-permute-start.4
  205.3 2.4 collective-permute-start.5
  211.5 3.2 collective-permute-start
  214.7 2.4 collective-permute-start.1
  222.7 2.9 collective-permute-start.2
  225.6 2.6 collective-permute-start.3
  231.3 1.3 fusion.149
  233.7 3.2 collective-permute-start.4
  236.9 2.4 collective-permute-start.5
  243.1 3.2 collective-permute-start
  246.3 2.4 collective-permute-start.1
  254.3 2.9 collective-permute-start.2
  257.2 2.6 collective-permute-start.3
  265.3 3.2 collective-permute-start.4
  268.5 2.4 collective-permute-start.5
  277.2 2.3 bitcast_reduce_fusion
  281.8 1.4 fusion.51
  287.3 150.9 %all-gather.4.cloned.1.call-done = f32[64,4,8192]{2,1,0:T(4,128)} async-done(((f32[1,4,8192]{2,1,0:T(4,128)}), f32[64,4,8192]{2,1,0:T(4,128)}) %all-gather.4.cloned.1.call-update) | async-done | bytes 8388624 | tf_op jit(solution)/shard_map/all_gather | solution.py:149
  438.2 96.0 %while.27 = (s32[]{:T(128)}, f32[4,8192]{1,0:T(4,128)S(1)}, s32[]{:T(128)}, f32[4,4,8192]{2,1,0:T(4,128)S(1)}, f32[64,4,8192]{2,1,0:T(4,128)}, /*index=5*/s32[]{:T(128)}, s32[]{:T(128)}) while((s32[]{:T(128)}, f32[4,8192]{1,0:T(4,128)S(1)}, s32[]{:T(128)}, f32[4,4,8192]{2,1,0:T(4,128)S(1)}, f32[64,4,8192]{2,1,0:T(4,128)}, ...), condition=%wide.region_19.20_spmd.clone, body=%wide.region_17.19_spmd.clone.sunk | while | flops 360452 | bytes 1572966 | solution.py:156
  (624 shorter events, 216.4 us)
Async XLA Ops:
  6.5 431.6 %all-gather.4.cloned.1.call-start = ((), (), s32[]{:S(2)}) async-start(), calls=%async_computation | async-start | bytes 8519680 | tf_op jit(solution)/shard_map/all_gather | solution.py:149
  8.0 10.2 %collective-permute-start.7 = (f32[2,1]{1,0:T(2,128)S(1)}, f32[2,1]{1,0:T(2,128)S(1)}, u32[]{:S(2)}, u32[]{:S(2)}) collective-permute-start(f32[2,1]{1,0:T(2,128)S(1)} %get-tuple-element.563), channel_id=1, source_target_pairs={{0,1},{1,2},{2,3},{3,4},{4,5},{5,6},{6,7},{8,9},{9,10},{10,11},{11... | collective-permute-start | bytes 32 | tf_op jit(solution)/shard_map/ppermute | solution.py:30
  10.0 8.3 %collective-permute-start.8 = (f32[2,1]{1,0:T(2,128)S(1)}, f32[2,1]{1,0:T(2,128)S(1)}, u32[]{:S(2)}, u32[]{:S(2)}) collective-permute-start(f32[2,1]{1,0:T(2,128)S(1)} %get-tuple-element.562), channel_id=1, source_target_pairs={{1,0},{2,1},{3,2},{4,3},{5,4},{6,5},{7,6},{9,8},{10,9},{11,10},{12... | collective-permute-start | bytes 32 | tf_op jit(solution)/shard_map/ppermute | solution.py:32
  13.6 6.9 %collective-permute-start.6 = (f32[4,8192]{1,0:T(4,128)}, f32[4,8192]{1,0:T(4,128)S(1)}, u32[]{:S(2)}, u32[]{:S(2)}) collective-permute-start(f32[4,8192]{1,0:T(4,128)} %bitcast.156), channel_id=1, source_target_pairs={{0,8},{8,16},{16,24},{24,32},{32,40},{40,48},{48,56},{56,64},{64,7... | collective-permute-start | bytes 393224 | tf_op jit(solution)/shard_map/ppermute | solution.py:19
  21.5 253.1 %copy-start.1 = (f32[1,4,8192]{2,1,0:T(4,128)S(1)}, f32[1,4,8192]{2,1,0:T(4,128)}, u32[]{:S(2)}) copy-start(f32[1,4,8192]{2,1,0:T(4,128)} %param.69) | copy-start | bytes 393220
  21.5 254.1 %copy-start.5 = (f32[4,4,1]{1,0,2:T(4,128)S(1)}, f32[4,4,1]{1,0,2:T(4,128)}, u32[]{:S(2)}) copy-start(f32[4,4,1]{1,0,2:T(4,128)} %constant.120) | copy-start | bytes 196
  21.5 255.1 %copy-start = (f32[8192]{0:T(1024)S(1)}, f32[8192]{0:T(1024)}, u32[]{:S(2)}) copy-start(f32[8192]{0:T(1024)} %param.70) | copy-start | bytes 98308
  21.5 255.7 %copy-start.6 = (f32[4,4,1]{1,0,2:T(4,128)S(1)}, f32[4,4,1]{1,0,2:T(4,128)}, u32[]{:S(2)}) copy-start(f32[4,4,1]{1,0,2:T(4,128)} %constant.119) | copy-start | bytes 196
  21.5 31.0 %copy-start.2 = (f32[4]{0:T(128)S(1)}, f32[4]{0:T(128)}, u32[]{:S(2)}) copy-start(f32[4]{0:T(128)} %get-tuple-element.741) | copy-start | bytes 52 | tf_op jit(solution)/shard_map/while
  21.7 7.1 %collective-permute-start = (f32[4,1]{1,0:T(4,128)S(1)}, f32[4,1]{1,0:T(4,128)S(1)}, u32[]{:S(2)}, u32[]{:S(2)}) collective-permute-start(f32[4,1]{1,0:T(4,128)S(1)} %get-tuple-element.662), channel_id=1, source_target_pairs={{0,1},{1,2},{2,3},{3,4},{4,5},{5,6},{6,7},{8,9},{9,10},{10,11},{11... | collective-permute-start | bytes 56 | tf_op jit(solution)/shard_map/while/body/eval_jaxpr/ppermute | solution.py:30
  23.6 5.2 collective-permute-start.1
  32.9 5.6 %collective-permute-start.2 = (f32[4,1]{1,0:T(4,128)S(1)}, f32[4,1]{1,0:T(4,128)S(1)}, u32[]{:S(2)}, u32[]{:S(2)}) collective-permute-start(f32[4,1]{1,0:T(4,128)S(1)} %get-tuple-element.681), channel_id=1, source_target_pairs={{0,1},{1,2},{2,3},{3,4},{4,5},{5,6},{6,7},{8,9},{9,10},{10,11},{11... | collective-permute-start | bytes 56 | tf_op jit(solution)/shard_map/while/body/eval_jaxpr/ppermute | solution.py:30
  35.8 3.9 collective-permute-start.3
  43.9 5.6 %collective-permute-start.4 = (f32[4,1]{1,0:T(4,128)S(1)}, f32[4,1]{1,0:T(4,128)S(1)}, u32[]{:S(2)}, u32[]{:S(2)}) collective-permute-start(f32[4,1]{1,0:T(4,128)S(1)} %get-tuple-element.695), channel_id=1, source_target_pairs={{0,1},{1,2},{2,3},{3,4},{4,5},{5,6},{6,7},{8,9},{9,10},{10,11},{11... | collective-permute-start | bytes 56 | tf_op jit(solution)/shard_map/while/body/eval_jaxpr/ppermute | solution.py:30
  47.1 3.7 collective-permute-start.5
  53.2 31.0 %copy-start.2 = (f32[4]{0:T(128)S(1)}, f32[4]{0:T(128)}, u32[]{:S(2)}) copy-start(f32[4]{0:T(128)} %get-tuple-element.741) | copy-start | bytes 52 | tf_op jit(solution)/shard_map/while
  53.3 7.1 %collective-permute-start = (f32[4,1]{1,0:T(4,128)S(1)}, f32[4,1]{1,0:T(4,128)S(1)}, u32[]{:S(2)}, u32[]{:S(2)}) collective-permute-start(f32[4,1]{1,0:T(4,128)S(1)} %get-tuple-element.662), channel_id=1, source_target_pairs={{0,1},{1,2},{2,3},{3,4},{4,5},{5,6},{6,7},{8,9},{9,10},{10,11},{11... | collective-permute-start | bytes 56 | tf_op jit(solution)/shard_map/while/body/eval_jaxpr/ppermute | solution.py:30
  56.5 3.9 collective-permute-start.1
  64.5 5.6 %collective-permute-start.2 = (f32[4,1]{1,0:T(4,128)S(1)}, f32[4,1]{1,0:T(4,128)S(1)}, u32[]{:S(2)}, u32[]{:S(2)}) collective-permute-start(f32[4,1]{1,0:T(4,128)S(1)} %get-tuple-element.681), channel_id=1, source_target_pairs={{0,1},{1,2},{2,3},{3,4},{4,5},{5,6},{6,7},{8,9},{9,10},{10,11},{11... | collective-permute-start | bytes 56 | tf_op jit(solution)/shard_map/while/body/eval_jaxpr/ppermute | solution.py:30
  67.4 3.9 collective-permute-start.3
  75.5 5.6 %collective-permute-start.4 = (f32[4,1]{1,0:T(4,128)S(1)}, f32[4,1]{1,0:T(4,128)S(1)}, u32[]{:S(2)}, u32[]{:S(2)}) collective-permute-start(f32[4,1]{1,0:T(4,128)S(1)} %get-tuple-element.695), channel_id=1, source_target_pairs={{0,1},{1,2},{2,3},{3,4},{4,5},{5,6},{6,7},{8,9},{9,10},{10,11},{11... | collective-permute-start | bytes 56 | tf_op jit(solution)/shard_map/while/body/eval_jaxpr/ppermute | solution.py:30
  78.7 3.7 collective-permute-start.5
  84.8 31.0 %copy-start.2 = (f32[4]{0:T(128)S(1)}, f32[4]{0:T(128)}, u32[]{:S(2)}) copy-start(f32[4]{0:T(128)} %get-tuple-element.741) | copy-start | bytes 52 | tf_op jit(solution)/shard_map/while
  84.9 7.1 %collective-permute-start = (f32[4,1]{1,0:T(4,128)S(1)}, f32[4,1]{1,0:T(4,128)S(1)}, u32[]{:S(2)}, u32[]{:S(2)}) collective-permute-start(f32[4,1]{1,0:T(4,128)S(1)} %get-tuple-element.662), channel_id=1, source_target_pairs={{0,1},{1,2},{2,3},{3,4},{4,5},{5,6},{6,7},{8,9},{9,10},{10,11},{11... | collective-permute-start | bytes 56 | tf_op jit(solution)/shard_map/while/body/eval_jaxpr/ppermute | solution.py:30
  88.1 3.9 collective-permute-start.1
  96.1 5.6 %collective-permute-start.2 = (f32[4,1]{1,0:T(4,128)S(1)}, f32[4,1]{1,0:T(4,128)S(1)}, u32[]{:S(2)}, u32[]{:S(2)}) collective-permute-start(f32[4,1]{1,0:T(4,128)S(1)} %get-tuple-element.681), channel_id=1, source_target_pairs={{0,1},{1,2},{2,3},{3,4},{4,5},{5,6},{6,7},{8,9},{9,10},{10,11},{11... | collective-permute-start | bytes 56 | tf_op jit(solution)/shard_map/while/body/eval_jaxpr/ppermute | solution.py:30
  99.1 3.9 collective-permute-start.3
  107.2 5.6 %collective-permute-start.4 = (f32[4,1]{1,0:T(4,128)S(1)}, f32[4,1]{1,0:T(4,128)S(1)}, u32[]{:S(2)}, u32[]{:S(2)}) collective-permute-start(f32[4,1]{1,0:T(4,128)S(1)} %get-tuple-element.695), channel_id=1, source_target_pairs={{0,1},{1,2},{2,3},{3,4},{4,5},{5,6},{6,7},{8,9},{9,10},{10,11},{11... | collective-permute-start | bytes 56 | tf_op jit(solution)/shard_map/while/body/eval_jaxpr/ppermute | solution.py:30
  110.4 3.7 collective-permute-start.5
  116.4 31.0 %copy-start.2 = (f32[4]{0:T(128)S(1)}, f32[4]{0:T(128)}, u32[]{:S(2)}) copy-start(f32[4]{0:T(128)} %get-tuple-element.741) | copy-start | bytes 52 | tf_op jit(solution)/shard_map/while
  116.6 7.1 %collective-permute-start = (f32[4,1]{1,0:T(4,128)S(1)}, f32[4,1]{1,0:T(4,128)S(1)}, u32[]{:S(2)}, u32[]{:S(2)}) collective-permute-start(f32[4,1]{1,0:T(4,128)S(1)} %get-tuple-element.662), channel_id=1, source_target_pairs={{0,1},{1,2},{2,3},{3,4},{4,5},{5,6},{6,7},{8,9},{9,10},{10,11},{11... | collective-permute-start | bytes 56 | tf_op jit(solution)/shard_map/while/body/eval_jaxpr/ppermute | solution.py:30
  119.8 3.9 collective-permute-start.1
  127.8 5.6 %collective-permute-start.2 = (f32[4,1]{1,0:T(4,128)S(1)}, f32[4,1]{1,0:T(4,128)S(1)}, u32[]{:S(2)}, u32[]{:S(2)}) collective-permute-start(f32[4,1]{1,0:T(4,128)S(1)} %get-tuple-element.681), channel_id=1, source_target_pairs={{0,1},{1,2},{2,3},{3,4},{4,5},{5,6},{6,7},{8,9},{9,10},{10,11},{11... | collective-permute-start | bytes 56 | tf_op jit(solution)/shard_map/while/body/eval_jaxpr/ppermute | solution.py:30
  130.7 3.9 collective-permute-start.3
  138.8 5.6 %collective-permute-start.4 = (f32[4,1]{1,0:T(4,128)S(1)}, f32[4,1]{1,0:T(4,128)S(1)}, u32[]{:S(2)}, u32[]{:S(2)}) collective-permute-start(f32[4,1]{1,0:T(4,128)S(1)} %get-tuple-element.695), channel_id=1, source_target_pairs={{0,1},{1,2},{2,3},{3,4},{4,5},{5,6},{6,7},{8,9},{9,10},{10,11},{11... | collective-permute-start | bytes 56 | tf_op jit(solution)/shard_map/while/body/eval_jaxpr/ppermute | solution.py:30
  142.0 3.7 collective-permute-start.5
  148.1 31.0 %copy-start.2 = (f32[4]{0:T(128)S(1)}, f32[4]{0:T(128)}, u32[]{:S(2)}) copy-start(f32[4]{0:T(128)} %get-tuple-element.741) | copy-start | bytes 52 | tf_op jit(solution)/shard_map/while
  148.2 7.1 %collective-permute-start = (f32[4,1]{1,0:T(4,128)S(1)}, f32[4,1]{1,0:T(4,128)S(1)}, u32[]{:S(2)}, u32[]{:S(2)}) collective-permute-start(f32[4,1]{1,0:T(4,128)S(1)} %get-tuple-element.662), channel_id=1, source_target_pairs={{0,1},{1,2},{2,3},{3,4},{4,5},{5,6},{6,7},{8,9},{9,10},{10,11},{11... | collective-permute-start | bytes 56 | tf_op jit(solution)/shard_map/while/body/eval_jaxpr/ppermute | solution.py:30
  151.4 3.9 collective-permute-start.1
  159.4 5.6 %collective-permute-start.2 = (f32[4,1]{1,0:T(4,128)S(1)}, f32[4,1]{1,0:T(4,128)S(1)}, u32[]{:S(2)}, u32[]{:S(2)}) collective-permute-start(f32[4,1]{1,0:T(4,128)S(1)} %get-tuple-element.681), channel_id=1, source_target_pairs={{0,1},{1,2},{2,3},{3,4},{4,5},{5,6},{6,7},{8,9},{9,10},{10,11},{11... | collective-permute-start | bytes 56 | tf_op jit(solution)/shard_map/while/body/eval_jaxpr/ppermute | solution.py:30
  162.3 3.9 collective-permute-start.3
  170.4 5.6 %collective-permute-start.4 = (f32[4,1]{1,0:T(4,128)S(1)}, f32[4,1]{1,0:T(4,128)S(1)}, u32[]{:S(2)}, u32[]{:S(2)}) collective-permute-start(f32[4,1]{1,0:T(4,128)S(1)} %get-tuple-element.695), channel_id=1, source_target_pairs={{0,1},{1,2},{2,3},{3,4},{4,5},{5,6},{6,7},{8,9},{9,10},{10,11},{11... | collective-permute-start | bytes 56 | tf_op jit(solution)/shard_map/while/body/eval_jaxpr/ppermute | solution.py:30
  173.6 3.7 collective-permute-start.5
  179.7 31.0 %copy-start.2 = (f32[4]{0:T(128)S(1)}, f32[4]{0:T(128)}, u32[]{:S(2)}) copy-start(f32[4]{0:T(128)} %get-tuple-element.741) | copy-start | bytes 52 | tf_op jit(solution)/shard_map/while
  179.8 7.1 %collective-permute-start = (f32[4,1]{1,0:T(4,128)S(1)}, f32[4,1]{1,0:T(4,128)S(1)}, u32[]{:S(2)}, u32[]{:S(2)}) collective-permute-start(f32[4,1]{1,0:T(4,128)S(1)} %get-tuple-element.662), channel_id=1, source_target_pairs={{0,1},{1,2},{2,3},{3,4},{4,5},{5,6},{6,7},{8,9},{9,10},{10,11},{11... | collective-permute-start | bytes 56 | tf_op jit(solution)/shard_map/while/body/eval_jaxpr/ppermute | solution.py:30
  183.0 3.9 collective-permute-start.1
  191.0 5.6 %collective-permute-start.2 = (f32[4,1]{1,0:T(4,128)S(1)}, f32[4,1]{1,0:T(4,128)S(1)}, u32[]{:S(2)}, u32[]{:S(2)}) collective-permute-start(f32[4,1]{1,0:T(4,128)S(1)} %get-tuple-element.681), channel_id=1, source_target_pairs={{0,1},{1,2},{2,3},{3,4},{4,5},{5,6},{6,7},{8,9},{9,10},{10,11},{11... | collective-permute-start | bytes 56 | tf_op jit(solution)/shard_map/while/body/eval_jaxpr/ppermute | solution.py:30
  194.0 3.9 collective-permute-start.3
  202.1 5.6 %collective-permute-start.4 = (f32[4,1]{1,0:T(4,128)S(1)}, f32[4,1]{1,0:T(4,128)S(1)}, u32[]{:S(2)}, u32[]{:S(2)}) collective-permute-start(f32[4,1]{1,0:T(4,128)S(1)} %get-tuple-element.695), channel_id=1, source_target_pairs={{0,1},{1,2},{2,3},{3,4},{4,5},{5,6},{6,7},{8,9},{9,10},{10,11},{11... | collective-permute-start | bytes 56 | tf_op jit(solution)/shard_map/while/body/eval_jaxpr/ppermute | solution.py:30
  205.3 3.7 collective-permute-start.5
  211.3 31.0 %copy-start.2 = (f32[4]{0:T(128)S(1)}, f32[4]{0:T(128)}, u32[]{:S(2)}) copy-start(f32[4]{0:T(128)} %get-tuple-element.741) | copy-start | bytes 52 | tf_op jit(solution)/shard_map/while
  211.5 7.1 %collective-permute-start = (f32[4,1]{1,0:T(4,128)S(1)}, f32[4,1]{1,0:T(4,128)S(1)}, u32[]{:S(2)}, u32[]{:S(2)}) collective-permute-start(f32[4,1]{1,0:T(4,128)S(1)} %get-tuple-element.662), channel_id=1, source_target_pairs={{0,1},{1,2},{2,3},{3,4},{4,5},{5,6},{6,7},{8,9},{9,10},{10,11},{11... | collective-permute-start | bytes 56 | tf_op jit(solution)/shard_map/while/body/eval_jaxpr/ppermute | solution.py:30
  214.7 3.9 collective-permute-start.1
  222.7 5.6 %collective-permute-start.2 = (f32[4,1]{1,0:T(4,128)S(1)}, f32[4,1]{1,0:T(4,128)S(1)}, u32[]{:S(2)}, u32[]{:S(2)}) collective-permute-start(f32[4,1]{1,0:T(4,128)S(1)} %get-tuple-element.681), channel_id=1, source_target_pairs={{0,1},{1,2},{2,3},{3,4},{4,5},{5,6},{6,7},{8,9},{9,10},{10,11},{11... | collective-permute-start | bytes 56 | tf_op jit(solution)/shard_map/while/body/eval_jaxpr/ppermute | solution.py:30
  225.6 3.9 collective-permute-start.3
  233.7 5.6 %collective-permute-start.4 = (f32[4,1]{1,0:T(4,128)S(1)}, f32[4,1]{1,0:T(4,128)S(1)}, u32[]{:S(2)}, u32[]{:S(2)}) collective-permute-start(f32[4,1]{1,0:T(4,128)S(1)} %get-tuple-element.695), channel_id=1, source_target_pairs={{0,1},{1,2},{2,3},{3,4},{4,5},{5,6},{6,7},{8,9},{9,10},{10,11},{11... | collective-permute-start | bytes 56 | tf_op jit(solution)/shard_map/while/body/eval_jaxpr/ppermute | solution.py:30
  236.9 3.7 collective-permute-start.5
  243.0 31.0 %copy-start.2 = (f32[4]{0:T(128)S(1)}, f32[4]{0:T(128)}, u32[]{:S(2)}) copy-start(f32[4]{0:T(128)} %get-tuple-element.741) | copy-start | bytes 52 | tf_op jit(solution)/shard_map/while
  243.1 7.1 %collective-permute-start = (f32[4,1]{1,0:T(4,128)S(1)}, f32[4,1]{1,0:T(4,128)S(1)}, u32[]{:S(2)}, u32[]{:S(2)}) collective-permute-start(f32[4,1]{1,0:T(4,128)S(1)} %get-tuple-element.662), channel_id=1, source_target_pairs={{0,1},{1,2},{2,3},{3,4},{4,5},{5,6},{6,7},{8,9},{9,10},{10,11},{11... | collective-permute-start | bytes 56 | tf_op jit(solution)/shard_map/while/body/eval_jaxpr/ppermute | solution.py:30
  246.3 3.9 collective-permute-start.1
  254.3 5.6 %collective-permute-start.2 = (f32[4,1]{1,0:T(4,128)S(1)}, f32[4,1]{1,0:T(4,128)S(1)}, u32[]{:S(2)}, u32[]{:S(2)}) collective-permute-start(f32[4,1]{1,0:T(4,128)S(1)} %get-tuple-element.681), channel_id=1, source_target_pairs={{0,1},{1,2},{2,3},{3,4},{4,5},{5,6},{6,7},{8,9},{9,10},{10,11},{11... | collective-permute-start | bytes 56 | tf_op jit(solution)/shard_map/while/body/eval_jaxpr/ppermute | solution.py:30
  257.2 3.9 collective-permute-start.3
  265.3 5.6 %collective-permute-start.4 = (f32[4,1]{1,0:T(4,128)S(1)}, f32[4,1]{1,0:T(4,128)S(1)}, u32[]{:S(2)}, u32[]{:S(2)}) collective-permute-start(f32[4,1]{1,0:T(4,128)S(1)} %get-tuple-element.695), channel_id=1, source_target_pairs={{0,1},{1,2},{2,3},{3,4},{4,5},{5,6},{6,7},{8,9},{9,10},{10,11},{11... | collective-permute-start | bytes 56 | tf_op jit(solution)/shard_map/while/body/eval_jaxpr/ppermute | solution.py:30
  268.5 3.7 collective-permute-start.5
  (33 other events, 1002.0 us)
Sparse Core Ops, SparseCore 0:
  275.4 162.6 all-gather.3
where the time goes:
time: 546 us; the launch traced here: 542 us
  waiting for transfers between devices  173 us (32%)
  starting transfers between devices  143 us (26%)
  other arithmetic  140 us (26%)
  matrix products  58 us (11%)
  between operations  13.6 us (2%)
  local copies, waits for them, and re-layouts  11 us (2%)
    all_gather x1, waiting for transfers between devices, body(): gathered = lax.all_gather(residual[None], 'tm', axis=0, tiled=True)  151 us
    ppermute x25, starting transfers between devices, with_halo(): lax.ppermute(tail, axis, [(i, (i + 1) % count) for i in range(ends)])  75.1 us
    select_n x64, other arithmetic, relay(): jnp.where(counter < my_slab, apply_map(matrices, carry) + term, carry)  69.4 us
    ppermute x25, starting transfers between devices, with_halo(): lax.ppermute(head, axis, [((i + 1) % count, i) for i in range(ends)])  63.9 us
    dot_general x54, matrix products, multiply(): jnp.einsum('ij,je->ie', jnp.asarray(table, field.dtype), field, precision...  58 us
    reduce_sum x24, other arithmetic, spatial_rhs(): slope_r = jnp.sum(column(right_slope, dtype) * padded, 0)  26.3 us
    reduce_sum x65, other arithmetic, apply_map(): return jnp.sum(matrices * field[None, :, :], axis=1)  23.9 us
    ppermute x25, waiting for transfers between devices, with_halo(): lax.ppermute(head, axis, [((i + 1) % count, i) for i in range(ends)])  20.4 us
  transfers between devices with their start and end apart: 52, of which 18 were waited for; matrix products, arithmetic and copies ran while one was open for 5% of the time, Pallas kernels for 0%

commit v1 on v0

v1 whole, which is shorter than its diff:
```python
import functools

import jax
import jax.numpy as jnp
from jax import lax
from jax.experimental import pallas as pl
from jax.experimental.pallas import tpu as pltpu
from jax.sharding import PartitionSpec as P

MODES = 4
STEPS = 8
LANES = 128
VISCOSITY = 0.02
PENALTY = 10.0
STEP = 0.015625
JACOBIAN = 8.0
INV_MASS = (0.5, 1.5, 2.5, 3.5)


def column_scales(delta):
    return [JACOBIAN * m * delta for m in INV_MASS]


def before(x):
    rolled = pltpu.roll(x, 1, 1)
    lane = lax.broadcasted_iota(jnp.int32, x.shape, 1)
    return jnp.where(lane == 0, pltpu.roll(rolled, 1, 0), rolled)


def after(x):
    rows, lanes = x.shape
    rolled = pltpu.roll(x, lanes - 1, 1)
    lane = lax.broadcasted_iota(jnp.int32, x.shape, 1)
    return jnp.where(lane == lanes - 1, pltpu.roll(rolled, rows - 1, 0), rolled)


def volume_terms(u, speed2, drain, p, q):
    a, b, c, d = u
    vq = (2.0 * VISCOSITY) * q
    m1 = speed2 * a - vq
    m2 = speed2 * b - (6.0 * VISCOSITY) * c
    m3 = speed2 * p - vq - (10.0 * VISCOSITY) * d
    return m1, m2, m3


def local_rhs(u, speed, speed2):
    a, b, c, d = u
    p, q = a + c, b + d
    out = -(speed * (p + q))
    m1, m2, m3 = volume_terms(u, speed2, out, p, q)
    return out, out + m1, out + m2, out + m3


def full_rhs(u, speed, speed2, inflow, gate, gate_after):
    a, b, c, d = u
    p, q = a + c, b + d
    tr, tl = p + q, p - q
    odd, even = b + 6.0 * d, 3.0 * c
    sr, sl = odd + even, odd - even
    tr_b, sr_b = before(tr), before(sr)
    tl_a, sl_a = after(tl), after(sl)
    jump = tr_b - tl
    k_l = gate * jump
    h_l = gate * (sr_b + sl - (2.0 * PENALTY) * jump)
    g_l = inflow * tr_b - h_l
    jump_a = tr - tl_a
    k_r = gate_after * jump_a
    h_r = gate_after * (sr + sl_a - (2.0 * PENALTY) * jump_a)
    base = h_r - speed * tr
    plus, minus = base + g_l, base - g_l
    k_sum, k_dif = k_r + k_l, k_r - k_l
    m1, m2, m3 = volume_terms(u, speed2, base, p, q)
    return plus, minus + k_sum + m1, plus + 3.0 * k_dif + m2, minus + 6.0 * k_sum + m3


def three_sections(u, rhs, delta):
    v = u
    for share in (3.0, 2.0, 1.0):
        scale = column_scales(delta / share)
        v = [x + f * r for x, f, r in zip(u, scale, rhs(v))]
    return v


def fine_kernel(slabs, blocks, guess_ref, initial_ref, left_ref, right_ref, speed_ref, flag_ref, out_ref):
    rows = speed_ref.shape[0]
    wide = rows + 8
    slab, block = lax.axis_index("tm"), lax.axis_index("space")
    last = slab == slabs - 1

    def ring(main, k):
        unused = jnp.zeros((6, LANES), jnp.float32)
        return jnp.concatenate([main, right_ref[pl.ds(k, 1), :], unused, left_ref[pl.ds(k, 1), :]], 0)

    own = []
    for k in range(MODES):
        here = pl.ds(k, rows, stride=MODES)
        own.append(jnp.where(last, initial_ref[here, :], guess_ref[here, :]))
    start = [ring(x, k) for k, x in enumerate(own)]
    speed_own = speed_ref[...]
    open_own = 1.0 - flag_ref[...].astype(jnp.float32)
    speed = ring(speed_own, MODES)
    opened = ring(open_own, MODES + 1)
    row = lax.broadcasted_iota(jnp.int32, (wide, LANES), 0)
    lane = lax.broadcasted_iota(jnp.int32, (wide, LANES), 1)
    first = jnp.logical_and(jnp.logical_and(row == 0, lane == 0), block == 0)
    opened = jnp.where(first, 0.0, opened)
    gate = (0.5 * VISCOSITY) * opened
    gate_after = after(gate)
    inflow = opened * before(speed)
    speed2 = 2.0 * speed

    def rhs(u):
        return full_rhs(u, speed, speed2, inflow, gate, gate_after)

    final = lax.fori_loop(0, STEPS, lambda i, u: tuple(three_sections(u, rhs, STEP)), tuple(start))
    speed2_own = 2.0 * speed_own
    coarse = three_sections(own, lambda u: local_rhs(u, speed_own, speed2_own), STEPS * STEP)
    for k in range(MODES):
        share = jnp.where(last, 0.0, coarse[k])
        out_ref[pl.ds(k, rows, stride=MODES), :] = final[k][:rows] - share


def fine_part(guess, initial, left, right, speeds, flags, slabs, blocks):
    return pl.pallas_call(
        functools.partial(fine_kernel, slabs, blocks),
        out_shape=jax.ShapeDtypeStruct(guess.shape, jnp.float32),
        in_specs=[pl.BlockSpec(memory_space=pltpu.VMEM)] * 6,
        out_specs=pl.BlockSpec(memory_space=pltpu.VMEM),
        compiler_params=pltpu.CompilerParams(vmem_limit_bytes=16 * 1024 * 1024),
        cost_estimate=pl.CostEstimate(flops=24 * 60 * 8192, bytes_accessed=4 * guess.size * 4, transcendentals=0),
        name="fine_steps",
    )(guess, initial, left, right, speeds, flags)


def times(matrix, field):
    return [sum(matrix[i][j] * field[j] for j in range(1, MODES)) + matrix[i][0] * field[0] for i in range(MODES)]


def square(matrix):
    columns = [times(matrix, [matrix[i][j] for i in range(MODES)]) for j in range(MODES)]
    return [[columns[j][i] for j in range(MODES)] for i in range(MODES)]


def scan_kernel(group, term_ref, speed_ref, out_ref):
    slabs = term_ref.shape[0] // MODES
    groups = slabs // group
    shape = (groups, LANES)
    row = lax.broadcasted_iota(jnp.int32, shape, 0)
    speed = jnp.broadcast_to(speed_ref[pl.ds(lax.axis_index("tm"), 1), :], shape)
    speed2 = 2.0 * speed
    zero, one = jnp.zeros(shape, jnp.float32), jnp.ones(shape, jnp.float32)
    columns = [
        three_sections([one if i == j else zero for i in range(MODES)], lambda u: local_rhs(u, speed, speed2), STEPS * STEP)
        for j in range(MODES)
    ]
    matrix = [[columns[j][i] for j in range(MODES)] for i in range(MODES)]

    def term(i):
        source = (i - 1) % group
        read = [term_ref[pl.ds(source * MODES + k, groups, stride=group * MODES), :] for k in range(MODES)]
        return [pltpu.roll(x, 1, 0) for x in read] if i == 0 else read

    sums = [term(0)]
    for i in range(1, group):
        sums.append([x + y for x, y in zip(times(matrix, sums[-1]), term(i))])
    power, size = matrix, 1
    while size < group:
        power, size = square(power), 2 * size
    total, reach = sums[-1], 1
    while reach < groups:
        earlier = [jnp.where(row >= reach, pltpu.roll(x, reach, 0), 0.0) for x in total]
        total = [x + y for x, y in zip(total, times(power, earlier))]
        reach *= 2
        if reach < groups:
            power = square(power)
    carry = [jnp.where(row >= 1, pltpu.roll(x, 1, 0), 0.0) for x in total]
    for i in range(group):
        carry = times(matrix, carry)
        for k in range(MODES):
            out_ref[pl.ds(i * MODES + k, groups, stride=group * MODES), :] = sums[i][k] + carry[k]


def scan_part(terms, speeds):
    return pl.pallas_call(
        functools.partial(scan_kernel, 8),
        out_shape=jax.ShapeDtypeStruct(terms.shape, jnp.float32),
        in_specs=[pl.BlockSpec(memory_space=pltpu.VMEM)] * 2,
        out_specs=pl.BlockSpec(memory_space=pltpu.VMEM),
        name="slab_scan",
    )(terms, speeds)


def body(initial, guess, speeds, flags):
    slabs, blocks = lax.axis_size("tm"), lax.axis_size("space")
    count = initial.shape[1]
    rows = count // LANES

    def by_row(x):
        return x.reshape(MODES, rows, LANES).transpose(1, 0, 2).reshape(rows * MODES, LANES)

    last = lax.axis_index("tm") == slabs - 1

    def strip(lo):
        cut = slice(lo, lo + LANES)
        state = jnp.where(last, initial[:, cut], guess[0][:, cut])
        coefs = jnp.stack([speeds[cut], (1 - flags[cut]).astype(jnp.float32)])
        return jnp.concatenate([state, coefs, jnp.zeros((2, LANES), jnp.float32)], 0)

    left = lax.ppermute(strip(count - LANES), "space", [(i, i + 1) for i in range(blocks - 1)])
    right = lax.ppermute(strip(0), "space", [(i + 1, i) for i in range(blocks - 1)])
    speed_rows = speeds.reshape(rows, LANES)
    terms = fine_part(
        by_row(guess[0]), by_row(initial), left, right, speed_rows, flags.reshape(rows, LANES), slabs, blocks
    )
    terms = lax.all_to_all(terms.reshape(rows, MODES, LANES), "tm", 0, 0, tiled=True)
    sums = scan_part(terms.reshape(rows * MODES, LANES), speed_rows)
    sums = lax.all_to_all(sums.reshape(rows, MODES, LANES), "tm", 0, 0, tiled=True)
    return sums.transpose(1, 0, 2).reshape(1, MODES, count)


def solution(mesh):
    return jax.shard_map(
        body,
        mesh=mesh,
        in_specs=(P(None, "space"), P("tm", None, "space"), P("space"), P("space")),
        out_specs=P("tm", None, "space"),
        check_vma=False,
    )
```

time: 546 us -> 73.4 us (0.13)
  waiting for transfers between devices: 173 us -> 6.78 us
  starting transfers between devices: 143 us -> 4.31 us
  other arithmetic: 140 us -> 1.51 us
  matrix products: 58 us -> 0 us
  blocking collectives: 0 us -> 51.5 us
  between operations: 13.6 us -> 0.04 us
  local copies, waits for them, and re-layouts: 11 us -> 3.31 us
  Pallas kernels: 0 us -> 5.49 us
    all_gather x1 -> x0, waiting for transfers between devices: 151 us -> none  [body(): gathered = lax.all_gather(residual[None], 'tm', axis=0, tiled=True)]
    ppermute x51 -> x2, starting transfers between devices: 143 us -> 4.31 us  [the longest x1 2.41 us: body(): lax.ppermute(strip(count - LANES), 'space', [(i, i + 1) for i in range(bl...]
    select_n x65 -> x1, other arithmetic: 70.4 us -> 0.73 us  [strip(): state = jnp.where(last, initial[:, cut], guess[0][:, cut])]
    dot_general x54 -> x0, matrix products: 58 us -> none  [multiply(): jnp.einsum('ij,je->ie', jnp.asarray(table, field.dtype), field, precision...]
    all_to_all x0 -> x2, blocking collectives: none -> 51.5 us  [the longest x1 30.3 us: body(): lax.all_to_all(terms.reshape(rows, MODES, LANES), 'tm', 0, 0, tiled=True)]
    reduce_sum x91 -> x0, other arithmetic: 51.3 us -> none  [the longest x24 26.3 us: spatial_rhs(): slope_r = jnp.sum(column(right_slope, dtype) * padded, 0)]
    ppermute x51 -> x2, waiting for transfers between devices: 22.5 us -> 6.78 us  [the longest x1 6.78 us: body(): lax.ppermute(strip(count - LANES), 'space', [(i, i + 1) for i in range(bl...]
    mul x96 -> x0, other arithmetic: 8.02 us -> none  [the longest x24 1.95 us: spatial_rhs(): 0.5 * jumps[1:] * column(right_slope, dtype)]
  transfers between devices with their start and end apart: 52 -> 2, of which waited for: 18 -> 1; matrix products, arithmetic and copies ran while one was open for 5% -> 0% of each run, Pallas kernels for 0% -> 0%
where the time goes in v1:
time: 73.4 us; the launch traced here: 73 us
  blocking collectives  51.5 us (70%)
  waiting for transfers between devices  6.78 us (9%)
  Pallas kernels  5.49 us (7%)
  starting transfers between devices  4.31 us (6%)
  local copies, waits for them, and re-layouts  3.31 us (5%)
  other arithmetic  1.51 us (2%)
    all_to_all x1, blocking collectives, body(): lax.all_to_all(terms.reshape(rows, MODES, LANES), 'tm', 0, 0, tiled=True)  30.3 us
    all_to_all x1, blocking collectives, body(): lax.all_to_all(sums.reshape(rows, MODES, LANES), 'tm', 0, 0, tiled=True)  21.3 us
    ppermute x1, waiting for transfers between devices, body(): lax.ppermute(strip(count - LANES), 'space', [(i, i + 1) for i in range(bl...  6.78 us
    pallas_call x1, Pallas kernels, fine_part(): pl.pallas_call(functools.partial(fine_kernel, slabs, blocks), out_shape=j...  3.63 us
    unnamed x9, local copies, waits for them, and re-layouts  2.47 us
    ppermute x1, starting transfers between devices, body(): lax.ppermute(strip(count - LANES), 'space', [(i, i + 1) for i in range(bl...  2.41 us
    ppermute x1, starting transfers between devices, body(): lax.ppermute(strip(0), 'space', [(i + 1, i) for i in range(blocks - 1)])  1.91 us
    pallas_call x1, Pallas kernels, scan_part(): pl.pallas_call(functools.partial(scan_kernel, 8), out_shape=jax.ShapeDtyp...  1.86 us
  transfers between devices with their start and end apart: 2, of which 1 were waited for; matrix products, arithmetic and copies ran while one was open for 0% of the time, Pallas kernels for 0%

profile of v1, /device:TPU:2, one launch (start us, length us, event | category | flops | bytes accessed | tf_op | source)
XLA Modules:
  0.0 73.0 jit_solution(17557657044307791817)
XLA Ops:
  0.0 0.0 copy-start.3
  0.0 0.0 copy-start.2
  0.0 0.8 %slice_bitcast_fusion = (f32[1,128]{1,0:T(1,128)S(1)}, f32[1,128]{1,0:T(1,128)S(1)}) fusion(f32[8192]{0:T(1024)} %param.6), kind=kLoop, calls=%fused_computation.5 | loop fusion | bytes 2048 | tf_op jit(solution)/shard_map/stack | solution.py:206
  0.8 0.7 convert_bitcast_fusion
  1.5 0.1 pad.7.clone
  1.6 0.7 %slice_select_fusion = (f32[4,128]{1,0:T(4,128)S(1)}, f32[4,128]{1,0:T(4,128)S(1)}) fusion(f32[4,8192]{1,0:T(4,128)} %bitcast.28, f32[4,8192]{1,0:T(4,128)} %param.4, pred[]{:T(512)S(6)} %eq.3), kind=kLoop, calls=%fused_computation.2 | loop fusion | flops 1024 | bytes 12289 | tf_op jit(solution)/shard_map/jit(_where)/select_n | solution.py:205
  2.3 0.1 maximum_maximum_fusion.1
  2.4 1.9 %collective-permute-start.1 = (f32[8,128]{1,0:T(8,128)S(1)}, f32[8,128]{1,0:T(8,128)S(1)}, u32[]{:S(2)}, u32[]{:S(2)}) collective-permute-start(f32[8,128]{1,0:T(8,128)S(1)} %get-tuple-element.11), channel_id=1, source_target_pairs={{1,0},{2,1},{3,2},{4,3},{5,4},{6,5},{7,6},{9,8},{10,9},{11,10},{12... | collective-permute-start | bytes 12296 | tf_op jit(solution)/shard_map/ppermute | solution.py:210
  4.3 2.4 %collective-permute-start = (f32[8,128]{1,0:T(8,128)S(1)}, f32[8,128]{1,0:T(8,128)S(1)}, u32[]{:S(2)}, u32[]{:S(2)}) collective-permute-start(f32[8,128]{1,0:T(8,128)S(1)} %get-tuple-element.12), channel_id=1, source_target_pairs={{0,1},{1,2},{2,3},{3,4},{4,5},{5,6},{6,7},{8,9},{9,10},{10,11},{11... | collective-permute-start | bytes 12296 | tf_op jit(solution)/shard_map/ppermute | solution.py:209
  6.7 0.0 collective-permute-done.1.right_ref
  6.7 6.8 %collective-permute-done.left_ref = f32[8,128]{1,0:T(8,128)S(1)} collective-permute-done((f32[8,128]{1,0:T(8,128)S(1)}, f32[8,128]{1,0:T(8,128)S(1)}, u32[]{:S(2)}, u32[]{:S(2)}) %collective-permute-start) | collective-permute-done | bytes 4128 | tf_op jit(solution)/shard_map/ppermute | solution.py:209
  13.5 0.0 copy-done.3
  13.5 0.0 copy-done.2
  13.5 0.0 copy-start
  13.5 0.9 %copy-done = f32[1,4,8192]{2,1,0:T(4,128)S(1)} copy-done((f32[1,4,8192]{2,1,0:T(4,128)S(1)}, f32[1,4,8192]{2,1,0:T(4,128)}, u32[]{:S(2)}) %copy-start) | copy-done | bytes 131096
  14.4 0.0 copy-start.1
  14.4 0.9 %copy-done.1 = f32[4,8192]{1,0:T(4,128)S(1)} copy-done((f32[4,8192]{1,0:T(4,128)S(1)}, f32[4,8192]{1,0:T(4,128)}, u32[]{:S(2)}) %copy-start.1) | copy-done | bytes 131096
  15.3 3.6 %fine_steps.1 = f32[256,128]{1,0:T(8,128)S(1)} custom-call(f32[256,128]{1,0:T(8,128)S(1)} %bitcast.29, f32[256,128]{1,0:T(8,128)S(1)} %bitcast.30, f32[8,128]{1,0:T(8,128)S(1)} %collective-permute-done.left_ref, f32[8,128]{1,0:T(8,128)S(1)} %collective-permute-done.1.right_ref, f32[64,128]{1,0:T(8,128)S(1)} %bitcast.32, s32[64,128]{1,0:T(8,128)S(1)} %bitcast.33), custom_call_target="tpu_custom_call" | custom-call | flops 11796480 | bytes 524288 | tf_op jit(solution)/shard_map/fine_steps/pallas_call | solution.py:124
  18.9 30.3 %all_to_all.10 = f32[64,4,128]{2,1,0:T(4,128)} all-to-all(f32[64,4,128]{2,1,0:T(4,128)S(1)} %bitcast.27), channel_id=1, replica_groups=mesh['tm'=64,'space'=8] {'tm'}, dimensions={0} | all-to-all | bytes 262144 | tf_op jit(solution)/shard_map/all_to_all | solution.py:215
  49.2 1.9 %slab_scan.1 = f32[256,128]{1,0:T(8,128)} custom-call(f32[256,128]{1,0:T(8,128)} %bitcast.34, f32[64,128]{1,0:T(8,128)} %bitcast.31), custom_call_target="tpu_custom_call" | custom-call | tf_op jit(solution)/shard_map/slab_scan/pallas_call | solution.py:184
  51.1 21.3 %all_to_all.11 = f32[64,4,128]{2,1,0:T(4,128)S(1)} all-to-all(f32[64,4,128]{2,1,0:T(4,128)} %bitcast.35), channel_id=1, replica_groups=mesh['tm'=64,'space'=8] {'tm'}, dimensions={0} | all-to-all | bytes 262144 | tf_op jit(solution)/shard_map/all_to_all | solution.py:217
  72.3 0.7 copy.9
  (1 shorter events, 0.0 us)
Async XLA Ops:
  0.0 13.5 %copy-start.3 = (s32[8192]{0:T(1024)S(1)}, s32[8192]{0:T(1024)}, u32[]{:S(2)}) copy-start(s32[8192]{0:T(1024)} %param.7) | copy-start | bytes 98308
  0.0 13.5 %copy-start.2 = (f32[8192]{0:T(1024)S(1)}, f32[8192]{0:T(1024)}, u32[]{:S(2)}) copy-start(f32[8192]{0:T(1024)} %param.6) | copy-start | bytes 98308
  2.4 4.3 %collective-permute-start.1 = (f32[8,128]{1,0:T(8,128)S(1)}, f32[8,128]{1,0:T(8,128)S(1)}, u32[]{:S(2)}, u32[]{:S(2)}) collective-permute-start(f32[8,128]{1,0:T(8,128)S(1)} %get-tuple-element.11), channel_id=1, source_target_pairs={{1,0},{2,1},{3,2},{4,3},{5,4},{6,5},{7,6},{9,8},{10,9},{11,10},{12... | collective-permute-start | bytes 12296 | tf_op jit(solution)/shard_map/ppermute | solution.py:210
  4.3 9.2 %collective-permute-start = (f32[8,128]{1,0:T(8,128)S(1)}, f32[8,128]{1,0:T(8,128)S(1)}, u32[]{:S(2)}, u32[]{:S(2)}) collective-permute-start(f32[8,128]{1,0:T(8,128)S(1)} %get-tuple-element.12), channel_id=1, source_target_pairs={{0,1},{1,2},{2,3},{3,4},{4,5},{5,6},{6,7},{8,9},{9,10},{10,11},{11... | collective-permute-start | bytes 12296 | tf_op jit(solution)/shard_map/ppermute | solution.py:209
  13.5 0.9 %copy-start = (f32[1,4,8192]{2,1,0:T(4,128)S(1)}, f32[1,4,8192]{2,1,0:T(4,128)}, u32[]{:S(2)}) copy-start(f32[1,4,8192]{2,1,0:T(4,128)} %param.5) | copy-start | bytes 393220
  14.4 0.9 %copy-start.1 = (f32[4,8192]{1,0:T(4,128)S(1)}, f32[4,8192]{1,0:T(4,128)}, u32[]{:S(2)}) copy-start(f32[4,8192]{1,0:T(4,128)} %param.4) | copy-start | bytes 393220

commit v2 on v1

--- a/solution.py
+++ b/solution.py
@@ -81,25 +81,41 @@
     return v
 
 
-def fine_kernel(slabs, blocks, guess_ref, initial_ref, left_ref, right_ref, speed_ref, flag_ref, out_ref):
+def strip_kernel(state_ref, speed_ref, flag_ref, head_ref, tail_ref):
+    rows = speed_ref.shape[0]
+    for ref, row in ((head_ref, 0), (tail_ref, rows - 1)):
+        ref[pl.ds(0, MODES), :] = state_ref[pl.ds(row * MODES, MODES), :]
+        ref[pl.ds(MODES, 1), :] = speed_ref[pl.ds(row, 1), :]
+        ref[pl.ds(MODES + 1, 1), :] = 1.0 - flag_ref[pl.ds(row, 1), :].astype(jnp.float32)
+        ref[pl.ds(MODES + 2, 2), :] = jnp.zeros((2, LANES), jnp.float32)
+
+
+def strip_part(state, speeds, flags):
+    strip = jax.ShapeDtypeStruct((8, LANES), jnp.float32)
+    return pl.pallas_call(
+        strip_kernel,
+        out_shape=[strip, strip],
+        in_specs=[pl.BlockSpec(memory_space=pltpu.VMEM)] * 3,
+        out_specs=[pl.BlockSpec(memory_space=pltpu.VMEM)] * 2,
+        name="end_strips",
+    )(state, speeds, flags)
+
+
+def fine_kernel(slabs, state_ref, speed_ref, flag_ref, left_ref, right_ref, out_ref):
     rows = speed_ref.shape[0]
     wide = rows + 8
-    slab, block = lax.axis_index("tm"), lax.axis_index("space")
-    last = slab == slabs - 1
+    last = lax.axis_index("tm") == slabs - 1
+    block = lax.axis_index("space")
 
     def ring(main, k):
         unused = jnp.zeros((6, LANES), jnp.float32)
         return jnp.concatenate([main, right_ref[pl.ds(k, 1), :], unused, left_ref[pl.ds(k, 1), :]], 0)
 
-    own = []
-    for k in range(MODES):
-        here = pl.ds(k, rows, stride=MODES)
-        own.append(jnp.where(last, initial_ref[here, :], guess_ref[here, :]))
+    own = [state_ref[pl.ds(k, rows, stride=MODES), :] for k in range(MODES)]
     start = [ring(x, k) for k, x in enumerate(own)]
     speed_own = speed_ref[...]
-    open_own = 1.0 - flag_ref[...].astype(jnp.float32)
     speed = ring(speed_own, MODES)
-    opened = ring(open_own, MODES + 1)
+    opened = ring(1.0 - flag_ref[...].astype(jnp.float32), MODES + 1)
     row = lax.broadcasted_iota(jnp.int32, (wide, LANES), 0)
     lane = lax.broadcasted_iota(jnp.int32, (wide, LANES), 1)
     first = jnp.logical_and(jnp.logical_and(row == 0, lane == 0), block == 0)
@@ -120,16 +136,16 @@
         out_ref[pl.ds(k, rows, stride=MODES), :] = final[k][:rows] - share
 
 
-def fine_part(guess, initial, left, right, speeds, flags, slabs, blocks):
+def fine_part(state, speeds, flags, left, right, slabs):
     return pl.pallas_call(
-        functools.partial(fine_kernel, slabs, blocks),
-        out_shape=jax.ShapeDtypeStruct(guess.shape, jnp.float32),
-        in_specs=[pl.BlockSpec(memory_space=pltpu.VMEM)] * 6,
+        functools.partial(fine_kernel, slabs),
+        out_shape=jax.ShapeDtypeStruct(state.shape, jnp.float32),
+        in_specs=[pl.BlockSpec(memory_space=pltpu.VMEM)] * 5,
         out_specs=pl.BlockSpec(memory_space=pltpu.VMEM),
         compiler_params=pltpu.CompilerParams(vmem_limit_bytes=16 * 1024 * 1024),
-        cost_estimate=pl.CostEstimate(flops=24 * 60 * 8192, bytes_accessed=4 * guess.size * 4, transcendentals=0),
+        cost_estimate=pl.CostEstimate(flops=24 * 60 * 8192, bytes_accessed=2 * state.size * 4, transcendentals=0),
         name="fine_steps",
-    )(guess, initial, left, right, speeds, flags)
+    )(state, speeds, flags, left, right)
 
 
 def times(matrix, field):
@@ -198,20 +214,13 @@
     def by_row(x):
         return x.reshape(MODES, rows, LANES).transpose(1, 0, 2).reshape(rows * MODES, LANES)
 
+    speed_rows, flag_rows = speeds.reshape(rows, LANES), flags.reshape(rows, LANES)
     last = lax.axis_index("tm") == slabs - 1
-
-    def strip(lo):
-        cut = slice(lo, lo + LANES)
-        state = jnp.where(last, initial[:, cut], guess[0][:, cut])
-        coefs = jnp.stack([speeds[cut], (1 - flags[cut]).astype(jnp.float32)])
-        return jnp.concatenate([state, coefs, jnp.zeros((2, LANES), jnp.float32)], 0)
-
-    left = lax.ppermute(strip(count - LANES), "space", [(i, i + 1) for i in range(blocks - 1)])
-    right = lax.ppermute(strip(0), "space", [(i + 1, i) for i in range(blocks - 1)])
-    speed_rows = speeds.reshape(rows, LANES)
-    terms = fine_part(
-        by_row(guess[0]), by_row(initial), left, right, speed_rows, flags.reshape(rows, LANES), slabs, blocks
-    )
+    state = by_row(jnp.where(last, initial, guess[0]))
+    head, tail = strip_part(state, speed_rows, flag_rows)
+    left = lax.ppermute(tail, "space", [(i, i + 1) for i in range(blocks - 1)])
+    right = lax.ppermute(head, "space", [(i + 1, i) for i in range(blocks - 1)])
+    terms = fine_part(state, speed_rows, flag_rows, left, right, slabs)
     terms = lax.all_to_all(terms.reshape(rows, MODES, LANES), "tm", 0, 0, tiled=True)
     sums = scan_part(terms.reshape(rows * MODES, LANES), speed_rows)
     sums = lax.all_to_all(sums.reshape(rows, MODES, LANES), "tm", 0, 0, tiled=True)

time: 73.4 us -> 74.7 us (1.018)
  the two profiles are of different devices: /device:TPU:2 before, /device:TPU:4 now
where the time goes in v2:
time: 74.7 us; the launch traced here: 74.5 us
  blocking collectives  58 us (78%)
  Pallas kernels  7.06 us (9%)
  starting transfers between devices  5.55 us (7%)
  other arithmetic  1.6 us (2%)
  waiting for transfers between devices  1.51 us (2%)
    all_to_all x1, blocking collectives, body(): lax.all_to_all(terms.reshape(rows, MODES, LANES), 'tm', 0, 0, tiled=True)  35.3 us
    all_to_all x1, blocking collectives, body(): lax.all_to_all(sums.reshape(rows, MODES, LANES), 'tm', 0, 0, tiled=True)  22.8 us
    ppermute x1, starting transfers between devices, body(): right = lax.ppermute(head, 'space', [(i + 1, i) for i in range(blocks - 1)])  3.64 us
    pallas_call x1, Pallas kernels, fine_part(): pl.pallas_call(functools.partial(fine_kernel, slabs), out_shape=jax.Shape...  3.62 us
    ppermute x1, starting transfers between devices, body(): left = lax.ppermute(tail, 'space', [(i, i + 1) for i in range(blocks - 1)])  1.91 us
    pallas_call x1, Pallas kernels, scan_part(): pl.pallas_call(functools.partial(scan_kernel, 8), out_shape=jax.ShapeDtyp...  1.86 us
    select_n x1, other arithmetic, body(): state = by_row(jnp.where(last, initial, guess[0]))  1.6 us
    pallas_call x1, Pallas kernels, strip_part(): pl.pallas_call(strip_kernel, out_shape=[strip, strip], in_specs=[pl.Block...  1.58 us
  transfers between devices with their start and end apart: 2, of which 1 were waited for; matrix products, arithmetic and copies ran while one was open for 0% of the time, Pallas kernels for 0%

profile of v2, /device:TPU:4, one launch (start us, length us, event | category | flops | bytes accessed | tf_op | source)
XLA Modules:
  0.0 74.5 jit_solution(16929845471704459009)
XLA Ops:
  0.0 1.6 %bitcast_select_fusion = f32[4,8192]{1,0:T(4,128)} fusion(f32[4,8192]{1,0:T(4,128)} %param.4, f32[1,4,8192]{2,1,0:T(4,128)} %param.5, pred[]{:T(512)S(6)} %eq.3), kind=kLoop, calls=%fused_computation | loop fusion | flops 32768 | bytes 393217 | tf_op jit(solution)/shard_map/jit(_where)/select_n | solution.py:219
  1.6 0.0 copy-start
  1.6 0.0 copy-start.1
  1.6 0.0 copy-start.2
  1.6 1.6 %end_strips.1 = (f32[8,128]{1,0:T(8,128)}, f32[8,128]{1,0:T(8,128)}) custom-call(f32[256,128]{1,0:T(8,128)} %bitcast.15, f32[64,128]{1,0:T(8,128)} %bitcast.18, s32[64,128]{1,0:T(8,128)} %bitcast.21), custom_call_target="tpu_custom_call" | custom-call | tf_op jit(solution)/shard_map/end_strips/pallas_call | solution.py:95
  3.2 1.9 %collective-permute-start = (f32[8,128]{1,0:T(8,128)}, f32[8,128]{1,0:T(8,128)S(1)}, u32[]{:S(2)}, u32[]{:S(2)}) collective-permute-start(f32[8,128]{1,0:T(8,128)} %get-tuple-element.7), channel_id=1, source_target_pairs={{0,1},{1,2},{2,3},{3,4},{4,5},{5,6},{6,7},{8,9},{9,10},{10,11},{11... | collective-permute-start | bytes 12296 | tf_op jit(solution)/shard_map/ppermute | solution.py:221
  5.1 3.6 %collective-permute-start.1 = (f32[8,128]{1,0:T(8,128)}, f32[8,128]{1,0:T(8,128)S(1)}, u32[]{:S(2)}, u32[]{:S(2)}) collective-permute-start(f32[8,128]{1,0:T(8,128)} %get-tuple-element.8), channel_id=1, source_target_pairs={{1,0},{2,1},{3,2},{4,3},{5,4},{6,5},{7,6},{9,8},{10,9},{11,10},{12... | collective-permute-start | bytes 12296 | tf_op jit(solution)/shard_map/ppermute | solution.py:222
  8.7 0.0 collective-permute-done.left_ref
  8.8 1.5 %collective-permute-done.1.right_ref = f32[8,128]{1,0:T(8,128)S(1)} collective-permute-done((f32[8,128]{1,0:T(8,128)}, f32[8,128]{1,0:T(8,128)S(1)}, u32[]{:S(2)}, u32[]{:S(2)}) %collective-permute-start.1) | collective-permute-done | bytes 4128 | tf_op jit(solution)/shard_map/ppermute | solution.py:222
  10.3 0.0 copy-done
  10.3 0.0 copy-done.1
  10.3 0.0 copy-done.2
  10.3 3.6 %fine_steps.1 = f32[256,128]{1,0:T(8,128)S(1)} custom-call(f32[256,128]{1,0:T(8,128)S(1)} %bitcast.16, f32[64,128]{1,0:T(8,128)S(1)} %bitcast.20, s32[64,128]{1,0:T(8,128)S(1)} %bitcast.22, f32[8,128]{1,0:T(8,128)S(1)} %collective-permute-done.left_ref, f32[8,128]{1,0:T(8,128)S(1)} %collective-permute-done.1.right_ref), custom_call_target="tpu_custom_call" | custom-call | flops 11796480 | bytes 262144 | tf_op jit(solution)/shard_map/fine_steps/pallas_call | solution.py:140
  13.9 35.3 %all_to_all.10 = f32[64,4,128]{2,1,0:T(4,128)} all-to-all(f32[64,4,128]{2,1,0:T(4,128)S(1)} %bitcast.17), channel_id=1, replica_groups=mesh['tm'=64,'space'=8] {'tm'}, dimensions={0} | all-to-all | bytes 262144 | tf_op jit(solution)/shard_map/all_to_all | solution.py:224
  49.2 1.9 %slab_scan.1 = f32[256,128]{1,0:T(8,128)} custom-call(f32[256,128]{1,0:T(8,128)} %bitcast.23, f32[64,128]{1,0:T(8,128)} %bitcast.19), custom_call_target="tpu_custom_call" | custom-call | tf_op jit(solution)/shard_map/slab_scan/pallas_call | solution.py:200
  51.0 22.8 %all_to_all.11 = f32[64,4,128]{2,1,0:T(4,128)S(1)} all-to-all(f32[64,4,128]{2,1,0:T(4,128)} %bitcast.24), channel_id=1, replica_groups=mesh['tm'=64,'space'=8] {'tm'}, dimensions={0} | all-to-all | bytes 262144 | tf_op jit(solution)/shard_map/all_to_all | solution.py:226
  73.8 0.7 copy.8
Async XLA Ops:
  1.6 8.7 %copy-start = (f32[4,8192]{1,0:T(4,128)S(1)}, f32[4,8192]{1,0:T(4,128)}, u32[]{:S(2)}) copy-start(f32[4,8192]{1,0:T(4,128)} %bitcast_select_fusion) | copy-start | bytes 393220
  1.6 8.7 %copy-start.1 = (f32[8192]{0:T(1024)S(1)}, f32[8192]{0:T(1024)}, u32[]{:S(2)}) copy-start(f32[8192]{0:T(1024)} %param.6) | copy-start | bytes 98308
  1.6 8.7 %copy-start.2 = (s32[8192]{0:T(1024)S(1)}, s32[8192]{0:T(1024)}, u32[]{:S(2)}) copy-start(s32[8192]{0:T(1024)} %param.7) | copy-start | bytes 98308
  3.2 5.6 %collective-permute-start = (f32[8,128]{1,0:T(8,128)}, f32[8,128]{1,0:T(8,128)S(1)}, u32[]{:S(2)}, u32[]{:S(2)}) collective-permute-start(f32[8,128]{1,0:T(8,128)} %get-tuple-element.7), channel_id=1, source_target_pairs={{0,1},{1,2},{2,3},{3,4},{4,5},{5,6},{6,7},{8,9},{9,10},{10,11},{11... | collective-permute-start | bytes 12296 | tf_op jit(solution)/shard_map/ppermute | solution.py:221
  5.1 5.2 %collective-permute-start.1 = (f32[8,128]{1,0:T(8,128)}, f32[8,128]{1,0:T(8,128)S(1)}, u32[]{:S(2)}, u32[]{:S(2)}) collective-permute-start(f32[8,128]{1,0:T(8,128)} %get-tuple-element.8), channel_id=1, source_target_pairs={{1,0},{2,1},{3,2},{4,3},{5,4},{6,5},{7,6},{9,8},{10,9},{11,10},{12... | collective-permute-start | bytes 12296 | tf_op jit(solution)/shard_map/ppermute | solution.py:222

commit v3 on v2

--- a/solution.py
+++ b/solution.py
@@ -10,6 +10,7 @@
 MODES = 4
 STEPS = 8
 LANES = 128
+ROWS = 8
 VISCOSITY = 0.02
 PENALTY = 10.0
 STEP = 0.015625
@@ -81,35 +82,77 @@
     return v
 
 
-def strip_kernel(state_ref, speed_ref, flag_ref, head_ref, tail_ref):
+def strip_kernel(slabs, guess_ref, initial_ref, speed_ref, flag_ref, near_ref, far_ref, states, speeds, flags, sems):
     rows = speed_ref.shape[0]
-    for ref, row in ((head_ref, 0), (tail_ref, rows - 1)):
-        ref[pl.ds(0, MODES), :] = state_ref[pl.ds(row * MODES, MODES), :]
-        ref[pl.ds(MODES, 1), :] = speed_ref[pl.ds(row, 1), :]
-        ref[pl.ds(MODES + 1, 1), :] = 1.0 - flag_ref[pl.ds(row, 1), :].astype(jnp.float32)
-        ref[pl.ds(MODES + 2, 2), :] = jnp.zeros((2, LANES), jnp.float32)
-
-
-def strip_part(state, speeds, flags):
-    strip = jax.ShapeDtypeStruct((8, LANES), jnp.float32)
+    last = lax.axis_index("tm") == slabs - 1
+    ends = (0, 1)
+
+    def tile(ref, end):
+        return ref.at[pl.ds(end * (ref.shape[0] - ROWS), ROWS)]
+
+    def copies(source):
+        return [pltpu.make_async_copy(tile(source, e), states.at[e], sems.at[e]) for e in ends]
+
+    others = [pltpu.make_async_copy(tile(speed_ref, e), speeds.at[e], sems.at[2 + e]) for e in ends]
+    others += [pltpu.make_async_copy(tile(flag_ref, e), flags.at[e], sems.at[4 + e]) for e in ends]
+
+    @pl.when(last)
+    def _():
+        for copy in copies(initial_ref):
+            copy.start()
+
+    @pl.when(jnp.logical_not(last))
+    def _():
+        for copy in copies(guess_ref):
+            copy.start()
+
+    for copy in others:
+        copy.start()
+    for copy in others + copies(guess_ref):
+        copy.wait()
+    strips = []
+    for end in ends:
+        row = end * (ROWS - 1)
+        state = states[end, pl.ds(end * (ROWS - MODES), MODES), :]
+        opened = 1.0 - flags[end, pl.ds(row, 1), :].astype(jnp.float32)
+        unused = jnp.zeros((2, LANES), jnp.float32)
+        strips.append(jnp.concatenate([state, speeds[end, pl.ds(row, 1), :], opened, unused], 0))
+    head, tail = strips
+    even = lax.axis_index("space") % 2 == 0
+    near_ref[...] = jnp.where(even, tail, head)
+    far_ref[...] = jnp.where(even, head, tail)
+
+
+def strip_part(guess, initial, speeds, flags, slabs):
+    strip = jax.ShapeDtypeStruct((ROWS, LANES), jnp.float32)
     return pl.pallas_call(
-        strip_kernel,
+        functools.partial(strip_kernel, slabs),
         out_shape=[strip, strip],
-        in_specs=[pl.BlockSpec(memory_space=pltpu.VMEM)] * 3,
+        in_specs=[pl.BlockSpec(memory_space=pltpu.HBM)] * 4,
         out_specs=[pl.BlockSpec(memory_space=pltpu.VMEM)] * 2,
+        scratch_shapes=[
+            pltpu.VMEM((2, ROWS, LANES), jnp.float32),
+            pltpu.VMEM((2, ROWS, LANES), jnp.float32),
+            pltpu.VMEM((2, ROWS, LANES), jnp.int32),
+            pltpu.SemaphoreType.DMA((6,)),
+        ],
+        compiler_params=pltpu.CompilerParams(vmem_limit_bytes=60 * 1024 * 1024),
         name="end_strips",
-    )(state, speeds, flags)
-
-
-def fine_kernel(slabs, state_ref, speed_ref, flag_ref, left_ref, right_ref, out_ref):
+    )(guess, initial, speeds, flags)
+
+
+def fine_kernel(slabs, state_ref, speed_ref, flag_ref, near_ref, far_ref, out_ref):
     rows = speed_ref.shape[0]
     wide = rows + 8
     last = lax.axis_index("tm") == slabs - 1
     block = lax.axis_index("space")
+    even = block % 2 == 0
+    near, far = near_ref[...], far_ref[...]
+    left, right = jnp.where(even, far, near), jnp.where(even, near, far)
 
     def ring(main, k):
         unused = jnp.zeros((6, LANES), jnp.float32)
-        return jnp.concatenate([main, right_ref[pl.ds(k, 1), :], unused, left_ref[pl.ds(k, 1), :]], 0)
+        return jnp.concatenate([main, right[k : k + 1], unused, left[k : k + 1]], 0)
 
     own = [state_ref[pl.ds(k, rows, stride=MODES), :] for k in range(MODES)]
     start = [ring(x, k) for k, x in enumerate(own)]
@@ -136,7 +179,7 @@
         out_ref[pl.ds(k, rows, stride=MODES), :] = final[k][:rows] - share
 
 
-def fine_part(state, speeds, flags, left, right, slabs):
+def fine_part(state, speeds, flags, near, far, slabs):
     return pl.pallas_call(
         functools.partial(fine_kernel, slabs),
         out_shape=jax.ShapeDtypeStruct(state.shape, jnp.float32),
@@ -145,7 +188,7 @@
         compiler_params=pltpu.CompilerParams(vmem_limit_bytes=16 * 1024 * 1024),
         cost_estimate=pl.CostEstimate(flops=24 * 60 * 8192, bytes_accessed=2 * state.size * 4, transcendentals=0),
         name="fine_steps",
-    )(state, speeds, flags, left, right)
+    )(state, speeds, flags, near, far)
 
 
 def times(matrix, field):
@@ -215,12 +258,12 @@
         return x.reshape(MODES, rows, LANES).transpose(1, 0, 2).reshape(rows * MODES, LANES)
 
     speed_rows, flag_rows = speeds.reshape(rows, LANES), flags.reshape(rows, LANES)
-    last = lax.axis_index("tm") == slabs - 1
-    state = by_row(jnp.where(last, initial, guess[0]))
-    head, tail = strip_part(state, speed_rows, flag_rows)
-    left = lax.ppermute(tail, "space", [(i, i + 1) for i in range(blocks - 1)])
-    right = lax.ppermute(head, "space", [(i + 1, i) for i in range(blocks - 1)])
-    terms = fine_part(state, speed_rows, flag_rows, left, right, slabs)
+    near, far = strip_part(by_row(guess[0]), by_row(initial), speed_rows, flag_rows, slabs)
+    ours, _ = lax.optimization_barrier((guess[0], near))
+    far = lax.ppermute(far, "space", [p for i in range(1, blocks - 1, 2) for p in ((i, i + 1), (i + 1, i))])
+    near = lax.ppermute(near, "space", [p for i in range(0, blocks, 2) for p in ((i, i + 1), (i + 1, i))])
+    state = by_row(jnp.where(lax.axis_index("tm") == slabs - 1, initial, ours))
+    terms = fine_part(state, speed_rows, flag_rows, near, far, slabs)
     terms = lax.all_to_all(terms.reshape(rows, MODES, LANES), "tm", 0, 0, tiled=True)
     sums = scan_part(terms.reshape(rows * MODES, LANES), speed_rows)
     sums = lax.all_to_all(sums.reshape(rows, MODES, LANES), "tm", 0, 0, tiled=True)

time: 74.7 us -> 71.7 us (0.960)
  the two profiles are of different devices: /device:TPU:4 before, /device:TPU:2 now
where the time goes in v3:
time: 71.7 us; the launch traced here: 71.4 us
  blocking collectives  57.3 us (80%)
  Pallas kernels  6.95 us (10%)
  starting transfers between devices  5.42 us (8%)
  waiting for transfers between devices  0.91 us (1%)
    all_to_all x1, blocking collectives, body(): lax.all_to_all(terms.reshape(rows, MODES, LANES), 'tm', 0, 0, tiled=True)  34.8 us
    all_to_all x1, blocking collectives, body(): lax.all_to_all(sums.reshape(rows, MODES, LANES), 'tm', 0, 0, tiled=True)  22.5 us
    pallas_call x1, Pallas kernels, fine_part(): pl.pallas_call(functools.partial(fine_kernel, slabs), out_shape=jax.Shape...  3.62 us
    ppermute x1, starting transfers between devices, body(): lax.ppermute(near, 'space', [p for i in range(0, blocks, 2) for p in ((i,...  3.5 us
    ppermute x1, starting transfers between devices, body(): lax.ppermute(far, 'space', [p for i in range(1, blocks - 1, 2) for p in (...  1.92 us
    pallas_call x1, Pallas kernels, scan_part(): pl.pallas_call(functools.partial(scan_kernel, 8), out_shape=jax.ShapeDtyp...  1.86 us
    pallas_call x1, Pallas kernels, strip_part(): pl.pallas_call(functools.partial(strip_kernel, slabs), out_shape=[strip,...  1.47 us
  transfers between devices with their start and end apart: 2, of which 1 were waited for; matrix products, arithmetic and copies ran while one was open for 0% of the time, Pallas kernels for 0%

profile of v3, /device:TPU:2, one launch (start us, length us, event | category | flops | bytes accessed | tf_op | source)
XLA Modules:
  0.0 71.4 jit_solution(16627302299875519893)
XLA Ops:
  0.0 0.0 copy-start.2
  0.0 0.0 copy-start.3
  0.0 1.5 %end_strips.1 = (f32[8,128]{1,0:T(8,128)}, f32[8,128]{1,0:T(8,128)}) custom-call(f32[256,128]{1,0:T(8,128)} %bitcast.32, f32[256,128]{1,0:T(8,128)} %bitcast.31, f32[64,128]{1,0:T(8,128)} %bitcast.26, s32[64,128]{1,0:T(8,128)} %bitcast.29), custom_call_target="tpu_custom_call" | custom-call | tf_op jit(solution)/shard_map/end_strips/pallas_call | solution.py:128
  1.5 1.9 %collective-permute-start.1 = (f32[8,128]{1,0:T(8,128)}, f32[8,128]{1,0:T(8,128)S(1)}, u32[]{:S(2)}, u32[]{:S(2)}) collective-permute-start(f32[8,128]{1,0:T(8,128)} %get-tuple-element.10), channel_id=1, source_target_pairs={{1,2},{2,1},{3,4},{4,3},{5,6},{6,5},{9,10},{10,9},{11,12},{12,11},... | collective-permute-start | bytes 12296 | tf_op jit(solution)/shard_map/ppermute | solution.py:263
  3.4 3.5 %collective-permute-start = (f32[8,128]{1,0:T(8,128)}, f32[8,128]{1,0:T(8,128)S(1)}, u32[]{:S(2)}, u32[]{:S(2)}) collective-permute-start(f32[8,128]{1,0:T(8,128)} %get-tuple-element.8), channel_id=1, source_target_pairs={{0,1},{1,0},{2,3},{3,2},{4,5},{5,4},{6,7},{7,6},{8,9},{9,8},{10,11... | collective-permute-start | bytes 12296 | tf_op jit(solution)/shard_map/ppermute | solution.py:264
  6.9 0.0 copy-done.2
  6.9 0.0 copy-done.3
  7.0 0.0 copy-start
  7.0 0.0 copy-start.1
  7.0 0.0 collective-permute-done.1.far_ref
  7.0 0.9 %collective-permute-done.near_ref = f32[8,128]{1,0:T(8,128)S(1)} collective-permute-done((f32[8,128]{1,0:T(8,128)}, f32[8,128]{1,0:T(8,128)S(1)}, u32[]{:S(2)}, u32[]{:S(2)}) %collective-permute-start) | collective-permute-done | bytes 4128 | tf_op jit(solution)/shard_map/ppermute | solution.py:264
  7.9 0.0 copy-done
  7.9 0.0 copy-done.1
  7.9 3.6 %fine_steps.1 = f32[256,128]{1,0:T(8,128)S(1)} custom-call(f32[256,128]{1,0:T(8,128)S(1)} %bitcast.24, f32[64,128]{1,0:T(8,128)S(1)} %bitcast.28, s32[64,128]{1,0:T(8,128)S(1)} %bitcast.30, f32[8,128]{1,0:T(8,128)S(1)} %collective-permute-done.near_ref, f32[8,128]{1,0:T(8,128)S(1)} %collective-permute-done.1.far_ref), custom_call_target="tpu_custom_call" | custom-call | flops 11796480 | bytes 262144 | tf_op jit(solution)/shard_map/fine_steps/pallas_call | solution.py:183
  11.6 34.8 %all_to_all.10 = f32[64,4,128]{2,1,0:T(4,128)} all-to-all(f32[64,4,128]{2,1,0:T(4,128)S(1)} %bitcast.25), channel_id=1, replica_groups=mesh['tm'=64,'space'=8] {'tm'}, dimensions={0} | all-to-all | bytes 262144 | tf_op jit(solution)/shard_map/all_to_all | solution.py:267
  46.4 1.9 %slab_scan.1 = f32[256,128]{1,0:T(8,128)} custom-call(f32[256,128]{1,0:T(8,128)} %bitcast.34, f32[64,128]{1,0:T(8,128)} %bitcast.27), custom_call_target="tpu_custom_call" | custom-call | tf_op jit(solution)/shard_map/slab_scan/pallas_call | solution.py:243
  48.2 22.5 %all_to_all.11 = f32[64,4,128]{2,1,0:T(4,128)S(1)} all-to-all(f32[64,4,128]{2,1,0:T(4,128)} %bitcast.35), channel_id=1, replica_groups=mesh['tm'=64,'space'=8] {'tm'}, dimensions={0} | all-to-all | bytes 262144 | tf_op jit(solution)/shard_map/all_to_all | solution.py:269
  70.8 0.7 copy.10
  (1 shorter events, 0.0 us)
Async XLA Ops:
  0.0 6.9 %copy-start.2 = (f32[4,8192]{1,0:T(4,128)S(1)}, f32[4,8192]{1,0:T(4,128)}, u32[]{:S(2)}) copy-start(f32[4,8192]{1,0:T(4,128)} %param.4) | copy-start | bytes 393220
  0.0 6.9 %copy-start.3 = (f32[1,4,8192]{2,1,0:T(4,128)S(1)}, f32[1,4,8192]{2,1,0:T(4,128)}, u32[]{:S(2)}) copy-start(f32[1,4,8192]{2,1,0:T(4,128)} %param.5) | copy-start | bytes 393220
  1.5 5.5 %collective-permute-start.1 = (f32[8,128]{1,0:T(8,128)}, f32[8,128]{1,0:T(8,128)S(1)}, u32[]{:S(2)}, u32[]{:S(2)}) collective-permute-start(f32[8,128]{1,0:T(8,128)} %get-tuple-element.10), channel_id=1, source_target_pairs={{1,2},{2,1},{3,4},{4,3},{5,6},{6,5},{9,10},{10,9},{11,12},{12,11},... | collective-permute-start | bytes 12296 | tf_op jit(solution)/shard_map/ppermute | solution.py:263
  3.4 4.5 %collective-permute-start = (f32[8,128]{1,0:T(8,128)}, f32[8,128]{1,0:T(8,128)S(1)}, u32[]{:S(2)}, u32[]{:S(2)}) collective-permute-start(f32[8,128]{1,0:T(8,128)} %get-tuple-element.8), channel_id=1, source_target_pairs={{0,1},{1,0},{2,3},{3,2},{4,5},{5,4},{6,7},{7,6},{8,9},{9,8},{10,11... | collective-permute-start | bytes 12296 | tf_op jit(solution)/shard_map/ppermute | solution.py:264
  7.0 1.0 %copy-start = (f32[8192]{0:T(1024)S(1)}, f32[8192]{0:T(1024)}, u32[]{:S(2)}) copy-start(f32[8192]{0:T(1024)} %param.6) | copy-start | bytes 98308
  7.0 1.0 %copy-start.1 = (s32[8192]{0:T(1024)S(1)}, s32[8192]{0:T(1024)}, u32[]{:S(2)}) copy-start(s32[8192]{0:T(1024)} %param.7) | copy-start | bytes 98308

commit v4 on v3

--- a/solution.py
+++ b/solution.py
@@ -192,7 +192,13 @@
 
 
 def times(matrix, field):
-    return [sum(matrix[i][j] * field[j] for j in range(1, MODES)) + matrix[i][0] * field[0] for i in range(MODES)]
+    out = []
+    for row in matrix:
+        total = row[0] * field[0]
+        for entry, value in zip(row[1:], field[1:]):
+            total = total + entry * value
+        out.append(total)
+    return out
 
 
 def square(matrix):
@@ -200,53 +206,136 @@
     return [[columns[j][i] for j in range(MODES)] for i in range(MODES)]
 
 
-def scan_kernel(group, term_ref, speed_ref, out_ref):
-    slabs = term_ref.shape[0] // MODES
-    groups = slabs // group
-    shape = (groups, LANES)
-    row = lax.broadcasted_iota(jnp.int32, shape, 0)
-    speed = jnp.broadcast_to(speed_ref[pl.ds(lax.axis_index("tm"), 1), :], shape)
+def added(xs, ys):
+    return [x + y for x, y in zip(xs, ys)]
+
+
+def chosen(test, xs, ys):
+    return [jnp.where(test, x, y) for x, y in zip(xs, ys)]
+
+
+QUAD = 4
+CHUNK = 4
+HALVES = 2
+
+
+def place():
+    slab = lax.axis_index("tm")
+    y, z = slab // (QUAD * QUAD), slab % (QUAD * QUAD)
+    return z // QUAD, (z % QUAD) * QUAD + y
+
+
+def coarse_matrix(speed_ref, chunk):
+    rows = [speed_ref[pl.ds(chunk * CHUNK + r, 1), :] for r in range(CHUNK)]
+    speed = jnp.concatenate(rows * (ROWS // CHUNK), 0)
     speed2 = 2.0 * speed
-    zero, one = jnp.zeros(shape, jnp.float32), jnp.ones(shape, jnp.float32)
+    zero, one = jnp.zeros_like(speed), jnp.ones_like(speed)
     columns = [
         three_sections([one if i == j else zero for i in range(MODES)], lambda u: local_rhs(u, speed, speed2), STEPS * STEP)
         for j in range(MODES)
     ]
-    matrix = [[columns[j][i] for j in range(MODES)] for i in range(MODES)]
-
-    def term(i):
-        source = (i - 1) % group
-        read = [term_ref[pl.ds(source * MODES + k, groups, stride=group * MODES), :] for k in range(MODES)]
-        return [pltpu.roll(x, 1, 0) for x in read] if i == 0 else read
-
-    sums = [term(0)]
-    for i in range(1, group):
-        sums.append([x + y for x, y in zip(times(matrix, sums[-1]), term(i))])
-    power, size = matrix, 1
-    while size < group:
-        power, size = square(power), 2 * size
-    total, reach = sums[-1], 1
-    while reach < groups:
-        earlier = [jnp.where(row >= reach, pltpu.roll(x, reach, 0), 0.0) for x in total]
-        total = [x + y for x, y in zip(total, times(power, earlier))]
-        reach *= 2
-        if reach < groups:
-            power = square(power)
-    carry = [jnp.where(row >= 1, pltpu.roll(x, 1, 0), 0.0) for x in total]
-    for i in range(group):
-        carry = times(matrix, carry)
+    return [[columns[j][i] for j in range(MODES)] for i in range(MODES)]
+
+
+def term_rows(step, half, k):
+    return pl.ds((step * QUAD * CHUNK + half * ROWS) * MODES + k, ROWS, stride=MODES)
+
+
+def carry_rows(half, k):
+    return pl.ds((k * HALVES + half) * ROWS, ROWS)
+
+
+def quad_kernel(term_ref, speed_ref, carry_ref):
+    quad, chunk = place()
+    matrix = coarse_matrix(speed_ref, chunk)
+    row = lax.broadcasted_iota(jnp.int32, (ROWS, LANES), 0)
+    for half in range(HALVES):
+        terms = [[term_ref[term_rows(step, half, k), :] for k in range(MODES)] for step in range(QUAD)]
+        total = terms[0]
+        for step in range(1, QUAD):
+            total = added(times(matrix, total), terms[step])
+        if half == HALVES - 1:
+            total = chosen(jnp.logical_and(quad == QUAD - 1, row >= CHUNK), terms[-1], total)
         for k in range(MODES):
-            out_ref[pl.ds(i * MODES + k, groups, stride=group * MODES), :] = sums[i][k] + carry[k]
-
-
-def scan_part(terms, speeds):
+            carry_ref[carry_rows(half, k), :] = total[k]
+
+
+def read_carry(ref, half):
+    return [ref[carry_rows(half, k), :] for k in range(MODES)]
+
+
+def joined(over_quad, quad, own, partner, half, row):
+    odd = quad % 2 == 1
+    earlier, later = chosen(odd, partner, own), chosen(odd, own, partner)
+    both = added(times(over_quad, earlier), later)
+    if half < HALVES - 1:
+        return both
+    return chosen(jnp.logical_and(quad >= 2, row >= CHUNK), later, both)
+
+
+def pair_kernel(carry_ref, partner_ref, speed_ref, out_ref):
+    quad, chunk = place()
+    over_quad = square(square(coarse_matrix(speed_ref, chunk)))
+    row = lax.broadcasted_iota(jnp.int32, (ROWS, LANES), 0)
+    for half in range(HALVES):
+        both = joined(over_quad, quad, read_carry(carry_ref, half), read_carry(partner_ref, half), half, row)
+        for k in range(MODES):
+            out_ref[carry_rows(half, k), :] = both[k]
+
+
+def slab_kernel(term_ref, carry_ref, partner_ref, far_ref, speed_ref, out_ref):
+    quad, chunk = place()
+    matrix = coarse_matrix(speed_ref, chunk)
+    over_quad = square(square(matrix))
+    over_pair = square(over_quad)
+    over_y = square(over_pair)
+    row = lax.broadcasted_iota(jnp.int32, (ROWS, LANES), 0)
+    low = row < CHUNK
+    high_pair, odd = quad >= 2, quad % 2 == 1
+
+    def swapped(xs):
+        return [pltpu.roll(x, CHUNK, 0) for x in xs]
+
+    here, total = [], []
+    for half in range(HALVES):
+        own, partner, far = (read_carry(ref, half) for ref in (carry_ref, partner_ref, far_ref))
+        both = joined(over_quad, quad, own, partner, half, row)
+        before_pair = [jnp.where(high_pair, x, 0.0) for x in far]
+        here.append(chosen(odd, added(times(over_quad, before_pair), partner), before_pair))
+        first_pair, second_pair = chosen(high_pair, far, both), chosen(high_pair, both, far)
+        total.append(added(times(over_pair, first_pair), second_pair))
+    first = swapped(second_pair)
+    second = swapped(added(times(over_y, first), total[0]))
+    pair = chosen(low, first, second)
+    third = swapped(added(times(over_y, pair), total[0]))
+    fourth = swapped(added(times(over_y, third), total[1]))
+    starts = [pair, chosen(low, third, fourth)]
+    for half in range(HALVES):
+        state = starts[half]
+        state = chosen(high_pair, times(over_pair, state), state)
+        state = chosen(odd, times(over_quad, state), state)
+        state = added(state, here[half])
+        for step in range(QUAD):
+            for k in range(MODES):
+                out_ref[term_rows(step, half, k), :] = state[k]
+            if step < QUAD - 1:
+                terms = [term_ref[term_rows(step, half, k), :] for k in range(MODES)]
+                state = added(times(matrix, state), terms)
+
+
+def on_device(kernel, name, rows, *operands):
     return pl.pallas_call(
-        functools.partial(scan_kernel, 8),
-        out_shape=jax.ShapeDtypeStruct(terms.shape, jnp.float32),
-        in_specs=[pl.BlockSpec(memory_space=pltpu.VMEM)] * 2,
+        kernel,
+        out_shape=jax.ShapeDtypeStruct((rows, LANES), jnp.float32),
+        in_specs=[pl.BlockSpec(memory_space=pltpu.VMEM)] * len(operands),
         out_specs=pl.BlockSpec(memory_space=pltpu.VMEM),
-        name="slab_scan",
-    )(terms, speeds)
+        compiler_params=pltpu.CompilerParams(vmem_limit_bytes=16 * 1024 * 1024),
+        name=name,
+    )(*operands)
+
+
+def swap_blocks(x, groups):
+    return lax.all_to_all(x.reshape(-1, MODES, LANES), "tm", 0, 0, axis_index_groups=groups, tiled=True).reshape(x.shape)
 
 
 def body(initial, guess, speeds, flags):
@@ -264,9 +353,17 @@
     near = lax.ppermute(near, "space", [p for i in range(0, blocks, 2) for p in ((i, i + 1), (i + 1, i))])
     state = by_row(jnp.where(lax.axis_index("tm") == slabs - 1, initial, ours))
     terms = fine_part(state, speed_rows, flag_rows, near, far, slabs)
-    terms = lax.all_to_all(terms.reshape(rows, MODES, LANES), "tm", 0, 0, tiled=True)
-    sums = scan_part(terms.reshape(rows * MODES, LANES), speed_rows)
-    sums = lax.all_to_all(sums.reshape(rows, MODES, LANES), "tm", 0, 0, tiled=True)
+    quads, ys = range(QUAD), range(slabs // QUAD**2)
+    of_quad = [[y * QUAD**2 + q * QUAD + step for step in range(QUAD) for y in ys] for q in quads]
+    terms = swap_blocks(terms, of_quad)
+    size = MODES * HALVES * ROWS
+    carry = on_device(quad_kernel, "quad_carry", size, terms, speed_rows)
+    partner = lax.ppermute(carry, "tm", [(c, c ^ QUAD) for c in range(slabs)])
+    joint = on_device(pair_kernel, "pair_carry", size, carry, partner, speed_rows)
+    far = lax.ppermute(joint, "tm", [(c, c ^ (3 * QUAD)) for c in range(slabs)])
+    sums = on_device(slab_kernel, "slab_sums", rows * MODES, terms, carry, partner, far, speed_rows)
+    sums = swap_blocks(sums, of_quad)
+    sums = sums.reshape(rows, MODES, LANES)
     return sums.transpose(1, 0, 2).reshape(1, MODES, count)
 
 

time: 71.7 us -> 64.5 us (0.90)
  blocking collectives: 57.3 us -> 30 us
  starting transfers between devices: 5.42 us -> 22.7 us
  waiting for transfers between devices: 0.91 us -> 5.25 us
  Pallas kernels: 6.95 us -> 5.44 us
    all_to_all x2, blocking collectives: 57.3 us -> 30 us  [swap_blocks(): lax.all_to_all(x.reshape(-1, MODES, LANES), 'tm', 0, 0, axis_index_groups...]
    ppermute x0 -> x2, starting transfers between devices: none -> 17.3 us  [the longest x1 9.1 us: body(): partner = lax.ppermute(carry, 'tm', [(c, c ^ QUAD) for c in range(slabs)])]
    ppermute x0 -> x2, waiting for transfers between devices: none -> 4.34 us  [the longest x1 2.46 us: body(): partner = lax.ppermute(carry, 'tm', [(c, c ^ QUAD) for c in range(slabs)])]
    pallas_call x1 -> x3, Pallas kernels: 1.86 us -> 0.34 us  [on_device(): pl.pallas_call(kernel, out_shape=jax.ShapeDtypeStruct((rows, LANES), jnp....]
  transfers between devices with their start and end apart: 2 -> 4, of which waited for: 1 -> 3; matrix products, arithmetic and copies ran while one was open for 0% -> 0% of each run, Pallas kernels for 0% -> 0%
where the time goes in v4:
time: 64.5 us; the launch traced here: 64.2 us
  blocking collectives  30 us (47%)
  starting transfers between devices  22.7 us (35%)
  Pallas kernels  5.44 us (8%)
  waiting for transfers between devices  5.25 us (8%)
  local copies, waits for them, and re-layouts  0.68 us (1%)
    all_to_all x2, blocking collectives, swap_blocks(): lax.all_to_all(x.reshape(-1, MODES, LANES), 'tm', 0, 0, axis_index_groups...  30 us
    ppermute x1, starting transfers between devices, body(): partner = lax.ppermute(carry, 'tm', [(c, c ^ QUAD) for c in range(slabs)])  9.1 us
    ppermute x1, starting transfers between devices, body(): far = lax.ppermute(joint, 'tm', [(c, c ^ 3 * QUAD) for c in range(slabs)])  8.19 us
    pallas_call x1, Pallas kernels, fine_part(): pl.pallas_call(functools.partial(fine_kernel, slabs), out_shape=jax.Shape...  3.62 us
    ppermute x1, starting transfers between devices, body(): lax.ppermute(near, 'space', [p for i in range(0, blocks, 2) for p in ((i,...  3.5 us
    ppermute x1, waiting for transfers between devices, body(): partner = lax.ppermute(carry, 'tm', [(c, c ^ QUAD) for c in range(slabs)])  2.46 us
    ppermute x1, starting transfers between devices, body(): lax.ppermute(far, 'space', [p for i in range(1, blocks - 1, 2) for p in (...  1.92 us
    ppermute x1, waiting for transfers between devices, body(): far = lax.ppermute(joint, 'tm', [(c, c ^ 3 * QUAD) for c in range(slabs)])  1.88 us
  transfers between devices with their start and end apart: 4, of which 3 were waited for; matrix products, arithmetic and copies ran while one was open for 0% of the time, Pallas kernels for 0%

profile of v4, /device:TPU:2, one launch (start us, length us, event | category | flops | bytes accessed | tf_op | source)
XLA Modules:
  0.0 64.2 jit_solution(14560666366315229070)
XLA Ops:
  0.0 0.0 copy-start.2
  0.0 0.0 copy-start.3
  0.0 1.5 %end_strips.1 = (f32[8,128]{1,0:T(8,128)}, f32[8,128]{1,0:T(8,128)}) custom-call(f32[256,128]{1,0:T(8,128)} %bitcast.37, f32[256,128]{1,0:T(8,128)} %bitcast.36, f32[64,128]{1,0:T(8,128)} %bitcast.26, s32[64,128]{1,0:T(8,128)} %bitcast.34), custom_call_target="tpu_custom_call" | custom-call | tf_op jit(solution)/shard_map/end_strips/pallas_call | solution.py:128
  1.5 1.9 %collective-permute-start.1 = (f32[8,128]{1,0:T(8,128)}, f32[8,128]{1,0:T(8,128)S(1)}, u32[]{:S(2)}, u32[]{:S(2)}) collective-permute-start(f32[8,128]{1,0:T(8,128)} %get-tuple-element.10), channel_id=1, source_target_pairs={{1,2},{2,1},{3,4},{4,3},{5,6},{6,5},{9,10},{10,9},{11,12},{12,11},... | collective-permute-start | bytes 12296 | tf_op jit(solution)/shard_map/ppermute | solution.py:352
  3.4 3.5 %collective-permute-start = (f32[8,128]{1,0:T(8,128)}, f32[8,128]{1,0:T(8,128)S(1)}, u32[]{:S(2)}, u32[]{:S(2)}) collective-permute-start(f32[8,128]{1,0:T(8,128)} %get-tuple-element.8), channel_id=1, source_target_pairs={{0,1},{1,0},{2,3},{3,2},{4,5},{5,4},{6,7},{7,6},{8,9},{9,8},{10,11... | collective-permute-start | bytes 12296 | tf_op jit(solution)/shard_map/ppermute | solution.py:353
  6.9 0.0 copy-done.2
  6.9 0.0 copy-done.3
  7.0 0.0 copy-start
  7.0 0.0 copy-start.1
  7.0 0.0 collective-permute-done.1.far_ref
  7.0 0.9 %collective-permute-done.near_ref = f32[8,128]{1,0:T(8,128)S(1)} collective-permute-done((f32[8,128]{1,0:T(8,128)}, f32[8,128]{1,0:T(8,128)S(1)}, u32[]{:S(2)}, u32[]{:S(2)}) %collective-permute-start) | collective-permute-done | bytes 4128 | tf_op jit(solution)/shard_map/ppermute | solution.py:353
  7.9 0.0 copy-done
  7.9 0.0 copy-done.1
  7.9 3.6 %fine_steps.1 = f32[256,128]{1,0:T(8,128)S(1)} custom-call(f32[256,128]{1,0:T(8,128)S(1)} %bitcast.32, f32[64,128]{1,0:T(8,128)S(1)} %bitcast.27, s32[64,128]{1,0:T(8,128)S(1)} %bitcast.35, f32[8,128]{1,0:T(8,128)S(1)} %collective-permute-done.near_ref, f32[8,128]{1,0:T(8,128)S(1)} %collective-permute-done.1.far_ref), custom_call_target="tpu_custom_call" | custom-call | flops 11796480 | bytes 262144 | tf_op jit(solution)/shard_map/fine_steps/pallas_call | solution.py:183
  11.6 17.5 %all_to_all.10 = f32[64,4,128]{2,1,0:T(4,128)S(1)} all-to-all(f32[64,4,128]{2,1,0:T(4,128)S(1)} %bitcast.33), channel_id=1, replica_groups={{0,128,256,384,8,136,264,392,16,144,272,400,24,152,280,408},{32,160,288..., dimensions={0} | all-to-all | bytes 262144 | tf_op jit(solution)/shard_map/all_to_all | solution.py:338
  29.1 0.1 quad_carry.1.carry_ref
  29.2 9.1 %collective-permute-start.2 = (f32[64,128]{1,0:T(8,128)S(1)}, f32[64,128]{1,0:T(8,128)S(1)}, u32[]{:S(2)}, u32[]{:S(2)}) collective-permute-start(f32[64,128]{1,0:T(8,128)S(1)} %quad_carry.1.carry_ref), channel_id=1, source_target_pairs={{0,32},{8,40},{16,48},{24,56},{32,0},{40,8},{48,16},{56,24},{64,96... | collective-permute-start | bytes 98312 | tf_op jit(solution)/shard_map/ppermute | solution.py:361
  38.3 2.5 %collective-permute-done.2.partner_ref = f32[64,128]{1,0:T(8,128)S(1)} collective-permute-done((f32[64,128]{1,0:T(8,128)S(1)}, f32[64,128]{1,0:T(8,128)S(1)}, u32[]{:S(2)}, u32[]{:S(2)}) %collective-permute-start.2) | collective-permute-done | bytes 32800 | tf_op jit(solution)/shard_map/ppermute | solution.py:361
  40.7 0.1 pair_carry.1
  40.8 8.2 %collective-permute-start.3 = (f32[64,128]{1,0:T(8,128)S(1)}, f32[64,128]{1,0:T(8,128)S(1)}, u32[]{:S(2)}, u32[]{:S(2)}) collective-permute-start(f32[64,128]{1,0:T(8,128)S(1)} %pair_carry.1), channel_id=1, source_target_pairs={{0,96},{8,104},{16,112},{24,120},{32,64},{40,72},{48,80},{56,88},{... | collective-permute-start | bytes 98312 | tf_op jit(solution)/shard_map/ppermute | solution.py:363
  49.0 1.9 %collective-permute-done.3.far_ref = f32[64,128]{1,0:T(8,128)S(1)} collective-permute-done((f32[64,128]{1,0:T(8,128)S(1)}, f32[64,128]{1,0:T(8,128)S(1)}, u32[]{:S(2)}, u32[]{:S(2)}) %collective-permute-start.3) | collective-permute-done | bytes 32800 | tf_op jit(solution)/shard_map/ppermute | solution.py:363
  50.9 0.2 slab_sums.1
  51.1 12.4 %all_to_all.11 = f32[64,4,128]{2,1,0:T(4,128)S(1)} all-to-all(f32[64,4,128]{2,1,0:T(4,128)S(1)} %bitcast.31), channel_id=1, replica_groups={{0,128,256,384,8,136,264,392,16,144,272,400,24,152,280,408},{32,160,288..., dimensions={0} | all-to-all | bytes 262144 | tf_op jit(solution)/shard_map/all_to_all | solution.py:338
  63.5 0.7 %copy.10 = f32[1,4,8192]{2,1,0:T(4,128)} copy(f32[1,4,8192]{2,1,0:T(4,128)S(1)} %bitcast.39) | data formatting | bytes 262144
  (1 shorter events, 0.0 us)
Async XLA Ops:
  0.0 6.9 %copy-start.2 = (f32[4,8192]{1,0:T(4,128)S(1)}, f32[4,8192]{1,0:T(4,128)}, u32[]{:S(2)}) copy-start(f32[4,8192]{1,0:T(4,128)} %param.4) | copy-start | bytes 393220
  0.0 6.9 %copy-start.3 = (f32[1,4,8192]{2,1,0:T(4,128)S(1)}, f32[1,4,8192]{2,1,0:T(4,128)}, u32[]{:S(2)}) copy-start(f32[1,4,8192]{2,1,0:T(4,128)} %param.5) | copy-start | bytes 393220
  1.5 5.5 %collective-permute-start.1 = (f32[8,128]{1,0:T(8,128)}, f32[8,128]{1,0:T(8,128)S(1)}, u32[]{:S(2)}, u32[]{:S(2)}) collective-permute-start(f32[8,128]{1,0:T(8,128)} %get-tuple-element.10), channel_id=1, source_target_pairs={{1,2},{2,1},{3,4},{4,3},{5,6},{6,5},{9,10},{10,9},{11,12},{12,11},... | collective-permute-start | bytes 12296 | tf_op jit(solution)/shard_map/ppermute | solution.py:352
  3.4 4.5 %collective-permute-start = (f32[8,128]{1,0:T(8,128)}, f32[8,128]{1,0:T(8,128)S(1)}, u32[]{:S(2)}, u32[]{:S(2)}) collective-permute-start(f32[8,128]{1,0:T(8,128)} %get-tuple-element.8), channel_id=1, source_target_pairs={{0,1},{1,0},{2,3},{3,2},{4,5},{5,4},{6,7},{7,6},{8,9},{9,8},{10,11... | collective-permute-start | bytes 12296 | tf_op jit(solution)/shard_map/ppermute | solution.py:353
  7.0 1.0 %copy-start = (f32[8192]{0:T(1024)S(1)}, f32[8192]{0:T(1024)}, u32[]{:S(2)}) copy-start(f32[8192]{0:T(1024)} %param.6) | copy-start | bytes 98308
  7.0 1.0 %copy-start.1 = (s32[8192]{0:T(1024)S(1)}, s32[8192]{0:T(1024)}, u32[]{:S(2)}) copy-start(s32[8192]{0:T(1024)} %param.7) | copy-start | bytes 98308
  29.2 11.6 %collective-permute-start.2 = (f32[64,128]{1,0:T(8,128)S(1)}, f32[64,128]{1,0:T(8,128)S(1)}, u32[]{:S(2)}, u32[]{:S(2)}) collective-permute-start(f32[64,128]{1,0:T(8,128)S(1)} %quad_carry.1.carry_ref), channel_id=1, source_target_pairs={{0,32},{8,40},{16,48},{24,56},{32,0},{40,8},{48,16},{56,24},{64,96... | collective-permute-start | bytes 98312 | tf_op jit(solution)/shard_map/ppermute | solution.py:361
  40.8 10.1 %collective-permute-start.3 = (f32[64,128]{1,0:T(8,128)S(1)}, f32[64,128]{1,0:T(8,128)S(1)}, u32[]{:S(2)}, u32[]{:S(2)}) collective-permute-start(f32[64,128]{1,0:T(8,128)S(1)} %pair_carry.1), channel_id=1, source_target_pairs={{0,96},{8,104},{16,112},{24,120},{32,64},{40,72},{48,80},{56,88},{... | collective-permute-start | bytes 98312 | tf_op jit(solution)/shard_map/ppermute | solution.py:363

commit v5 on v4

--- a/solution.py
+++ b/solution.py
@@ -22,17 +22,17 @@
     return [JACOBIAN * m * delta for m in INV_MASS]
 
 
-def before(x):
-    rolled = pltpu.roll(x, 1, 1)
-    lane = lax.broadcasted_iota(jnp.int32, x.shape, 1)
-    return jnp.where(lane == 0, pltpu.roll(rolled, 1, 0), rolled)
-
-
-def after(x):
-    rows, lanes = x.shape
-    rolled = pltpu.roll(x, lanes - 1, 1)
-    lane = lax.broadcasted_iota(jnp.int32, x.shape, 1)
-    return jnp.where(lane == lanes - 1, pltpu.roll(rolled, rows - 1, 0), rolled)
+def shifted(xs, step):
+    n = len(xs)
+    rolled = [pltpu.roll(x, step % LANES, 1) for x in xs]
+    lane = lax.broadcasted_iota(jnp.int32, xs[0].shape, 1)
+    edge = lane == (0 if step == 1 else LANES - 1)
+    out = []
+    for v in range(n):
+        at = v - step
+        row = rolled[at] if 0 <= at < n else pltpu.roll(rolled[at % n], step % ROWS, 0)
+        out.append(jnp.where(edge, row, rolled[v]))
+    return out
 
 
 def volume_terms(u, speed2, drain, p, q):
@@ -52,26 +52,30 @@
     return out, out + m1, out + m2, out + m3
 
 
-def full_rhs(u, speed, speed2, inflow, gate, gate_after):
+def traces(u):
     a, b, c, d = u
     p, q = a + c, b + d
-    tr, tl = p + q, p - q
     odd, even = b + 6.0 * d, 3.0 * c
-    sr, sl = odd + even, odd - even
-    tr_b, sr_b = before(tr), before(sr)
-    tl_a, sl_a = after(tl), after(sl)
-    jump = tr_b - tl
-    k_l = gate * jump
-    h_l = gate * (sr_b + sl - (2.0 * PENALTY) * jump)
-    g_l = inflow * tr_b - h_l
-    jump_a = tr - tl_a
-    k_r = gate_after * jump_a
-    h_r = gate_after * (sr + sl_a - (2.0 * PENALTY) * jump_a)
-    base = h_r - speed * tr
-    plus, minus = base + g_l, base - g_l
-    k_sum, k_dif = k_r + k_l, k_r - k_l
-    m1, m2, m3 = volume_terms(u, speed2, base, p, q)
-    return plus, minus + k_sum + m1, plus + 3.0 * k_dif + m2, minus + 6.0 * k_sum + m3
+    return p + q, p - q, odd + even, odd - even
+
+
+def full_step(start, now, scale, speed, speed2, inflow, gate, gate_after):
+    tr, tl, sr, sl = zip(*(traces(u) for u in now))
+    tr_b, sr_b, tl_a, sl_a = shifted(tr, 1), shifted(sr, 1), shifted(tl, -1), shifted(sl, -1)
+    result = []
+    for v, u in enumerate(now):
+        jump = tr_b[v] - tl[v]
+        k_l = gate[v] * jump
+        g_l = inflow[v] * tr_b[v] - gate[v] * (sr_b[v] + sl[v] - (2.0 * PENALTY) * jump)
+        jump = tr[v] - tl_a[v]
+        k_r = gate_after[v] * jump
+        base = gate_after[v] * (sr[v] + sl_a[v] - (2.0 * PENALTY) * jump) - speed[v] * tr[v]
+        plus, minus = base + g_l, base - g_l
+        k_sum, k_dif = k_r + k_l, k_r - k_l
+        m1, m2, m3 = volume_terms(u, speed2[v], None, u[0] + u[2], u[1] + u[3])
+        rhs = plus, minus + k_sum + m1, plus + 3.0 * k_dif + m2, minus + 6.0 * k_sum + m3
+        result.append([x + f * r for x, f, r in zip(start[v], scale, rhs)])
+    return result
 
 
 def three_sections(u, rhs, delta):
@@ -136,47 +140,56 @@
             pltpu.VMEM((2, ROWS, LANES), jnp.int32),
             pltpu.SemaphoreType.DMA((6,)),
         ],
-        compiler_params=pltpu.CompilerParams(vmem_limit_bytes=60 * 1024 * 1024),
+        compiler_params=pltpu.CompilerParams(vmem_limit_bytes=16 * 1024 * 1024),
         name="end_strips",
-    )(guess, initial, speeds, flags)
-
-
-def fine_kernel(slabs, state_ref, speed_ref, flag_ref, near_ref, far_ref, out_ref):
+    )(*(pltpu.with_memory_space_constraint(x, pltpu.HBM) for x in (guess, initial, speeds, flags)))
+
+
+def fine_kernel(slabs, state_ref, speed_ref, flag_ref, near_ref, far_ref, out_ref, field, coef):
     rows = speed_ref.shape[0]
-    wide = rows + 8
+    wide = rows + ROWS
+    n = wide // ROWS
     last = lax.axis_index("tm") == slabs - 1
     block = lax.axis_index("space")
     even = block % 2 == 0
     near, far = near_ref[...], far_ref[...]
     left, right = jnp.where(even, far, near), jnp.where(even, near, far)
 
-    def ring(main, k):
-        unused = jnp.zeros((6, LANES), jnp.float32)
-        return jnp.concatenate([main, right[k : k + 1], unused, left[k : k + 1]], 0)
-
-    own = [state_ref[pl.ds(k, rows, stride=MODES), :] for k in range(MODES)]
-    start = [ring(x, k) for k, x in enumerate(own)]
-    speed_own = speed_ref[...]
-    speed = ring(speed_own, MODES)
-    opened = ring(1.0 - flag_ref[...].astype(jnp.float32), MODES + 1)
-    row = lax.broadcasted_iota(jnp.int32, (wide, LANES), 0)
-    lane = lax.broadcasted_iota(jnp.int32, (wide, LANES), 1)
+    unused = ROWS - 2
+    field[pl.ds(0, rows * MODES), :] = state_ref[...]
+    field[pl.ds(rows * MODES, MODES), :] = right[:MODES]
+    field[pl.ds((rows + 1) * MODES, unused * MODES), :] = jnp.zeros((unused * MODES, LANES), jnp.float32)
+    field[pl.ds((wide - 1) * MODES, MODES), :] = left[:MODES]
+    for part, own in ((0, speed_ref[...]), (1, 1.0 - flag_ref[...].astype(jnp.float32))):
+        coef[pl.ds(part * wide, rows), :] = own
+        coef[pl.ds(part * wide + rows, 1), :] = right[MODES + part : MODES + part + 1]
+        coef[pl.ds(part * wide + rows + 1, unused), :] = jnp.zeros((unused, LANES), jnp.float32)
+        coef[pl.ds(part * wide + wide - 1, 1), :] = left[MODES + part : MODES + part + 1]
+
+    start = [[field[pl.ds(MODES * v + k, ROWS, stride=MODES * n), :] for k in range(MODES)] for v in range(n)]
+    speed = [coef[pl.ds(v, ROWS, stride=n), :] for v in range(n)]
+    opened = [coef[pl.ds(wide + v, ROWS, stride=n), :] for v in range(n)]
+    row = lax.broadcasted_iota(jnp.int32, (ROWS, LANES), 0)
+    lane = lax.broadcasted_iota(jnp.int32, (ROWS, LANES), 1)
     first = jnp.logical_and(jnp.logical_and(row == 0, lane == 0), block == 0)
-    opened = jnp.where(first, 0.0, opened)
-    gate = (0.5 * VISCOSITY) * opened
-    gate_after = after(gate)
-    inflow = opened * before(speed)
-    speed2 = 2.0 * speed
-
-    def rhs(u):
-        return full_rhs(u, speed, speed2, inflow, gate, gate_after)
-
-    final = lax.fori_loop(0, STEPS, lambda i, u: tuple(three_sections(u, rhs, STEP)), tuple(start))
-    speed2_own = 2.0 * speed_own
-    coarse = three_sections(own, lambda u: local_rhs(u, speed_own, speed2_own), STEPS * STEP)
-    for k in range(MODES):
-        share = jnp.where(last, 0.0, coarse[k])
-        out_ref[pl.ds(k, rows, stride=MODES), :] = final[k][:rows] - share
+    opened[0] = jnp.where(first, 0.0, opened[0])
+    gate = [(0.5 * VISCOSITY) * x for x in opened]
+    gate_after = shifted(gate, -1)
+    inflow = [x * y for x, y in zip(opened, shifted(speed, 1))]
+    speed2 = [2.0 * x for x in speed]
+
+    def advance(_, u):
+        now = u
+        for share in (3.0, 2.0, 1.0):
+            now = full_step(u, now, column_scales(STEP / share), speed, speed2, inflow, gate, gate_after)
+        return now
+
+    final = lax.fori_loop(0, STEPS, advance, start, unroll=True)
+    for v in range(n):
+        coarse = three_sections(start[v], lambda u: local_rhs(u, speed[v], speed2[v]), STEPS * STEP)
+        for k in range(MODES):
+            field[pl.ds(MODES * v + k, ROWS, stride=MODES * n), :] = final[v][k] - jnp.where(last, 0.0, coarse[k])
+    out_ref[...] = field[pl.ds(0, rows * MODES), :]
 
 
 def fine_part(state, speeds, flags, near, far, slabs):
@@ -185,6 +198,10 @@
         out_shape=jax.ShapeDtypeStruct(state.shape, jnp.float32),
         in_specs=[pl.BlockSpec(memory_space=pltpu.VMEM)] * 5,
         out_specs=pl.BlockSpec(memory_space=pltpu.VMEM),
+        scratch_shapes=[
+            pltpu.VMEM(((speeds.shape[0] + ROWS) * MODES, LANES), jnp.float32),
+            pltpu.VMEM(((speeds.shape[0] + ROWS) * 2, LANES), jnp.float32),
+        ],
         compiler_params=pltpu.CompilerParams(vmem_limit_bytes=16 * 1024 * 1024),
         cost_estimate=pl.CostEstimate(flops=24 * 60 * 8192, bytes_accessed=2 * state.size * 4, transcendentals=0),
         name="fine_steps",

time: 64.5 us -> 63.2 us (0.980)
  Pallas kernels: 5.44 us -> 4.37 us
where the time goes in v5:
time: 63.2 us; the launch traced here: 62.9 us
  blocking collectives  30 us (47%)
  starting transfers between devices  22.7 us (36%)
  waiting for transfers between devices  5.04 us (8%)
  Pallas kernels  4.37 us (7%)
  local copies, waits for them, and re-layouts  0.68 us (1%)
    all_to_all x2, blocking collectives, swap_blocks(): lax.all_to_all(x.reshape(-1, MODES, LANES), 'tm', 0, 0, axis_index_groups...  30 us
    ppermute x1, starting transfers between devices, body(): partner = lax.ppermute(carry, 'tm', [(c, c ^ QUAD) for c in range(slabs)])  9.1 us
    ppermute x1, starting transfers between devices, body(): far = lax.ppermute(joint, 'tm', [(c, c ^ 3 * QUAD) for c in range(slabs)])  8.19 us
    ppermute x1, starting transfers between devices, body(): lax.ppermute(near, 'space', [p for i in range(0, blocks, 2) for p in ((i,...  3.5 us
    pallas_call x1, Pallas kernels, fine_part(): pl.pallas_call(functools.partial(fine_kernel, slabs), out_shape=jax.Shape...  3.16 us
    ppermute x1, waiting for transfers between devices, body(): partner = lax.ppermute(carry, 'tm', [(c, c ^ QUAD) for c in range(slabs)])  2.46 us
    ppermute x1, starting transfers between devices, body(): lax.ppermute(far, 'space', [p for i in range(1, blocks - 1, 2) for p in (...  1.92 us
    ppermute x1, waiting for transfers between devices, body(): far = lax.ppermute(joint, 'tm', [(c, c ^ 3 * QUAD) for c in range(slabs)])  1.88 us
  transfers between devices with their start and end apart: 4, of which 3 were waited for; matrix products, arithmetic and copies ran while one was open for 0% of the time, Pallas kernels for 0%

profile of v5, /device:TPU:2, one launch (start us, length us, event | category | flops | bytes accessed | tf_op | source)
XLA Modules:
  0.0 62.9 jit_solution(8239934407148121618)
XLA Ops:
  0.0 0.0 copy-start.2
  0.0 0.0 copy-start.3
  0.0 0.9 %end_strips.1 = (f32[8,128]{1,0:T(8,128)S(1)}, f32[8,128]{1,0:T(8,128)S(1)}) custom-call(f32[256,128]{1,0:T(8,128)} %bitcast.37, f32[256,128]{1,0:T(8,128)} %bitcast.36, f32[64,128]{1,0:T(8,128)} %bitcast.26, s32[64,128]{1,0:T(8,128)} %bitcast.34), custom_call_target="tpu_custom_call" | custom-call | tf_op jit(solution)/shard_map/end_strips/pallas_call | solution.py:132
  0.9 1.9 %collective-permute-start.1 = (f32[8,128]{1,0:T(8,128)S(1)}, f32[8,128]{1,0:T(8,128)S(1)}, u32[]{:S(2)}, u32[]{:S(2)}) collective-permute-start(f32[8,128]{1,0:T(8,128)S(1)} %get-tuple-element.10), channel_id=1, source_target_pairs={{1,2},{2,1},{3,4},{4,3},{5,6},{6,5},{9,10},{10,9},{11,12},{12,11},... | collective-permute-start | bytes 12296 | tf_op jit(solution)/shard_map/ppermute | solution.py:369
  2.8 3.5 %collective-permute-start = (f32[8,128]{1,0:T(8,128)S(1)}, f32[8,128]{1,0:T(8,128)S(1)}, u32[]{:S(2)}, u32[]{:S(2)}) collective-permute-start(f32[8,128]{1,0:T(8,128)S(1)} %get-tuple-element.8), channel_id=1, source_target_pairs={{0,1},{1,0},{2,3},{3,2},{4,5},{5,4},{6,7},{7,6},{8,9},{9,8},{10,11... | collective-permute-start | bytes 12296 | tf_op jit(solution)/shard_map/ppermute | solution.py:370
  6.3 0.0 copy-done.2
  6.3 0.0 copy-done.3
  6.3 0.0 copy-start
  6.4 0.0 copy-start.1
  6.4 0.0 collective-permute-done.1.far_ref
  6.4 0.7 %collective-permute-done.near_ref = f32[8,128]{1,0:T(8,128)S(1)} collective-permute-done((f32[8,128]{1,0:T(8,128)S(1)}, f32[8,128]{1,0:T(8,128)S(1)}, u32[]{:S(2)}, u32[]{:S(2)}) %collective-permute-start) | collective-permute-done | bytes 4128 | tf_op jit(solution)/shard_map/ppermute | solution.py:370
  7.1 0.0 copy-done
  7.1 0.0 copy-done.1
  7.1 3.2 %fine_steps.1 = f32[256,128]{1,0:T(8,128)S(1)} custom-call(f32[256,128]{1,0:T(8,128)S(1)} %bitcast.32, f32[64,128]{1,0:T(8,128)S(1)} %bitcast.27, s32[64,128]{1,0:T(8,128)S(1)} %bitcast.35, f32[8,128]{1,0:T(8,128)S(1)} %collective-permute-done.near_ref, f32[8,128]{1,0:T(8,128)S(1)} %collective-permute-done.1.far_ref), custom_call_target="tpu_custom_call" | custom-call | flops 11796480 | bytes 262144 | tf_op jit(solution)/shard_map/fine_steps/pallas_call | solution.py:196
  10.3 17.5 %all_to_all.10 = f32[64,4,128]{2,1,0:T(4,128)S(1)} all-to-all(f32[64,4,128]{2,1,0:T(4,128)S(1)} %bitcast.33), channel_id=1, replica_groups={{0,128,256,384,8,136,264,392,16,144,272,400,24,152,280,408},{32,160,288..., dimensions={0} | all-to-all | bytes 262144 | tf_op jit(solution)/shard_map/all_to_all | solution.py:355
  27.8 0.1 quad_carry.1.carry_ref
  27.9 9.1 %collective-permute-start.2 = (f32[64,128]{1,0:T(8,128)S(1)}, f32[64,128]{1,0:T(8,128)S(1)}, u32[]{:S(2)}, u32[]{:S(2)}) collective-permute-start(f32[64,128]{1,0:T(8,128)S(1)} %quad_carry.1.carry_ref), channel_id=1, source_target_pairs={{0,32},{8,40},{16,48},{24,56},{32,0},{40,8},{48,16},{56,24},{64,96... | collective-permute-start | bytes 98312 | tf_op jit(solution)/shard_map/ppermute | solution.py:378
  37.0 2.5 %collective-permute-done.2.partner_ref = f32[64,128]{1,0:T(8,128)S(1)} collective-permute-done((f32[64,128]{1,0:T(8,128)S(1)}, f32[64,128]{1,0:T(8,128)S(1)}, u32[]{:S(2)}, u32[]{:S(2)}) %collective-permute-start.2) | collective-permute-done | bytes 32800 | tf_op jit(solution)/shard_map/ppermute | solution.py:378
  39.4 0.1 pair_carry.1
  39.5 8.2 %collective-permute-start.3 = (f32[64,128]{1,0:T(8,128)S(1)}, f32[64,128]{1,0:T(8,128)S(1)}, u32[]{:S(2)}, u32[]{:S(2)}) collective-permute-start(f32[64,128]{1,0:T(8,128)S(1)} %pair_carry.1), channel_id=1, source_target_pairs={{0,96},{8,104},{16,112},{24,120},{32,64},{40,72},{48,80},{56,88},{... | collective-permute-start | bytes 98312 | tf_op jit(solution)/shard_map/ppermute | solution.py:380
  47.7 1.9 %collective-permute-done.3.far_ref = f32[64,128]{1,0:T(8,128)S(1)} collective-permute-done((f32[64,128]{1,0:T(8,128)S(1)}, f32[64,128]{1,0:T(8,128)S(1)}, u32[]{:S(2)}, u32[]{:S(2)}) %collective-permute-start.3) | collective-permute-done | bytes 32800 | tf_op jit(solution)/shard_map/ppermute | solution.py:380
  49.6 0.2 slab_sums.1
  49.8 12.4 %all_to_all.11 = f32[64,4,128]{2,1,0:T(4,128)S(1)} all-to-all(f32[64,4,128]{2,1,0:T(4,128)S(1)} %bitcast.31), channel_id=1, replica_groups={{0,128,256,384,8,136,264,392,16,144,272,400,24,152,280,408},{32,160,288..., dimensions={0} | all-to-all | bytes 262144 | tf_op jit(solution)/shard_map/all_to_all | solution.py:355
  62.2 0.7 %copy.10 = f32[1,4,8192]{2,1,0:T(4,128)} copy(f32[1,4,8192]{2,1,0:T(4,128)S(1)} %bitcast.39) | data formatting | bytes 262144
  (1 shorter events, 0.0 us)
Async XLA Ops:
  0.0 6.3 %copy-start.2 = (f32[4,8192]{1,0:T(4,128)S(1)}, f32[4,8192]{1,0:T(4,128)}, u32[]{:S(2)}) copy-start(f32[4,8192]{1,0:T(4,128)} %param.4) | copy-start | bytes 393220
  0.0 6.3 %copy-start.3 = (f32[1,4,8192]{2,1,0:T(4,128)S(1)}, f32[1,4,8192]{2,1,0:T(4,128)}, u32[]{:S(2)}) copy-start(f32[1,4,8192]{2,1,0:T(4,128)} %param.5) | copy-start | bytes 393220
  0.9 5.5 %collective-permute-start.1 = (f32[8,128]{1,0:T(8,128)S(1)}, f32[8,128]{1,0:T(8,128)S(1)}, u32[]{:S(2)}, u32[]{:S(2)}) collective-permute-start(f32[8,128]{1,0:T(8,128)S(1)} %get-tuple-element.10), channel_id=1, source_target_pairs={{1,2},{2,1},{3,4},{4,3},{5,6},{6,5},{9,10},{10,9},{11,12},{12,11},... | collective-permute-start | bytes 12296 | tf_op jit(solution)/shard_map/ppermute | solution.py:369
  2.8 4.3 %collective-permute-start = (f32[8,128]{1,0:T(8,128)S(1)}, f32[8,128]{1,0:T(8,128)S(1)}, u32[]{:S(2)}, u32[]{:S(2)}) collective-permute-start(f32[8,128]{1,0:T(8,128)S(1)} %get-tuple-element.8), channel_id=1, source_target_pairs={{0,1},{1,0},{2,3},{3,2},{4,5},{5,4},{6,7},{7,6},{8,9},{9,8},{10,11... | collective-permute-start | bytes 12296 | tf_op jit(solution)/shard_map/ppermute | solution.py:370
  6.3 0.8 %copy-start = (f32[8192]{0:T(1024)S(1)}, f32[8192]{0:T(1024)}, u32[]{:S(2)}) copy-start(f32[8192]{0:T(1024)} %param.6) | copy-start | bytes 98308
  6.4 0.8 %copy-start.1 = (s32[8192]{0:T(1024)S(1)}, s32[8192]{0:T(1024)}, u32[]{:S(2)}) copy-start(s32[8192]{0:T(1024)} %param.7) | copy-start | bytes 98308
  27.9 11.6 %collective-permute-start.2 = (f32[64,128]{1,0:T(8,128)S(1)}, f32[64,128]{1,0:T(8,128)S(1)}, u32[]{:S(2)}, u32[]{:S(2)}) collective-permute-start(f32[64,128]{1,0:T(8,128)S(1)} %quad_carry.1.carry_ref), channel_id=1, source_target_pairs={{0,32},{8,40},{16,48},{24,56},{32,0},{40,8},{48,16},{56,24},{64,96... | collective-permute-start | bytes 98312 | tf_op jit(solution)/shard_map/ppermute | solution.py:378
  39.5 10.1 %collective-permute-start.3 = (f32[64,128]{1,0:T(8,128)S(1)}, f32[64,128]{1,0:T(8,128)S(1)}, u32[]{:S(2)}, u32[]{:S(2)}) collective-permute-start(f32[64,128]{1,0:T(8,128)S(1)} %pair_carry.1), channel_id=1, source_target_pairs={{0,96},{8,104},{16,112},{24,120},{32,64},{40,72},{48,80},{56,88},{... | collective-permute-start | bytes 98312 | tf_op jit(solution)/shard_map/ppermute | solution.py:380

commit v6 on v5

--- a/solution.py
+++ b/solution.py
@@ -23,19 +23,13 @@
 
 
 def shifted(xs, step):
-    n = len(xs)
     rolled = [pltpu.roll(x, step % LANES, 1) for x in xs]
     lane = lax.broadcasted_iota(jnp.int32, xs[0].shape, 1)
     edge = lane == (0 if step == 1 else LANES - 1)
-    out = []
-    for v in range(n):
-        at = v - step
-        row = rolled[at] if 0 <= at < n else pltpu.roll(rolled[at % n], step % ROWS, 0)
-        out.append(jnp.where(edge, row, rolled[v]))
-    return out
-
-
-def volume_terms(u, speed2, drain, p, q):
+    return [jnp.where(edge, rolled[(v - step) % len(xs)], x) for v, x in enumerate(rolled)]
+
+
+def volume_terms(u, speed2, p, q):
     a, b, c, d = u
     vq = (2.0 * VISCOSITY) * q
     m1 = speed2 * a - vq
@@ -48,7 +42,7 @@
     a, b, c, d = u
     p, q = a + c, b + d
     out = -(speed * (p + q))
-    m1, m2, m3 = volume_terms(u, speed2, out, p, q)
+    m1, m2, m3 = volume_terms(u, speed2, p, q)
     return out, out + m1, out + m2, out + m3
 
 
@@ -72,7 +66,7 @@
         base = gate_after[v] * (sr[v] + sl_a[v] - (2.0 * PENALTY) * jump) - speed[v] * tr[v]
         plus, minus = base + g_l, base - g_l
         k_sum, k_dif = k_r + k_l, k_r - k_l
-        m1, m2, m3 = volume_terms(u, speed2[v], None, u[0] + u[2], u[1] + u[3])
+        m1, m2, m3 = volume_terms(u, speed2[v], u[0] + u[2], u[1] + u[3])
         rhs = plus, minus + k_sum + m1, plus + 3.0 * k_dif + m2, minus + 6.0 * k_sum + m3
         result.append([x + f * r for x, f, r in zip(start[v], scale, rhs)])
     return result
@@ -86,126 +80,187 @@
     return v
 
 
-def strip_kernel(slabs, guess_ref, initial_ref, speed_ref, flag_ref, near_ref, far_ref, states, speeds, flags, sems):
+QUAD = 4
+CHUNK = 4
+HALVES = 2
+CHUNKS = 16
+WINDOW = (CHUNK + 1) * MODES
+ORDER = (4, 1, 2, 3, 0, 5, 6, 7, 15, 9, 10, 11, 12, 13, 14, 8)
+BACKWARDS = tuple(CHUNKS - 1 - chunk for chunk in ORDER)
+
+
+def even_block():
+    return lax.axis_index("space") % 2 == 0
+
+
+def place():
+    slab = lax.axis_index("tm")
+    y, z = slab // (QUAD * QUAD), slab % (QUAD * QUAD)
+    position = (z % QUAD) * QUAD + y
+    chunk = position
+    for i, there in enumerate(ORDER):
+        if i != there:
+            chunk = jnp.where(position == i, there, chunk)
+    return z // QUAD, jnp.where(even_block(), chunk, CHUNKS - 1 - chunk)
+
+
+def window_kernel(slabs, guess_ref, initial_ref, out_ref, state, sem):
+    last = lax.axis_index("tm") == slabs - 1
+
+    @pl.when(last)
+    def _():
+        pltpu.make_async_copy(initial_ref, state, sem).start()
+
+    @pl.when(jnp.logical_not(last))
+    def _():
+        pltpu.make_async_copy(guess_ref, state, sem).start()
+
+    pltpu.make_async_copy(guess_ref, state, sem).wait()
+    low = lax.broadcasted_iota(jnp.int32, (MODES, LANES), 1) < LANES // 2
+    size = CHUNK * MODES
+
+    def write(chunks):
+        for position, chunk in enumerate(chunks):
+            at, source = position * WINDOW, chunk * size
+            out_ref[pl.ds(at, size), :] = state[pl.ds(source, size), :]
+            after = state[pl.ds(min(source + size, (CHUNKS - 1) * size), MODES), :]
+            before = state[pl.ds(max(source - MODES, 0), MODES), :]
+            out_ref[pl.ds(at + size, MODES), :] = jnp.where(low, after, before)
+
+    @pl.when(even_block())
+    def _():
+        write(ORDER)
+
+    @pl.when(jnp.logical_not(even_block()))
+    def _():
+        write(BACKWARDS)
+
+
+def window_part(guess, initial, slabs):
+    return pl.pallas_call(
+        functools.partial(window_kernel, slabs),
+        out_shape=jax.ShapeDtypeStruct((CHUNKS * WINDOW, LANES), jnp.float32),
+        in_specs=[pl.BlockSpec(memory_space=pltpu.HBM)] * 2,
+        out_specs=pl.BlockSpec(memory_space=pltpu.VMEM),
+        scratch_shapes=[pltpu.VMEM(guess.shape, jnp.float32), pltpu.SemaphoreType.DMA],
+        compiler_params=pltpu.CompilerParams(vmem_limit_bytes=16 * 1024 * 1024),
+        name="windows",
+    )(*(pltpu.with_memory_space_constraint(x, pltpu.HBM) for x in (guess, initial)))
+
+
+def window_rows(half, r, k):
+    return pl.ds((half * ROWS * (CHUNK + 1) + r) * MODES + k, ROWS, stride=WINDOW)
+
+
+def message_rows(half, k):
+    return pl.ds((k * HALVES + half) * ROWS, ROWS)
+
+
+COEFS = MODES * HALVES * ROWS
+
+
+def edge_kernel(window_ref, speed_ref, flag_ref, out_ref):
+    _, chunk = place()
+    tail = chunk == CHUNKS - 1
     rows = speed_ref.shape[0]
-    last = lax.axis_index("tm") == slabs - 1
-    ends = (0, 1)
-
-    def tile(ref, end):
-        return ref.at[pl.ds(end * (ref.shape[0] - ROWS), ROWS)]
-
-    def copies(source):
-        return [pltpu.make_async_copy(tile(source, e), states.at[e], sems.at[e]) for e in ends]
-
-    others = [pltpu.make_async_copy(tile(speed_ref, e), speeds.at[e], sems.at[2 + e]) for e in ends]
-    others += [pltpu.make_async_copy(tile(flag_ref, e), flags.at[e], sems.at[4 + e]) for e in ends]
-
-    @pl.when(last)
-    def _():
-        for copy in copies(initial_ref):
-            copy.start()
-
-    @pl.when(jnp.logical_not(last))
-    def _():
-        for copy in copies(guess_ref):
-            copy.start()
-
-    for copy in others:
-        copy.start()
-    for copy in others + copies(guess_ref):
-        copy.wait()
-    strips = []
-    for end in ends:
-        row = end * (ROWS - 1)
-        state = states[end, pl.ds(end * (ROWS - MODES), MODES), :]
-        opened = 1.0 - flags[end, pl.ds(row, 1), :].astype(jnp.float32)
-        unused = jnp.zeros((2, LANES), jnp.float32)
-        strips.append(jnp.concatenate([state, speeds[end, pl.ds(row, 1), :], opened, unused], 0))
-    head, tail = strips
-    even = lax.axis_index("space") % 2 == 0
-    near_ref[...] = jnp.where(even, tail, head)
-    far_ref[...] = jnp.where(even, head, tail)
-
-
-def strip_part(guess, initial, speeds, flags, slabs):
-    strip = jax.ShapeDtypeStruct((ROWS, LANES), jnp.float32)
-    return pl.pallas_call(
-        functools.partial(strip_kernel, slabs),
-        out_shape=[strip, strip],
-        in_specs=[pl.BlockSpec(memory_space=pltpu.HBM)] * 4,
-        out_specs=[pl.BlockSpec(memory_space=pltpu.VMEM)] * 2,
-        scratch_shapes=[
-            pltpu.VMEM((2, ROWS, LANES), jnp.float32),
-            pltpu.VMEM((2, ROWS, LANES), jnp.float32),
-            pltpu.VMEM((2, ROWS, LANES), jnp.int32),
-            pltpu.SemaphoreType.DMA((6,)),
-        ],
-        compiler_params=pltpu.CompilerParams(vmem_limit_bytes=16 * 1024 * 1024),
-        name="end_strips",
-    )(*(pltpu.with_memory_space_constraint(x, pltpu.HBM) for x in (guess, initial, speeds, flags)))
-
-
-def fine_kernel(slabs, state_ref, speed_ref, flag_ref, near_ref, far_ref, out_ref, field, coef):
-    rows = speed_ref.shape[0]
-    wide = rows + ROWS
-    n = wide // ROWS
-    last = lax.axis_index("tm") == slabs - 1
-    block = lax.axis_index("space")
-    even = block % 2 == 0
-    near, far = near_ref[...], far_ref[...]
-    left, right = jnp.where(even, far, near), jnp.where(even, near, far)
-
-    unused = ROWS - 2
-    field[pl.ds(0, rows * MODES), :] = state_ref[...]
-    field[pl.ds(rows * MODES, MODES), :] = right[:MODES]
-    field[pl.ds((rows + 1) * MODES, unused * MODES), :] = jnp.zeros((unused * MODES, LANES), jnp.float32)
-    field[pl.ds((wide - 1) * MODES, MODES), :] = left[:MODES]
-    for part, own in ((0, speed_ref[...]), (1, 1.0 - flag_ref[...].astype(jnp.float32))):
-        coef[pl.ds(part * wide, rows), :] = own
-        coef[pl.ds(part * wide + rows, 1), :] = right[MODES + part : MODES + part + 1]
-        coef[pl.ds(part * wide + rows + 1, unused), :] = jnp.zeros((unused, LANES), jnp.float32)
-        coef[pl.ds(part * wide + wide - 1, 1), :] = left[MODES + part : MODES + part + 1]
-
-    start = [[field[pl.ds(MODES * v + k, ROWS, stride=MODES * n), :] for k in range(MODES)] for v in range(n)]
-    speed = [coef[pl.ds(v, ROWS, stride=n), :] for v in range(n)]
-    opened = [coef[pl.ds(wide + v, ROWS, stride=n), :] for v in range(n)]
-    row = lax.broadcasted_iota(jnp.int32, (ROWS, LANES), 0)
-    lane = lax.broadcasted_iota(jnp.int32, (ROWS, LANES), 1)
-    first = jnp.logical_and(jnp.logical_and(row == 0, lane == 0), block == 0)
-    opened[0] = jnp.where(first, 0.0, opened[0])
+    for half in range(HALVES):
+        for k in range(MODES):
+            first, final = window_ref[window_rows(half, 0, k), :], window_ref[window_rows(half, CHUNK - 1, k), :]
+            out_ref[message_rows(half, k), :] = jnp.where(tail, final, first)
+    at = jnp.where(tail, rows - 1, 0)
+    out_ref[pl.ds(COEFS, 1), :] = speed_ref[pl.ds(at, 1), :]
+    out_ref[pl.ds(COEFS + 1, 1), :] = 1.0 - flag_ref[pl.ds(at, 1), :].astype(jnp.float32)
+    out_ref[pl.ds(COEFS + 2, ROWS - 2), :] = jnp.zeros((ROWS - 2, LANES), jnp.float32)
+
+
+def fine_kernel(window_ref, message_ref, speed_ref, flag_ref, out_ref):
+    quad, chunk = place()
+    first, final = chunk == 0, chunk == CHUNKS - 1
+    shape = (ROWS, LANES)
+    row = lax.broadcasted_iota(jnp.int32, shape, 0)
+    lane = lax.broadcasted_iota(jnp.int32, shape, 1)
+    low = lane < LANES // 2
+    outside = jnp.logical_or(jnp.logical_and(low, final), jnp.logical_and(lane >= LANES // 2, first))
+
+    def coef(read, k):
+        def spread(x):
+            return jnp.broadcast_to(x, shape)
+
+        at = chunk * CHUNK
+        own = [spread(read(at + r)) for r in range(CHUNK)]
+        after = spread(read(jnp.minimum(at + CHUNK, CHUNKS * CHUNK - 1)))
+        before = spread(read(jnp.maximum(at - 1, 0)))
+        beyond = spread(message_ref[pl.ds(COEFS + k, 1), :])
+        return [*own, jnp.where(outside, beyond, jnp.where(low, after, before))]
+
+    speed = coef(lambda i: speed_ref[pl.ds(i, 1), :], 0)
+    opened = coef(lambda i: 1.0 - flag_ref[pl.ds(i, 1), :].astype(jnp.float32), 1)
+    wall = jnp.logical_and(jnp.logical_and(first, lax.axis_index("space") == 0), lane == 0)
+    opened[0] = jnp.where(wall, 0.0, opened[0])
     gate = [(0.5 * VISCOSITY) * x for x in opened]
     gate_after = shifted(gate, -1)
     inflow = [x * y for x, y in zip(opened, shifted(speed, 1))]
     speed2 = [2.0 * x for x in speed]
 
-    def advance(_, u):
-        now = u
+    starts = []
+    for half in range(HALVES):
+        start = [[window_ref[window_rows(half, r, k), :] for k in range(MODES)] for r in range(CHUNK + 1)]
+        start[CHUNK] = [
+            jnp.where(outside, message_ref[message_rows(half, k), :], x) for k, x in enumerate(start[CHUNK])
+        ]
+        starts.append(start)
+
+    def advance(_, us):
+        nows = us
         for share in (3.0, 2.0, 1.0):
-            now = full_step(u, now, column_scales(STEP / share), speed, speed2, inflow, gate, gate_after)
-        return now
-
-    final = lax.fori_loop(0, STEPS, advance, start, unroll=True)
-    for v in range(n):
-        coarse = three_sections(start[v], lambda u: local_rhs(u, speed[v], speed2[v]), STEPS * STEP)
-        for k in range(MODES):
-            field[pl.ds(MODES * v + k, ROWS, stride=MODES * n), :] = final[v][k] - jnp.where(last, 0.0, coarse[k])
-    out_ref[...] = field[pl.ds(0, rows * MODES), :]
-
-
-def fine_part(state, speeds, flags, near, far, slabs):
+            scale = column_scales(STEP / share)
+            nows = [full_step(u, now, scale, speed, speed2, inflow, gate, gate_after) for u, now in zip(us, nows)]
+        return nows
+
+    finals = lax.fori_loop(0, STEPS, advance, starts, unroll=True)
+    for half in range(HALVES):
+        for r in range(CHUNK):
+            coarse = three_sections(starts[half][r], lambda u: local_rhs(u, speed[r], speed2[r]), STEPS * STEP)
+            if half == HALVES - 1:
+                last = jnp.logical_and(quad == QUAD - 1, row == ROWS - 1)
+                coarse = [jnp.where(last, 0.0, x) for x in coarse]
+            for k in range(MODES):
+                rows = pl.ds((half * ROWS * CHUNK + r) * MODES + k, ROWS, stride=CHUNK * MODES)
+                out_ref[rows, :] = finals[half][r][k] - coarse[k]
+
+
+def write_kernel(sums_ref, out_ref, sems):
+    size = CHUNK * MODES
+
+    def write(chunks):
+        copies = []
+        for position, chunk in enumerate(chunks):
+            source, target = pl.ds(position * size, size), pl.ds(chunk * size, size)
+            copies.append(pltpu.make_async_copy(sums_ref.at[source], out_ref.at[target], sems.at[position]))
+        for copy in copies:
+            copy.start()
+        for copy in copies:
+            copy.wait()
+
+    @pl.when(even_block())
+    def _():
+        write(ORDER)
+
+    @pl.when(jnp.logical_not(even_block()))
+    def _():
+        write(BACKWARDS)
+
+
+def write_part(sums):
     return pl.pallas_call(
-        functools.partial(fine_kernel, slabs),
-        out_shape=jax.ShapeDtypeStruct(state.shape, jnp.float32),
-        in_specs=[pl.BlockSpec(memory_space=pltpu.VMEM)] * 5,
-        out_specs=pl.BlockSpec(memory_space=pltpu.VMEM),
-        scratch_shapes=[
-            pltpu.VMEM(((speeds.shape[0] + ROWS) * MODES, LANES), jnp.float32),
-            pltpu.VMEM(((speeds.shape[0] + ROWS) * 2, LANES), jnp.float32),
-        ],
+        write_kernel,
+        out_shape=jax.ShapeDtypeStruct(sums.shape, jnp.float32),
+        in_specs=[pl.BlockSpec(memory_space=pltpu.VMEM)],
+        out_specs=pl.BlockSpec(memory_space=pl.ANY),
+        scratch_shapes=[pltpu.SemaphoreType.DMA((CHUNKS,))],
         compiler_params=pltpu.CompilerParams(vmem_limit_bytes=16 * 1024 * 1024),
-        cost_estimate=pl.CostEstimate(flops=24 * 60 * 8192, bytes_accessed=2 * state.size * 4, transcendentals=0),
-        name="fine_steps",
-    )(state, speeds, flags, near, far)
+        name="write_out",
+    )(sums)
 
 
 def times(matrix, field):
@@ -229,17 +284,6 @@
 
 def chosen(test, xs, ys):
     return [jnp.where(test, x, y) for x, y in zip(xs, ys)]
-
-
-QUAD = 4
-CHUNK = 4
-HALVES = 2
-
-
-def place():
-    slab = lax.axis_index("tm")
-    y, z = slab // (QUAD * QUAD), slab % (QUAD * QUAD)
-    return z // QUAD, (z % QUAD) * QUAD + y
 
 
 def coarse_matrix(speed_ref, chunk):
@@ -364,23 +408,25 @@
         return x.reshape(MODES, rows, LANES).transpose(1, 0, 2).reshape(rows * MODES, LANES)
 
     speed_rows, flag_rows = speeds.reshape(rows, LANES), flags.reshape(rows, LANES)
-    near, far = strip_part(by_row(guess[0]), by_row(initial), speed_rows, flag_rows, slabs)
-    ours, _ = lax.optimization_barrier((guess[0], near))
-    far = lax.ppermute(far, "space", [p for i in range(1, blocks - 1, 2) for p in ((i, i + 1), (i + 1, i))])
-    near = lax.ppermute(near, "space", [p for i in range(0, blocks, 2) for p in ((i, i + 1), (i + 1, i))])
-    state = by_row(jnp.where(lax.axis_index("tm") == slabs - 1, initial, ours))
-    terms = fine_part(state, speed_rows, flag_rows, near, far, slabs)
     quads, ys = range(QUAD), range(slabs // QUAD**2)
     of_quad = [[y * QUAD**2 + q * QUAD + step for step in range(QUAD) for y in ys] for q in quads]
-    terms = swap_blocks(terms, of_quad)
+    windows = swap_blocks(window_part(by_row(guess[0]), by_row(initial), slabs), of_quad)
+    pairs = []
+    for group in of_quad:
+        for slab, start in ((group[ORDER.index(CHUNKS - 1)], 0), (group[ORDER.index(0)], 1)):
+            for i in range(start, blocks - 1, 2):
+                ends = slab * blocks + i, slab * blocks + i + 1
+                pairs += [ends, ends[::-1]]
+    edge = on_device(edge_kernel, "edge_rows", COEFS + ROWS, windows, speed_rows, flag_rows)
+    message = lax.ppermute(edge, ("tm", "space"), pairs)
+    terms = on_device(fine_kernel, "fine_steps", rows * MODES, windows, message, speed_rows, flag_rows)
     size = MODES * HALVES * ROWS
     carry = on_device(quad_kernel, "quad_carry", size, terms, speed_rows)
     partner = lax.ppermute(carry, "tm", [(c, c ^ QUAD) for c in range(slabs)])
     joint = on_device(pair_kernel, "pair_carry", size, carry, partner, speed_rows)
     far = lax.ppermute(joint, "tm", [(c, c ^ (3 * QUAD)) for c in range(slabs)])
     sums = on_device(slab_kernel, "slab_sums", rows * MODES, terms, carry, partner, far, speed_rows)
-    sums = swap_blocks(sums, of_quad)
-    sums = sums.reshape(rows, MODES, LANES)
+    sums = write_part(swap_blocks(sums, of_quad)).reshape(rows, MODES, LANES)
     return sums.transpose(1, 0, 2).reshape(1, MODES, count)
 
 

time: 63.2 us -> 60.5 us (0.957)
  starting transfers between devices: 22.7 us -> 18.6 us
  blocking collectives: 30 us -> 32.4 us
  waiting for transfers between devices: 5.04 us -> 3.77 us
  Pallas kernels: 4.37 us -> 5.4 us
  local copies, waits for them, and re-layouts: 0.68 us -> 0.01 us
    ppermute x2 -> x1, starting transfers between devices: 5.42 us -> 0.66 us  [body(): message = lax.ppermute(edge, ('tm', 'space'), pairs)]
    pallas_call x3 -> x5, Pallas kernels: 0.34 us -> 3.67 us  [on_device(): pl.pallas_call(kernel, out_shape=jax.ShapeDtypeStruct((rows, LANES), jnp....]
    all_to_all x2, blocking collectives: 30 us -> 32.4 us  [swap_blocks(): lax.all_to_all(x.reshape(-1, MODES, LANES), 'tm', 0, 0, axis_index_groups...]
    pallas_call x2, Pallas kernels: 4.03 us -> 1.73 us  [the longest x1 0.93 us: window_part(): pl.pallas_call(functools.partial(window_kernel, slabs), out_shape=jax.Sha...]
    ppermute x2 -> x1, waiting for transfers between devices: 0.7 us -> 0.01 us  [body(): message = lax.ppermute(edge, ('tm', 'space'), pairs)]
    ppermute x1, starting transfers between devices: 8.19 us -> 8.86 us  [body(): far = lax.ppermute(joint, 'tm', [(c, c ^ 3 * QUAD) for c in range(slabs)])]
    unnamed x9 -> x4, local copies, waits for them, and re-layouts: 0.68 us -> 0.01 us
  transfers between devices with their start and end apart: 4 -> 3, of which waited for: 3 -> 2; matrix products, arithmetic and copies ran while one was open for 0% -> 0% of each run, Pallas kernels for 0% -> 0%
where the time goes in v6:
time: 60.5 us; the launch traced here: 60.3 us
  blocking collectives  32.4 us (54%)
  starting transfers between devices  18.6 us (31%)
  Pallas kernels  5.4 us (9%)
  waiting for transfers between devices  3.77 us (6%)
    all_to_all x2, blocking collectives, swap_blocks(): lax.all_to_all(x.reshape(-1, MODES, LANES), 'tm', 0, 0, axis_index_groups...  32.4 us
    ppermute x1, starting transfers between devices, body(): partner = lax.ppermute(carry, 'tm', [(c, c ^ QUAD) for c in range(slabs)])  9.1 us
    ppermute x1, starting transfers between devices, body(): far = lax.ppermute(joint, 'tm', [(c, c ^ 3 * QUAD) for c in range(slabs)])  8.86 us
    pallas_call x5, Pallas kernels, on_device(): pl.pallas_call(kernel, out_shape=jax.ShapeDtypeStruct((rows, LANES), jnp....  3.67 us
    ppermute x1, waiting for transfers between devices, body(): partner = lax.ppermute(carry, 'tm', [(c, c ^ QUAD) for c in range(slabs)])  1.89 us
    ppermute x1, waiting for transfers between devices, body(): far = lax.ppermute(joint, 'tm', [(c, c ^ 3 * QUAD) for c in range(slabs)])  1.88 us
  transfers between devices with their start and end apart: 3, of which 2 were waited for; matrix products, arithmetic and copies ran while one was open for 0% of the time, Pallas kernels for 0%

profile of v6, /device:TPU:2, one launch (start us, length us, event | category | flops | bytes accessed | tf_op | source)
XLA Modules:
  0.0 60.3 jit_solution(602094118280534934)
XLA Ops:
  0.0 0.9 %windows.1 = f32[320,128]{1,0:T(8,128)S(1)} custom-call(f32[256,128]{1,0:T(8,128)} %bitcast.33, f32[256,128]{1,0:T(8,128)} %bitcast.34), custom_call_target="tpu_custom_call" | custom-call | tf_op jit(solution)/shard_map/windows/pallas_call | solution.py:140
  0.9 0.0 copy-start
  1.0 0.0 copy-start.1
  1.0 17.6 %all_to_all.10 = f32[80,4,128]{2,1,0:T(4,128)S(1)} all-to-all(f32[80,4,128]{2,1,0:T(4,128)S(1)} %bitcast.28), channel_id=1, replica_groups={{0,128,256,384,8,136,264,392,16,144,272,400,24,152,280,408},{32,160,288..., dimensions={0} | all-to-all | bytes 327680 | tf_op jit(solution)/shard_map/all_to_all | solution.py:399
  18.6 0.0 copy-done
  18.6 0.0 copy-done.1
  18.6 0.7 %collective-permute-start = (f32[72,128]{1,0:T(8,128)S(1)}, f32[72,128]{1,0:T(8,128)S(1)}, u32[]{:S(2)}, u32[]{:S(2)}) collective-permute-start(f32[72,128]{1,0:T(8,128)S(1)} %edge_rows.1), channel_id=1, source_target_pairs={{16,17},{17,16},{18,19},{19,18},{20,21},{21,20},{22,23},{23,22},{9... | collective-permute-start | bytes 110600 | tf_op jit(solution)/shard_map/ppermute | solution.py:421
  19.3 0.0 collective-permute-done.message_ref
  19.3 3.3 %fine_steps.1.term_ref = f32[256,128]{1,0:T(8,128)S(1)} custom-call(f32[320,128]{1,0:T(8,128)S(1)} %bitcast.22, f32[72,128]{1,0:T(8,128)S(1)} %collective-permute-done.message_ref, f32[64,128]{1,0:T(8,128)S(1)} %bitcast.24, s32[64,128]{1,0:T(8,128)S(1)} %bitcast.32), custom_call_target="tpu_custom_call" | custom-call | tf_op jit(solution)/shard_map/fine_steps/pallas_call | solution.py:388
  22.6 0.1 quad_carry.1.carry_ref
  22.7 9.1 %collective-permute-start.1 = (f32[64,128]{1,0:T(8,128)S(1)}, f32[64,128]{1,0:T(8,128)S(1)}, u32[]{:S(2)}, u32[]{:S(2)}) collective-permute-start(f32[64,128]{1,0:T(8,128)S(1)} %quad_carry.1.carry_ref), channel_id=1, source_target_pairs={{0,32},{8,40},{16,48},{24,56},{32,0},{40,8},{48,16},{56,24},{64,96... | collective-permute-start | bytes 98312 | tf_op jit(solution)/shard_map/ppermute | solution.py:425
  31.8 1.9 %collective-permute-done.1.partner_ref = f32[64,128]{1,0:T(8,128)S(1)} collective-permute-done((f32[64,128]{1,0:T(8,128)S(1)}, f32[64,128]{1,0:T(8,128)S(1)}, u32[]{:S(2)}, u32[]{:S(2)}) %collective-permute-start.1) | collective-permute-done | bytes 32800 | tf_op jit(solution)/shard_map/ppermute | solution.py:425
  33.7 0.1 pair_carry.1
  33.8 8.9 %collective-permute-start.2 = (f32[64,128]{1,0:T(8,128)S(1)}, f32[64,128]{1,0:T(8,128)S(1)}, u32[]{:S(2)}, u32[]{:S(2)}) collective-permute-start(f32[64,128]{1,0:T(8,128)S(1)} %pair_carry.1), channel_id=1, source_target_pairs={{0,96},{8,104},{16,112},{24,120},{32,64},{40,72},{48,80},{56,88},{... | collective-permute-start | bytes 98312 | tf_op jit(solution)/shard_map/ppermute | solution.py:427
  42.6 1.9 %collective-permute-done.2.far_ref = f32[64,128]{1,0:T(8,128)S(1)} collective-permute-done((f32[64,128]{1,0:T(8,128)S(1)}, f32[64,128]{1,0:T(8,128)S(1)}, u32[]{:S(2)}, u32[]{:S(2)}) %collective-permute-start.2) | collective-permute-done | bytes 32800 | tf_op jit(solution)/shard_map/ppermute | solution.py:427
  44.5 0.2 slab_sums.1
  44.7 14.7 %all_to_all.11 = f32[64,4,128]{2,1,0:T(4,128)S(1)} all-to-all(f32[64,4,128]{2,1,0:T(4,128)S(1)} %bitcast.29), channel_id=1, replica_groups={{0,128,256,384,8,136,264,392,16,144,272,400,24,152,280,408},{32,160,288..., dimensions={0} | all-to-all | bytes 262144 | tf_op jit(solution)/shard_map/all_to_all | solution.py:399
  59.5 0.8 %write_out.1 = f32[256,128]{1,0:T(8,128)} custom-call(f32[256,128]{1,0:T(8,128)S(1)} %bitcast.30), custom_call_target="tpu_custom_call" | custom-call | tf_op jit(solution)/shard_map/write_out/pallas_call | solution.py:255
  (1 shorter events, 0.0 us)
Async XLA Ops:
  0.9 17.7 %copy-start = (f32[8192]{0:T(1024)S(1)}, f32[8192]{0:T(1024)}, u32[]{:S(2)}) copy-start(f32[8192]{0:T(1024)} %param.6) | copy-start | bytes 98308
  1.0 17.6 %copy-start.1 = (s32[8192]{0:T(1024)S(1)}, s32[8192]{0:T(1024)}, u32[]{:S(2)}) copy-start(s32[8192]{0:T(1024)} %param.7) | copy-start | bytes 98308
  18.6 0.7 %collective-permute-start = (f32[72,128]{1,0:T(8,128)S(1)}, f32[72,128]{1,0:T(8,128)S(1)}, u32[]{:S(2)}, u32[]{:S(2)}) collective-permute-start(f32[72,128]{1,0:T(8,128)S(1)} %edge_rows.1), channel_id=1, source_target_pairs={{16,17},{17,16},{18,19},{19,18},{20,21},{21,20},{22,23},{23,22},{9... | collective-permute-start | bytes 110600 | tf_op jit(solution)/shard_map/ppermute | solution.py:421
  22.7 11.0 %collective-permute-start.1 = (f32[64,128]{1,0:T(8,128)S(1)}, f32[64,128]{1,0:T(8,128)S(1)}, u32[]{:S(2)}, u32[]{:S(2)}) collective-permute-start(f32[64,128]{1,0:T(8,128)S(1)} %quad_carry.1.carry_ref), channel_id=1, source_target_pairs={{0,32},{8,40},{16,48},{24,56},{32,0},{40,8},{48,16},{56,24},{64,96... | collective-permute-start | bytes 98312 | tf_op jit(solution)/shard_map/ppermute | solution.py:425
  33.8 10.7 %collective-permute-start.2 = (f32[64,128]{1,0:T(8,128)S(1)}, f32[64,128]{1,0:T(8,128)S(1)}, u32[]{:S(2)}, u32[]{:S(2)}) collective-permute-start(f32[64,128]{1,0:T(8,128)S(1)} %pair_carry.1), channel_id=1, source_target_pairs={{0,96},{8,104},{16,112},{24,120},{32,64},{40,72},{48,80},{56,88},{... | collective-permute-start | bytes 98312 | tf_op jit(solution)/shard_map/ppermute | solution.py:427

commit v7 on v6

--- a/solution.py
+++ b/solution.py
@@ -85,7 +85,7 @@
 HALVES = 2
 CHUNKS = 16
 WINDOW = (CHUNK + 1) * MODES
-ORDER = (4, 1, 2, 3, 0, 5, 6, 7, 15, 9, 10, 11, 12, 13, 14, 8)
+ORDER = (1, 2, 3, 4, 0, 15, 5, 6, 7, 8, 9, 10, 11, 12, 13, 14)
 BACKWARDS = tuple(CHUNKS - 1 - chunk for chunk in ORDER)
 
 
@@ -104,18 +104,29 @@
     return z // QUAD, jnp.where(even_block(), chunk, CHUNKS - 1 - chunk)
 
 
-def window_kernel(slabs, guess_ref, initial_ref, out_ref, state, sem):
+COPIES = 4
+
+
+def window_kernel(slabs, guess_ref, initial_ref, out_ref, state, sems):
     last = lax.axis_index("tm") == slabs - 1
+    rows = state.shape[0] // COPIES
+
+    def copies(source):
+        parts = [pl.ds(i * rows, rows) for i in range(COPIES)]
+        return [pltpu.make_async_copy(source.at[part], state.at[part], sems.at[i]) for i, part in enumerate(parts)]
 
     @pl.when(last)
     def _():
-        pltpu.make_async_copy(initial_ref, state, sem).start()
+        for copy in copies(initial_ref):
+            copy.start()
 
     @pl.when(jnp.logical_not(last))
     def _():
-        pltpu.make_async_copy(guess_ref, state, sem).start()
-
-    pltpu.make_async_copy(guess_ref, state, sem).wait()
+        for copy in copies(guess_ref):
+            copy.start()
+
+    for copy in copies(guess_ref):
+        copy.wait()
     low = lax.broadcasted_iota(jnp.int32, (MODES, LANES), 1) < LANES // 2
     size = CHUNK * MODES
 
@@ -142,7 +153,7 @@
         out_shape=jax.ShapeDtypeStruct((CHUNKS * WINDOW, LANES), jnp.float32),
         in_specs=[pl.BlockSpec(memory_space=pltpu.HBM)] * 2,
         out_specs=pl.BlockSpec(memory_space=pltpu.VMEM),
-        scratch_shapes=[pltpu.VMEM(guess.shape, jnp.float32), pltpu.SemaphoreType.DMA],
+        scratch_shapes=[pltpu.VMEM(guess.shape, jnp.float32), pltpu.SemaphoreType.DMA((COPIES,))],
         compiler_params=pltpu.CompilerParams(vmem_limit_bytes=16 * 1024 * 1024),
         name="windows",
     )(*(pltpu.with_memory_space_constraint(x, pltpu.HBM) for x in (guess, initial)))
@@ -152,90 +163,151 @@
     return pl.ds((half * ROWS * (CHUNK + 1) + r) * MODES + k, ROWS, stride=WINDOW)
 
 
-def message_rows(half, k):
-    return pl.ds((k * HALVES + half) * ROWS, ROWS)
-
-
-COEFS = MODES * HALVES * ROWS
+SHARE = LANES // MODES
+COEFS = HALVES * ROWS
 
 
 def edge_kernel(window_ref, speed_ref, flag_ref, out_ref):
     _, chunk = place()
     tail = chunk == CHUNKS - 1
     rows = speed_ref.shape[0]
-    for half in range(HALVES):
+    group = lax.broadcasted_iota(jnp.int32, (ROWS, LANES), 1) // SHARE
+    for half in range(HALVES):
+        packed = jnp.zeros((ROWS, LANES), jnp.float32)
         for k in range(MODES):
             first, final = window_ref[window_rows(half, 0, k), :], window_ref[window_rows(half, CHUNK - 1, k), :]
-            out_ref[message_rows(half, k), :] = jnp.where(tail, final, first)
+            moved = jnp.where(tail, pltpu.roll(final, (k + 1) * SHARE % LANES, 1), pltpu.roll(first, k * SHARE, 1))
+            packed = jnp.where(group == k, moved, packed)
+        out_ref[pl.ds(half * ROWS, ROWS), :] = packed
     at = jnp.where(tail, rows - 1, 0)
     out_ref[pl.ds(COEFS, 1), :] = speed_ref[pl.ds(at, 1), :]
     out_ref[pl.ds(COEFS + 1, 1), :] = 1.0 - flag_ref[pl.ds(at, 1), :].astype(jnp.float32)
     out_ref[pl.ds(COEFS + 2, ROWS - 2), :] = jnp.zeros((ROWS - 2, LANES), jnp.float32)
 
 
-def fine_kernel(window_ref, message_ref, speed_ref, flag_ref, out_ref):
+def coarse_kernel(window_ref, speed_ref, out_ref):
     quad, chunk = place()
-    first, final = chunk == 0, chunk == CHUNKS - 1
     shape = (ROWS, LANES)
-    row = lax.broadcasted_iota(jnp.int32, shape, 0)
-    lane = lax.broadcasted_iota(jnp.int32, shape, 1)
-    low = lane < LANES // 2
-    outside = jnp.logical_or(jnp.logical_and(low, final), jnp.logical_and(lane >= LANES // 2, first))
-
-    def coef(read, k):
-        def spread(x):
-            return jnp.broadcast_to(x, shape)
-
-        at = chunk * CHUNK
-        own = [spread(read(at + r)) for r in range(CHUNK)]
-        after = spread(read(jnp.minimum(at + CHUNK, CHUNKS * CHUNK - 1)))
-        before = spread(read(jnp.maximum(at - 1, 0)))
-        beyond = spread(message_ref[pl.ds(COEFS + k, 1), :])
-        return [*own, jnp.where(outside, beyond, jnp.where(low, after, before))]
-
-    speed = coef(lambda i: speed_ref[pl.ds(i, 1), :], 0)
-    opened = coef(lambda i: 1.0 - flag_ref[pl.ds(i, 1), :].astype(jnp.float32), 1)
-    wall = jnp.logical_and(jnp.logical_and(first, lax.axis_index("space") == 0), lane == 0)
-    opened[0] = jnp.where(wall, 0.0, opened[0])
+    last = jnp.logical_and(quad == QUAD - 1, lax.broadcasted_iota(jnp.int32, shape, 0) == ROWS - 1)
+    for r in range(CHUNK):
+        speed = jnp.broadcast_to(speed_ref[pl.ds(chunk * CHUNK + r, 1), :], shape)
+        speed2 = 2.0 * speed
+        for half in range(HALVES):
+            start = [window_ref[window_rows(half, r, k), :] for k in range(MODES)]
+            coarse = three_sections(start, lambda u: local_rhs(u, speed, speed2), STEPS * STEP)
+            if half == HALVES - 1:
+                coarse = [jnp.where(last, 0.0, x) for x in coarse]
+            for k in range(MODES):
+                out_ref[slab_rows(half, r, k), :] = coarse[k]
+
+
+def slab_rows(half, r, k):
+    return pl.ds((half * ROWS * CHUNK + r) * MODES + k, ROWS, stride=CHUNK * MODES)
+
+
+def derived(speed, opened):
     gate = [(0.5 * VISCOSITY) * x for x in opened]
-    gate_after = shifted(gate, -1)
     inflow = [x * y for x, y in zip(opened, shifted(speed, 1))]
-    speed2 = [2.0 * x for x in speed]
-
-    starts = []
-    for half in range(HALVES):
-        start = [[window_ref[window_rows(half, r, k), :] for k in range(MODES)] for r in range(CHUNK + 1)]
-        start[CHUNK] = [
-            jnp.where(outside, message_ref[message_rows(half, k), :], x) for k, x in enumerate(start[CHUNK])
-        ]
-        starts.append(start)
-
+    return speed, [2.0 * x for x in speed], inflow, gate, shifted(gate, -1)
+
+
+def fine_steps(starts, coefs):
     def advance(_, us):
         nows = us
         for share in (3.0, 2.0, 1.0):
             scale = column_scales(STEP / share)
-            nows = [full_step(u, now, scale, speed, speed2, inflow, gate, gate_after) for u, now in zip(us, nows)]
+            nows = [full_step(u, now, scale, *coefs) for u, now in zip(us, nows)]
         return nows
 
-    finals = lax.fori_loop(0, STEPS, advance, starts, unroll=True)
+    return lax.fori_loop(0, STEPS, advance, starts, unroll=True)
+
+
+def fine_kernel(window_ref, coarse_ref, speed_ref, flag_ref, out_ref):
+    _, chunk = place()
+    first, final = chunk == 0, chunk == CHUNKS - 1
+    shape = (ROWS, LANES)
+    lane = lax.broadcasted_iota(jnp.int32, shape, 1)
+    low = lane < LANES // 2
+    outside = jnp.logical_or(jnp.logical_and(low, final), jnp.logical_and(lane >= LANES // 2, first))
+
+    def coef(read):
+        at = chunk * CHUNK
+        own = [jnp.broadcast_to(read(at + r), shape) for r in range(CHUNK)]
+        after = jnp.broadcast_to(read(jnp.minimum(at + CHUNK, CHUNKS * CHUNK - 1)), shape)
+        before = jnp.broadcast_to(read(jnp.maximum(at - 1, 0)), shape)
+        return [*own, jnp.where(outside, 0.0, jnp.where(low, after, before))]
+
+    speed = coef(lambda i: speed_ref[pl.ds(i, 1), :])
+    opened = coef(lambda i: 1.0 - flag_ref[pl.ds(i, 1), :].astype(jnp.float32))
+    wall = jnp.logical_and(jnp.logical_and(first, lax.axis_index("space") == 0), lane == 0)
+    opened[0] = jnp.where(wall, 0.0, opened[0])
+    coefs = derived(speed, opened)
+    starts = []
+    for half in range(HALVES):
+        start = [[window_ref[window_rows(half, r, k), :] for k in range(MODES)] for r in range(CHUNK + 1)]
+        start[CHUNK] = [jnp.where(outside, 0.0, x) for x in start[CHUNK]]
+        starts.append(start)
+    finals = fine_steps(starts, coefs)
     for half in range(HALVES):
         for r in range(CHUNK):
-            coarse = three_sections(starts[half][r], lambda u: local_rhs(u, speed[r], speed2[r]), STEPS * STEP)
-            if half == HALVES - 1:
-                last = jnp.logical_and(quad == QUAD - 1, row == ROWS - 1)
-                coarse = [jnp.where(last, 0.0, x) for x in coarse]
             for k in range(MODES):
-                rows = pl.ds((half * ROWS * CHUNK + r) * MODES + k, ROWS, stride=CHUNK * MODES)
-                out_ref[rows, :] = finals[half][r][k] - coarse[k]
+                rows = slab_rows(half, r, k)
+                out_ref[rows, :] = finals[half][r][k] - coarse_ref[rows, :]
+
+
+def end_kernel(term_ref, window_ref, coarse_ref, message_ref, speed_ref, flag_ref, out_ref):
+    _, chunk = place()
+    first, final = chunk == 0, chunk == CHUNKS - 1
+    out_ref[...] = term_ref[...]
+
+    @pl.when(jnp.logical_or(first, final))
+    def _():
+        shape = (ROWS, LANES)
+        lane = lax.broadcasted_iota(jnp.int32, shape, 1)
+        low = lane < LANES // 2
+        own_side = jnp.logical_xor(low, final)
+        at = jnp.where(first, 0, CHUNKS * CHUNK - 1)
+
+        def joined_row(own, other):
+            return pltpu.roll(jnp.where(own_side, own, other), LANES // 2, 1)
+
+        opened = 1.0 - flag_ref[pl.ds(at, 1), :].astype(jnp.float32)
+        wall = jnp.logical_and(jnp.logical_and(first, lax.axis_index("space") == 0), lane == 0)
+        opened = jnp.where(wall, 0.0, jnp.broadcast_to(opened, shape))
+        beyond = [jnp.broadcast_to(message_ref[pl.ds(COEFS + i, 1), :], shape) for i in range(2)]
+        speed = joined_row(jnp.broadcast_to(speed_ref[pl.ds(at, 1), :], shape), beyond[0])
+        coefs = derived([speed], [joined_row(opened, beyond[1])])
+        starts = []
+        for half in range(HALVES):
+            packed = message_ref[pl.ds(half * ROWS, ROWS), :]
+            start = []
+            for k in range(MODES):
+                own = jnp.where(first, window_ref[window_rows(half, 0, k), :], window_ref[window_rows(half, CHUNK - 1, k), :])
+                after, before = pltpu.roll(packed, -k * SHARE % LANES, 1), pltpu.roll(packed, (MODES - 1 - k) * SHARE, 1)
+                start.append(joined_row(own, jnp.where(final, after, before)))
+            starts.append([start])
+        finals = fine_steps(starts, coefs)
+        near_end = jnp.logical_or(jnp.logical_and(first, lane < SHARE), jnp.logical_and(final, lane >= LANES - SHARE))
+        for r, here in ((0, first), (CHUNK - 1, final)):
+
+            @pl.when(here)
+            def _(r=r):
+                for half in range(HALVES):
+                    for k in range(MODES):
+                        rows = slab_rows(half, r, k)
+                        made = pltpu.roll(finals[half][0][k], LANES // 2, 1) - coarse_ref[rows, :]
+                        out_ref[rows, :] = jnp.where(near_end, made, term_ref[rows, :])
 
 
 def write_kernel(sums_ref, out_ref, sems):
     size = CHUNK * MODES
 
     def write(chunks):
+        starts = [i for i in range(CHUNKS) if i == 0 or chunks[i] != chunks[i - 1] + 1]
         copies = []
-        for position, chunk in enumerate(chunks):
-            source, target = pl.ds(position * size, size), pl.ds(chunk * size, size)
+        for position, end in zip(starts, [*starts[1:], CHUNKS]):
+            count = (end - position) * size
+            source, target = pl.ds(position * size, count), pl.ds(chunks[position] * size, count)
             copies.append(pltpu.make_async_copy(sums_ref.at[source], out_ref.at[target], sems.at[position]))
         for copy in copies:
             copy.start()
@@ -419,7 +491,9 @@
                 pairs += [ends, ends[::-1]]
     edge = on_device(edge_kernel, "edge_rows", COEFS + ROWS, windows, speed_rows, flag_rows)
     message = lax.ppermute(edge, ("tm", "space"), pairs)
-    terms = on_device(fine_kernel, "fine_steps", rows * MODES, windows, message, speed_rows, flag_rows)
+    coarse = on_device(coarse_kernel, "coarse_steps", rows * MODES, windows, speed_rows)
+    terms = on_device(fine_kernel, "fine_steps", rows * MODES, windows, coarse, speed_rows, flag_rows)
+    terms = on_device(end_kernel, "block_ends", rows * MODES, terms, windows, coarse, message, speed_rows, flag_rows)
     size = MODES * HALVES * ROWS
     carry = on_device(quad_kernel, "quad_carry", size, terms, speed_rows)
     partner = lax.ppermute(carry, "tm", [(c, c ^ QUAD) for c in range(slabs)])

time: 60.5 us -> 59.8 us (0.988)
  blocking collectives: 32.4 us -> 31.2 us
  waiting for transfers between devices: 3.77 us -> 4.65 us
  starting transfers between devices: 18.6 us -> 17.9 us
    all_to_all x2, blocking collectives: 32.4 us -> 31.2 us  [swap_blocks(): lax.all_to_all(x.reshape(-1, MODES, LANES), 'tm', 0, 0, axis_index_groups...]
    ppermute x1, starting transfers between devices: 8.86 us -> 8.11 us  [body(): far = lax.ppermute(joint, 'tm', [(c, c ^ 3 * QUAD) for c in range(slabs)])]
    ppermute x1, waiting for transfers between devices: 1.89 us -> 2.54 us  [body(): partner = lax.ppermute(carry, 'tm', [(c, c ^ QUAD) for c in range(slabs)])]
    pallas_call x5 -> x7, Pallas kernels: 3.67 us -> 3.92 us  [on_device(): pl.pallas_call(kernel, out_shape=jax.ShapeDtypeStruct((rows, LANES), jnp....]
  transfers between devices with their start and end apart: 3 -> 3, of which waited for: 2 -> 2; matrix products, arithmetic and copies ran while one was open for 0% -> 0% of each run, Pallas kernels for 0% -> 6%
where the time goes in v7:
time: 59.8 us; the launch traced here: 59.4 us
  blocking collectives  31.2 us (52%)
  starting transfers between devices  17.9 us (30%)
  Pallas kernels  5.57 us (9%)
  waiting for transfers between devices  4.65 us (8%)
    all_to_all x2, blocking collectives, swap_blocks(): lax.all_to_all(x.reshape(-1, MODES, LANES), 'tm', 0, 0, axis_index_groups...  31.2 us
    ppermute x1, starting transfers between devices, body(): partner = lax.ppermute(carry, 'tm', [(c, c ^ QUAD) for c in range(slabs)])  9.1 us
    ppermute x1, starting transfers between devices, body(): far = lax.ppermute(joint, 'tm', [(c, c ^ 3 * QUAD) for c in range(slabs)])  8.11 us
    pallas_call x7, Pallas kernels, on_device(): pl.pallas_call(kernel, out_shape=jax.ShapeDtypeStruct((rows, LANES), jnp....  3.92 us
    ppermute x1, waiting for transfers between devices, body(): partner = lax.ppermute(carry, 'tm', [(c, c ^ QUAD) for c in range(slabs)])  2.54 us
    ppermute x1, waiting for transfers between devices, body(): far = lax.ppermute(joint, 'tm', [(c, c ^ 3 * QUAD) for c in range(slabs)])  2.11 us
  transfers between devices with their start and end apart: 3, of which 2 were waited for; matrix products, arithmetic and copies ran while one was open for 0% of the time, Pallas kernels for 6%

profile of v7, /device:TPU:2, one launch (start us, length us, event | category | flops | bytes accessed | tf_op | source)
XLA Modules:
  0.0 59.4 jit_solution(18317485609590897165)
XLA Ops:
  0.0 0.9 %windows.1 = f32[320,128]{1,0:T(8,128)S(1)} custom-call(f32[256,128]{1,0:T(8,128)} %bitcast.38, f32[256,128]{1,0:T(8,128)} %bitcast.39), custom_call_target="tpu_custom_call" | custom-call | tf_op jit(solution)/shard_map/windows/pallas_call | solution.py:151
  0.9 0.0 copy-start
  0.9 0.0 copy-start.1
  0.9 17.6 %all_to_all.10 = f32[80,4,128]{2,1,0:T(4,128)S(1)} all-to-all(f32[80,4,128]{2,1,0:T(4,128)S(1)} %bitcast.32), channel_id=1, replica_groups={{0,128,256,384,8,136,264,392,16,144,272,400,24,152,280,408},{32,160,288..., dimensions={0} | all-to-all | bytes 327680 | tf_op jit(solution)/shard_map/all_to_all | solution.py:471
  18.5 0.0 copy-done
  18.5 0.0 copy-done.1
  18.5 0.1 edge_rows.1
  18.6 0.7 %collective-permute-start = (f32[24,128]{1,0:T(8,128)S(1)}, f32[24,128]{1,0:T(8,128)S(1)}, u32[]{:S(2)}, u32[]{:S(2)}) collective-permute-start(f32[24,128]{1,0:T(8,128)S(1)} %edge_rows.1), channel_id=1, source_target_pairs={{136,137},{137,136},{138,139},{139,138},{140,141},{141,140},{142,1... | collective-permute-start | bytes 36872 | tf_op jit(solution)/shard_map/ppermute | solution.py:493
  19.3 0.1 coarse_steps.1.coarse_ref
  19.4 3.3 %fine_steps.1.term_ref = f32[256,128]{1,0:T(8,128)S(1)} custom-call(f32[320,128]{1,0:T(8,128)S(1)} %bitcast.23, f32[256,128]{1,0:T(8,128)S(1)} %coarse_steps.1.coarse_ref, f32[64,128]{1,0:T(8,128)S(1)} %bitcast.27, s32[64,128]{1,0:T(8,128)S(1)} %bitcast.36), custom_call_target="tpu_custom_call" | custom-call | tf_op jit(solution)/shard_map/fine_steps/pallas_call | solution.py:460
  22.7 0.0 collective-permute-done.message_ref
  22.8 0.1 quad_carry.1.carry_ref
  22.9 9.1 %collective-permute-start.1 = (f32[64,128]{1,0:T(8,128)S(1)}, f32[64,128]{1,0:T(8,128)S(1)}, u32[]{:S(2)}, u32[]{:S(2)}) collective-permute-start(f32[64,128]{1,0:T(8,128)S(1)} %quad_carry.1.carry_ref), channel_id=1, source_target_pairs={{0,32},{8,40},{16,48},{24,56},{32,0},{40,8},{48,16},{56,24},{64,96... | collective-permute-start | bytes 98312 | tf_op jit(solution)/shard_map/ppermute | solution.py:499
  32.0 2.5 %collective-permute-done.1.partner_ref = f32[64,128]{1,0:T(8,128)S(1)} collective-permute-done((f32[64,128]{1,0:T(8,128)S(1)}, f32[64,128]{1,0:T(8,128)S(1)}, u32[]{:S(2)}, u32[]{:S(2)}) %collective-permute-start.1) | collective-permute-done | bytes 32800 | tf_op jit(solution)/shard_map/ppermute | solution.py:499
  34.5 0.1 pair_carry.1
  34.6 8.1 %collective-permute-start.2 = (f32[64,128]{1,0:T(8,128)S(1)}, f32[64,128]{1,0:T(8,128)S(1)}, u32[]{:S(2)}, u32[]{:S(2)}) collective-permute-start(f32[64,128]{1,0:T(8,128)S(1)} %pair_carry.1), channel_id=1, source_target_pairs={{0,96},{8,104},{16,112},{24,120},{32,64},{40,72},{48,80},{56,88},{... | collective-permute-start | bytes 98312 | tf_op jit(solution)/shard_map/ppermute | solution.py:501
  42.7 2.1 %collective-permute-done.2.far_ref = f32[64,128]{1,0:T(8,128)S(1)} collective-permute-done((f32[64,128]{1,0:T(8,128)S(1)}, f32[64,128]{1,0:T(8,128)S(1)}, u32[]{:S(2)}, u32[]{:S(2)}) %collective-permute-start.2) | collective-permute-done | bytes 32800 | tf_op jit(solution)/shard_map/ppermute | solution.py:501
  44.8 0.2 slab_sums.1
  45.0 13.6 %all_to_all.11 = f32[64,4,128]{2,1,0:T(4,128)S(1)} all-to-all(f32[64,4,128]{2,1,0:T(4,128)S(1)} %bitcast.33), channel_id=1, replica_groups={{0,128,256,384,8,136,264,392,16,144,272,400,24,152,280,408},{32,160,288..., dimensions={0} | all-to-all | bytes 262144 | tf_op jit(solution)/shard_map/all_to_all | solution.py:471
  58.6 0.8 %write_out.1 = f32[256,128]{1,0:T(8,128)} custom-call(f32[256,128]{1,0:T(8,128)S(1)} %bitcast.34), custom_call_target="tpu_custom_call" | custom-call | tf_op jit(solution)/shard_map/write_out/pallas_call | solution.py:327
  (1 shorter events, 0.0 us)
Async XLA Ops:
  0.9 17.7 %copy-start = (f32[8192]{0:T(1024)S(1)}, f32[8192]{0:T(1024)}, u32[]{:S(2)}) copy-start(f32[8192]{0:T(1024)} %param.6) | copy-start | bytes 98308
  0.9 17.6 %copy-start.1 = (s32[8192]{0:T(1024)S(1)}, s32[8192]{0:T(1024)}, u32[]{:S(2)}) copy-start(s32[8192]{0:T(1024)} %param.7) | copy-start | bytes 98308
  18.6 4.1 %collective-permute-start = (f32[24,128]{1,0:T(8,128)S(1)}, f32[24,128]{1,0:T(8,128)S(1)}, u32[]{:S(2)}, u32[]{:S(2)}) collective-permute-start(f32[24,128]{1,0:T(8,128)S(1)} %edge_rows.1), channel_id=1, source_target_pairs={{136,137},{137,136},{138,139},{139,138},{140,141},{141,140},{142,1... | collective-permute-start | bytes 36872 | tf_op jit(solution)/shard_map/ppermute | solution.py:493
  22.9 11.6 %collective-permute-start.1 = (f32[64,128]{1,0:T(8,128)S(1)}, f32[64,128]{1,0:T(8,128)S(1)}, u32[]{:S(2)}, u32[]{:S(2)}) collective-permute-start(f32[64,128]{1,0:T(8,128)S(1)} %quad_carry.1.carry_ref), channel_id=1, source_target_pairs={{0,32},{8,40},{16,48},{24,56},{32,0},{40,8},{48,16},{56,24},{64,96... | collective-permute-start | bytes 98312 | tf_op jit(solution)/shard_map/ppermute | solution.py:499
  34.6 10.2 %collective-permute-start.2 = (f32[64,128]{1,0:T(8,128)S(1)}, f32[64,128]{1,0:T(8,128)S(1)}, u32[]{:S(2)}, u32[]{:S(2)}) collective-permute-start(f32[64,128]{1,0:T(8,128)S(1)} %pair_carry.1), channel_id=1, source_target_pairs={{0,96},{8,104},{16,112},{24,120},{32,64},{40,72},{48,80},{56,88},{... | collective-permute-start | bytes 98312 | tf_op jit(solution)/shard_map/ppermute | solution.py:501

commit v8 on v7

--- a/solution.py
+++ b/solution.py
@@ -84,7 +84,8 @@
 CHUNK = 4
 HALVES = 2
 CHUNKS = 16
-WINDOW = (CHUNK + 1) * MODES
+WINDOW = CHUNK * MODES + 2
+SHARE = LANES // MODES
 ORDER = (1, 2, 3, 4, 0, 15, 5, 6, 7, 8, 9, 10, 11, 12, 13, 14)
 BACKWARDS = tuple(CHUNKS - 1 - chunk for chunk in ORDER)
 
@@ -127,16 +128,28 @@
 
     for copy in copies(guess_ref):
         copy.wait()
-    low = lax.broadcasted_iota(jnp.int32, (MODES, LANES), 1) < LANES // 2
     size = CHUNK * MODES
+    group = lax.broadcasted_iota(jnp.int32, (ROWS, LANES), 1) // SHARE
+
+    def packed(row, shift):
+        vectors = []
+        for i in range(CHUNKS // ROWS):
+            total = jnp.zeros((ROWS, LANES), jnp.float32)
+            for k in range(MODES):
+                read = state[pl.ds(i * ROWS * size + row * MODES + k, ROWS, stride=size), :]
+                total = jnp.where(group == k, pltpu.roll(read, (k * SHARE + shift) % LANES, 1), total)
+            vectors.append(total)
+        return [vectors[n // ROWS][n % ROWS : n % ROWS + 1] for n in range(CHUNKS)]
+
+    heads, tails = packed(0, 0), packed(CHUNK - 1, SHARE)
+    none = jnp.zeros((1, LANES), jnp.float32)
 
     def write(chunks):
         for position, chunk in enumerate(chunks):
-            at, source = position * WINDOW, chunk * size
-            out_ref[pl.ds(at, size), :] = state[pl.ds(source, size), :]
-            after = state[pl.ds(min(source + size, (CHUNKS - 1) * size), MODES), :]
-            before = state[pl.ds(max(source - MODES, 0), MODES), :]
-            out_ref[pl.ds(at + size, MODES), :] = jnp.where(low, after, before)
+            at = position * WINDOW
+            out_ref[pl.ds(at, size), :] = state[pl.ds(chunk * size, size), :]
+            out_ref[pl.ds(at + size, 1), :] = heads[chunk + 1] if chunk < CHUNKS - 1 else none
+            out_ref[pl.ds(at + size + 1, 1), :] = tails[chunk - 1] if chunk else none
 
     @pl.when(even_block())
     def _():
@@ -160,10 +173,13 @@
 
 
 def window_rows(half, r, k):
-    return pl.ds((half * ROWS * (CHUNK + 1) + r) * MODES + k, ROWS, stride=WINDOW)
-
-
-SHARE = LANES // MODES
+    return pl.ds(half * ROWS * WINDOW + r * MODES + k, ROWS, stride=WINDOW)
+
+
+def unpacked(after, before, k, low):
+    return jnp.where(low, pltpu.roll(after, -k * SHARE % LANES, 1), pltpu.roll(before, (MODES - 1 - k) * SHARE, 1))
+
+
 COEFS = HALVES * ROWS
 
 
@@ -244,8 +260,9 @@
     coefs = derived(speed, opened)
     starts = []
     for half in range(HALVES):
-        start = [[window_ref[window_rows(half, r, k), :] for k in range(MODES)] for r in range(CHUNK + 1)]
-        start[CHUNK] = [jnp.where(outside, 0.0, x) for x in start[CHUNK]]
+        start = [[window_ref[window_rows(half, r, k), :] for k in range(MODES)] for r in range(CHUNK)]
+        after, before = (window_ref[window_rows(half, CHUNK, i), :] for i in range(2))
+        start.append([jnp.where(outside, 0.0, unpacked(after, before, k, low)) for k in range(MODES)])
         starts.append(start)
     finals = fine_steps(starts, coefs)
     for half in range(HALVES):
@@ -283,8 +300,7 @@
             start = []
             for k in range(MODES):
                 own = jnp.where(first, window_ref[window_rows(half, 0, k), :], window_ref[window_rows(half, CHUNK - 1, k), :])
-                after, before = pltpu.roll(packed, -k * SHARE % LANES, 1), pltpu.roll(packed, (MODES - 1 - k) * SHARE, 1)
-                start.append(joined_row(own, jnp.where(final, after, before)))
+                start.append(joined_row(own, unpacked(packed, packed, k, low)))
             starts.append([start])
         finals = fine_steps(starts, coefs)
         near_end = jnp.logical_or(jnp.logical_and(first, lane < SHARE), jnp.logical_and(final, lane >= LANES - SHARE))
@@ -302,13 +318,11 @@
 def write_kernel(sums_ref, out_ref, sems):
     size = CHUNK * MODES
 
-    def write(chunks):
-        starts = [i for i in range(CHUNKS) if i == 0 or chunks[i] != chunks[i - 1] + 1]
+    def write(pairs, count):
         copies = []
-        for position, end in zip(starts, [*starts[1:], CHUNKS]):
-            count = (end - position) * size
-            source, target = pl.ds(position * size, count), pl.ds(chunks[position] * size, count)
-            copies.append(pltpu.make_async_copy(sums_ref.at[source], out_ref.at[target], sems.at[position]))
+        for i, (source, target) in enumerate(pairs):
+            source, target = pl.ds(source * size, count * size), pl.ds(target * size, count * size)
+            copies.append(pltpu.make_async_copy(sums_ref.at[source], out_ref.at[target], sems.at[i]))
         for copy in copies:
             copy.start()
         for copy in copies:
@@ -316,11 +330,11 @@
 
     @pl.when(even_block())
     def _():
-        write(ORDER)
+        write([(i, i) for i in range(0, CHUNKS, CHUNKS // COPIES)], CHUNKS // COPIES)
 
     @pl.when(jnp.logical_not(even_block()))
     def _():
-        write(BACKWARDS)
+        write([(i, CHUNKS - 1 - i) for i in range(CHUNKS)], 1)
 
 
 def write_part(sums):
@@ -449,8 +463,10 @@
         state = chosen(odd, times(over_quad, state), state)
         state = added(state, here[half])
         for step in range(QUAD):
-            for k in range(MODES):
-                out_ref[term_rows(step, half, k), :] = state[k]
+            for i in range(HALVES):
+                block = ORDER[step * QUAD + half * HALVES + i] * CHUNK * MODES
+                for k in range(MODES):
+                    out_ref[pl.ds(block + k, CHUNK, stride=MODES), :] = state[k][i * CHUNK : (i + 1) * CHUNK]
             if step < QUAD - 1:
                 terms = [term_ref[term_rows(step, half, k), :] for k in range(MODES)]
                 state = added(times(matrix, state), terms)
@@ -467,8 +483,8 @@
     )(*operands)
 
 
-def swap_blocks(x, groups):
-    return lax.all_to_all(x.reshape(-1, MODES, LANES), "tm", 0, 0, axis_index_groups=groups, tiled=True).reshape(x.shape)
+def swap_blocks(x, groups, rows=MODES):
+    return lax.all_to_all(x.reshape(-1, rows, LANES), "tm", 0, 0, axis_index_groups=groups, tiled=True).reshape(x.shape)
 
 
 def body(initial, guess, speeds, flags):
@@ -482,7 +498,7 @@
     speed_rows, flag_rows = speeds.reshape(rows, LANES), flags.reshape(rows, LANES)
     quads, ys = range(QUAD), range(slabs // QUAD**2)
     of_quad = [[y * QUAD**2 + q * QUAD + step for step in range(QUAD) for y in ys] for q in quads]
-    windows = swap_blocks(window_part(by_row(guess[0]), by_row(initial), slabs), of_quad)
+    windows = swap_blocks(window_part(by_row(guess[0]), by_row(initial), slabs), of_quad, 2)
     pairs = []
     for group in of_quad:
         for slab, start in ((group[ORDER.index(CHUNKS - 1)], 0), (group[ORDER.index(0)], 1)):
@@ -500,7 +516,8 @@
     joint = on_device(pair_kernel, "pair_carry", size, carry, partner, speed_rows)
     far = lax.ppermute(joint, "tm", [(c, c ^ (3 * QUAD)) for c in range(slabs)])
     sums = on_device(slab_kernel, "slab_sums", rows * MODES, terms, carry, partner, far, speed_rows)
-    sums = write_part(swap_blocks(sums, of_quad)).reshape(rows, MODES, LANES)
+    by_chunk = [[group[ORDER.index(i)] for i in range(CHUNKS)] for group in of_quad]
+    sums = write_part(swap_blocks(sums, by_chunk)).reshape(rows, MODES, LANES)
     return sums.transpose(1, 0, 2).reshape(1, MODES, count)
 
 

time: 59.8 us -> 58.9 us (0.985)
  blocking collectives: 31.2 us -> 30.5 us
    all_to_all x2, blocking collectives: 31.2 us -> 30.5 us  [swap_blocks(): lax.all_to_all(x.reshape(-1, rows, LANES), 'tm', 0, 0, axis_index_groups=...]
where the time goes in v8:
time: 58.9 us; the launch traced here: 58.5 us
  blocking collectives  30.5 us (52%)
  starting transfers between devices  18.2 us (31%)
  Pallas kernels  5.66 us (10%)
  waiting for transfers between devices  4.13 us (7%)
    all_to_all x2, blocking collectives, swap_blocks(): lax.all_to_all(x.reshape(-1, rows, LANES), 'tm', 0, 0, axis_index_groups=...  30.5 us
    ppermute x1, starting transfers between devices, body(): partner = lax.ppermute(carry, 'tm', [(c, c ^ QUAD) for c in range(slabs)])  9.1 us
    ppermute x1, starting transfers between devices, body(): far = lax.ppermute(joint, 'tm', [(c, c ^ 3 * QUAD) for c in range(slabs)])  8.4 us
    pallas_call x7, Pallas kernels, on_device(): pl.pallas_call(kernel, out_shape=jax.ShapeDtypeStruct((rows, LANES), jnp....  3.95 us
    ppermute x1, waiting for transfers between devices, body(): partner = lax.ppermute(carry, 'tm', [(c, c ^ QUAD) for c in range(slabs)])  2.25 us
    ppermute x1, waiting for transfers between devices, body(): far = lax.ppermute(joint, 'tm', [(c, c ^ 3 * QUAD) for c in range(slabs)])  1.88 us
  transfers between devices with their start and end apart: 3, of which 2 were waited for; matrix products, arithmetic and copies ran while one was open for 0% of the time, Pallas kernels for 6%

profile of v8, /device:TPU:2, one launch (start us, length us, event | category | flops | bytes accessed | tf_op | source)
XLA Modules:
  0.0 58.5 jit_solution(8945478983422037446)
XLA Ops:
  0.0 0.9 %windows.1 = f32[288,128]{1,0:T(8,128)S(1)} custom-call(f32[256,128]{1,0:T(8,128)} %bitcast.38, f32[256,128]{1,0:T(8,128)} %bitcast.39), custom_call_target="tpu_custom_call" | custom-call | tf_op jit(solution)/shard_map/windows/pallas_call | solution.py:164
  0.9 0.0 copy-start
  0.9 0.0 copy-start.1
  1.0 17.5 %all_to_all.10 = f32[144,2,128]{2,1,0:T(2,128)S(1)} all-to-all(f32[144,2,128]{2,1,0:T(2,128)S(1)} %bitcast.32), channel_id=1, replica_groups={{0,128,256,384,8,136,264,392,16,144,272,400,24,152,280,408},{32,160,288..., dimensions={0} | all-to-all | bytes 294912 | tf_op jit(solution)/shard_map/all_to_all | solution.py:487
  18.5 0.0 copy-done
  18.5 0.0 copy-done.1
  18.5 0.1 edge_rows.1
  18.5 0.7 %collective-permute-start = (f32[24,128]{1,0:T(8,128)S(1)}, f32[24,128]{1,0:T(8,128)S(1)}, u32[]{:S(2)}, u32[]{:S(2)}) collective-permute-start(f32[24,128]{1,0:T(8,128)S(1)} %edge_rows.1), channel_id=1, source_target_pairs={{136,137},{137,136},{138,139},{139,138},{140,141},{141,140},{142,1... | collective-permute-start | bytes 36872 | tf_op jit(solution)/shard_map/ppermute | solution.py:509
  19.2 0.1 coarse_steps.1.coarse_ref
  19.4 3.3 %fine_steps.1.term_ref = f32[256,128]{1,0:T(8,128)S(1)} custom-call(f32[288,128]{1,0:T(8,128)S(1)} %bitcast.23, f32[256,128]{1,0:T(8,128)S(1)} %coarse_steps.1.coarse_ref, f32[64,128]{1,0:T(8,128)S(1)} %bitcast.27, s32[64,128]{1,0:T(8,128)S(1)} %bitcast.36), custom_call_target="tpu_custom_call" | custom-call | tf_op jit(solution)/shard_map/fine_steps/pallas_call | solution.py:476
  22.7 0.0 collective-permute-done.message_ref
  22.7 0.1 quad_carry.1.carry_ref
  22.8 9.1 %collective-permute-start.1 = (f32[64,128]{1,0:T(8,128)S(1)}, f32[64,128]{1,0:T(8,128)S(1)}, u32[]{:S(2)}, u32[]{:S(2)}) collective-permute-start(f32[64,128]{1,0:T(8,128)S(1)} %quad_carry.1.carry_ref), channel_id=1, source_target_pairs={{0,32},{8,40},{16,48},{24,56},{32,0},{40,8},{48,16},{56,24},{64,96... | collective-permute-start | bytes 98312 | tf_op jit(solution)/shard_map/ppermute | solution.py:515
  31.9 2.2 %collective-permute-done.1.partner_ref = f32[64,128]{1,0:T(8,128)S(1)} collective-permute-done((f32[64,128]{1,0:T(8,128)S(1)}, f32[64,128]{1,0:T(8,128)S(1)}, u32[]{:S(2)}, u32[]{:S(2)}) %collective-permute-start.1) | collective-permute-done | bytes 32800 | tf_op jit(solution)/shard_map/ppermute | solution.py:515
  34.2 0.1 pair_carry.1
  34.3 8.4 %collective-permute-start.2 = (f32[64,128]{1,0:T(8,128)S(1)}, f32[64,128]{1,0:T(8,128)S(1)}, u32[]{:S(2)}, u32[]{:S(2)}) collective-permute-start(f32[64,128]{1,0:T(8,128)S(1)} %pair_carry.1), channel_id=1, source_target_pairs={{0,96},{8,104},{16,112},{24,120},{32,64},{40,72},{48,80},{56,88},{... | collective-permute-start | bytes 98312 | tf_op jit(solution)/shard_map/ppermute | solution.py:517
  42.7 1.9 %collective-permute-done.2.far_ref = f32[64,128]{1,0:T(8,128)S(1)} collective-permute-done((f32[64,128]{1,0:T(8,128)S(1)}, f32[64,128]{1,0:T(8,128)S(1)}, u32[]{:S(2)}, u32[]{:S(2)}) %collective-permute-start.2) | collective-permute-done | bytes 32800 | tf_op jit(solution)/shard_map/ppermute | solution.py:517
  44.6 0.2 slab_sums.1
  44.8 13.0 %all_to_all.11 = f32[64,4,128]{2,1,0:T(4,128)S(1)} all-to-all(f32[64,4,128]{2,1,0:T(4,128)S(1)} %bitcast.33), channel_id=1, replica_groups={{8,0,128,256,384,264,392,16,144,272,400,24,152,280,408,136},{40,32,160,..., dimensions={0} | all-to-all | bytes 262144 | tf_op jit(solution)/shard_map/all_to_all | solution.py:487
  57.7 0.8 %write_out.1 = f32[256,128]{1,0:T(8,128)} custom-call(f32[256,128]{1,0:T(8,128)S(1)} %bitcast.34), custom_call_target="tpu_custom_call" | custom-call | tf_op jit(solution)/shard_map/write_out/pallas_call | solution.py:341
  (1 shorter events, 0.0 us)
Async XLA Ops:
  0.9 17.5 %copy-start = (f32[8192]{0:T(1024)S(1)}, f32[8192]{0:T(1024)}, u32[]{:S(2)}) copy-start(f32[8192]{0:T(1024)} %param.6) | copy-start | bytes 98308
  0.9 17.5 %copy-start.1 = (s32[8192]{0:T(1024)S(1)}, s32[8192]{0:T(1024)}, u32[]{:S(2)}) copy-start(s32[8192]{0:T(1024)} %param.7) | copy-start | bytes 98308
  18.5 4.1 %collective-permute-start = (f32[24,128]{1,0:T(8,128)S(1)}, f32[24,128]{1,0:T(8,128)S(1)}, u32[]{:S(2)}, u32[]{:S(2)}) collective-permute-start(f32[24,128]{1,0:T(8,128)S(1)} %edge_rows.1), channel_id=1, source_target_pairs={{136,137},{137,136},{138,139},{139,138},{140,141},{141,140},{142,1... | collective-permute-start | bytes 36872 | tf_op jit(solution)/shard_map/ppermute | solution.py:509
  22.8 11.4 %collective-permute-start.1 = (f32[64,128]{1,0:T(8,128)S(1)}, f32[64,128]{1,0:T(8,128)S(1)}, u32[]{:S(2)}, u32[]{:S(2)}) collective-permute-start(f32[64,128]{1,0:T(8,128)S(1)} %quad_carry.1.carry_ref), channel_id=1, source_target_pairs={{0,32},{8,40},{16,48},{24,56},{32,0},{40,8},{48,16},{56,24},{64,96... | collective-permute-start | bytes 98312 | tf_op jit(solution)/shard_map/ppermute | solution.py:515
  34.3 10.3 %collective-permute-start.2 = (f32[64,128]{1,0:T(8,128)S(1)}, f32[64,128]{1,0:T(8,128)S(1)}, u32[]{:S(2)}, u32[]{:S(2)}) collective-permute-start(f32[64,128]{1,0:T(8,128)S(1)} %pair_carry.1), channel_id=1, source_target_pairs={{0,96},{8,104},{16,112},{24,120},{32,64},{40,72},{48,80},{56,88},{... | collective-permute-start | bytes 98312 | tf_op jit(solution)/shard_map/ppermute | solution.py:517

commit v9 on v8

--- a/solution.py
+++ b/solution.py
@@ -87,6 +87,7 @@
 WINDOW = CHUNK * MODES + 2
 SHARE = LANES // MODES
 ORDER = (1, 2, 3, 4, 0, 15, 5, 6, 7, 8, 9, 10, 11, 12, 13, 14)
+LISTED = (4, 5, 2, 3, 0, 1, 6, 7, 8, 9, 10, 11, 12, 13, 14, 15)
 BACKWARDS = tuple(CHUNKS - 1 - chunk for chunk in ORDER)
 
 
@@ -145,8 +146,8 @@
     none = jnp.zeros((1, LANES), jnp.float32)
 
     def write(chunks):
-        for position, chunk in enumerate(chunks):
-            at = position * WINDOW
+        for position, place_there in enumerate(LISTED):
+            at, chunk = position * WINDOW, chunks[place_there]
             out_ref[pl.ds(at, size), :] = state[pl.ds(chunk * size, size), :]
             out_ref[pl.ds(at + size, 1), :] = heads[chunk + 1] if chunk < CHUNKS - 1 else none
             out_ref[pl.ds(at + size + 1, 1), :] = tails[chunk - 1] if chunk else none
@@ -217,6 +218,11 @@
                 out_ref[slab_rows(half, r, k), :] = coarse[k]
 
 
+def by_place(half, x):
+    row = lax.broadcasted_iota(jnp.int32, x.shape, 0)
+    return jnp.where(row % QUAD < QUAD // 2, pltpu.roll(x, QUAD, 0), x) if half == 0 else x
+
+
 def slab_rows(half, r, k):
     return pl.ds((half * ROWS * CHUNK + r) * MODES + k, ROWS, stride=CHUNK * MODES)
 
@@ -269,7 +275,7 @@
         for r in range(CHUNK):
             for k in range(MODES):
                 rows = slab_rows(half, r, k)
-                out_ref[rows, :] = finals[half][r][k] - coarse_ref[rows, :]
+                out_ref[rows, :] = by_place(half, finals[half][r][k] - coarse_ref[rows, :])
 
 
 def end_kernel(term_ref, window_ref, coarse_ref, message_ref, speed_ref, flag_ref, out_ref):
@@ -312,7 +318,7 @@
                     for k in range(MODES):
                         rows = slab_rows(half, r, k)
                         made = pltpu.roll(finals[half][0][k], LANES // 2, 1) - coarse_ref[rows, :]
-                        out_ref[rows, :] = jnp.where(near_end, made, term_ref[rows, :])
+                        out_ref[rows, :] = jnp.where(near_end, by_place(half, made), term_ref[rows, :])
 
 
 def write_kernel(sums_ref, out_ref, sems):
@@ -498,7 +504,8 @@
     speed_rows, flag_rows = speeds.reshape(rows, LANES), flags.reshape(rows, LANES)
     quads, ys = range(QUAD), range(slabs // QUAD**2)
     of_quad = [[y * QUAD**2 + q * QUAD + step for step in range(QUAD) for y in ys] for q in quads]
-    windows = swap_blocks(window_part(by_row(guess[0]), by_row(initial), slabs), of_quad, 2)
+    listed = [[group[p] for p in LISTED] for group in of_quad]
+    windows = swap_blocks(window_part(by_row(guess[0]), by_row(initial), slabs), listed, 2)
     pairs = []
     for group in of_quad:
         for slab, start in ((group[ORDER.index(CHUNKS - 1)], 0), (group[ORDER.index(0)], 1)):

time: 58.9 us -> 58.5 us (level)
  no operation moved by 1% of the time
where the time goes in v9:
time: 58.5 us; the launch traced here: 58.1 us
  blocking collectives  30.1 us (51%)
  starting transfers between devices  18.2 us (31%)
  Pallas kernels  5.67 us (10%)
  waiting for transfers between devices  4.11 us (7%)
    all_to_all x2, blocking collectives, swap_blocks(): lax.all_to_all(x.reshape(-1, rows, LANES), 'tm', 0, 0, axis_index_groups=...  30.1 us
    ppermute x1, starting transfers between devices, body(): partner = lax.ppermute(carry, 'tm', [(c, c ^ QUAD) for c in range(slabs)])  9.1 us
    ppermute x1, starting transfers between devices, body(): far = lax.ppermute(joint, 'tm', [(c, c ^ 3 * QUAD) for c in range(slabs)])  8.42 us
    pallas_call x7, Pallas kernels, on_device(): pl.pallas_call(kernel, out_shape=jax.ShapeDtypeStruct((rows, LANES), jnp....  3.96 us
    ppermute x1, waiting for transfers between devices, body(): partner = lax.ppermute(carry, 'tm', [(c, c ^ QUAD) for c in range(slabs)])  2.23 us
    ppermute x1, waiting for transfers between devices, body(): far = lax.ppermute(joint, 'tm', [(c, c ^ 3 * QUAD) for c in range(slabs)])  1.88 us
  transfers between devices with their start and end apart: 3, of which 2 were waited for; matrix products, arithmetic and copies ran while one was open for 0% of the time, Pallas kernels for 6%

profile of v9, /device:TPU:2, one launch (start us, length us, event | category | flops | bytes accessed | tf_op | source)
XLA Modules:
  0.0 58.1 jit_solution(437125757383428006)
XLA Ops:
  0.0 0.9 %windows.1 = f32[288,128]{1,0:T(8,128)S(1)} custom-call(f32[256,128]{1,0:T(8,128)} %bitcast.38, f32[256,128]{1,0:T(8,128)} %bitcast.39), custom_call_target="tpu_custom_call" | custom-call | tf_op jit(solution)/shard_map/windows/pallas_call | solution.py:165
  0.9 0.0 copy-start
  0.9 0.0 copy-start.1
  1.0 16.1 %all_to_all.10 = f32[144,2,128]{2,1,0:T(2,128)S(1)} all-to-all(f32[144,2,128]{2,1,0:T(2,128)S(1)} %bitcast.32), channel_id=1, replica_groups={{8,136,256,384,0,128,264,392,16,144,272,400,24,152,280,408},{40,168,288..., dimensions={0} | all-to-all | bytes 294912 | tf_op jit(solution)/shard_map/all_to_all | solution.py:493
  17.0 0.0 copy-done
  17.0 0.0 copy-done.1
  17.0 0.1 edge_rows.1
  17.1 0.7 %collective-permute-start = (f32[24,128]{1,0:T(8,128)S(1)}, f32[24,128]{1,0:T(8,128)S(1)}, u32[]{:S(2)}, u32[]{:S(2)}) collective-permute-start(f32[24,128]{1,0:T(8,128)S(1)} %edge_rows.1), channel_id=1, source_target_pairs={{136,137},{137,136},{138,139},{139,138},{140,141},{141,140},{142,1... | collective-permute-start | bytes 36872 | tf_op jit(solution)/shard_map/ppermute | solution.py:516
  17.8 0.1 coarse_steps.1.coarse_ref
  18.0 3.3 %fine_steps.1.term_ref = f32[256,128]{1,0:T(8,128)S(1)} custom-call(f32[288,128]{1,0:T(8,128)S(1)} %bitcast.23, f32[256,128]{1,0:T(8,128)S(1)} %coarse_steps.1.coarse_ref, f32[64,128]{1,0:T(8,128)S(1)} %bitcast.27, s32[64,128]{1,0:T(8,128)S(1)} %bitcast.36), custom_call_target="tpu_custom_call" | custom-call | tf_op jit(solution)/shard_map/fine_steps/pallas_call | solution.py:482
  21.3 0.0 collective-permute-done.message_ref
  21.3 0.1 quad_carry.1.carry_ref
  21.4 9.1 %collective-permute-start.1 = (f32[64,128]{1,0:T(8,128)S(1)}, f32[64,128]{1,0:T(8,128)S(1)}, u32[]{:S(2)}, u32[]{:S(2)}) collective-permute-start(f32[64,128]{1,0:T(8,128)S(1)} %quad_carry.1.carry_ref), channel_id=1, source_target_pairs={{0,32},{8,40},{16,48},{24,56},{32,0},{40,8},{48,16},{56,24},{64,96... | collective-permute-start | bytes 98312 | tf_op jit(solution)/shard_map/ppermute | solution.py:522
  30.5 2.2 %collective-permute-done.1.partner_ref = f32[64,128]{1,0:T(8,128)S(1)} collective-permute-done((f32[64,128]{1,0:T(8,128)S(1)}, f32[64,128]{1,0:T(8,128)S(1)}, u32[]{:S(2)}, u32[]{:S(2)}) %collective-permute-start.1) | collective-permute-done | bytes 32800 | tf_op jit(solution)/shard_map/ppermute | solution.py:522
  32.8 0.1 pair_carry.1
  32.8 8.4 %collective-permute-start.2 = (f32[64,128]{1,0:T(8,128)S(1)}, f32[64,128]{1,0:T(8,128)S(1)}, u32[]{:S(2)}, u32[]{:S(2)}) collective-permute-start(f32[64,128]{1,0:T(8,128)S(1)} %pair_carry.1), channel_id=1, source_target_pairs={{0,96},{8,104},{16,112},{24,120},{32,64},{40,72},{48,80},{56,88},{... | collective-permute-start | bytes 98312 | tf_op jit(solution)/shard_map/ppermute | solution.py:524
  41.3 1.9 %collective-permute-done.2.far_ref = f32[64,128]{1,0:T(8,128)S(1)} collective-permute-done((f32[64,128]{1,0:T(8,128)S(1)}, f32[64,128]{1,0:T(8,128)S(1)}, u32[]{:S(2)}, u32[]{:S(2)}) %collective-permute-start.2) | collective-permute-done | bytes 32800 | tf_op jit(solution)/shard_map/ppermute | solution.py:524
  43.2 0.2 slab_sums.1
  43.4 14.0 %all_to_all.11 = f32[64,4,128]{2,1,0:T(4,128)S(1)} all-to-all(f32[64,4,128]{2,1,0:T(4,128)S(1)} %bitcast.33), channel_id=1, replica_groups={{8,0,128,256,384,264,392,16,144,272,400,24,152,280,408,136},{40,32,160,..., dimensions={0} | all-to-all | bytes 262144 | tf_op jit(solution)/shard_map/all_to_all | solution.py:493
  57.3 0.8 %write_out.1 = f32[256,128]{1,0:T(8,128)} custom-call(f32[256,128]{1,0:T(8,128)S(1)} %bitcast.34), custom_call_target="tpu_custom_call" | custom-call | tf_op jit(solution)/shard_map/write_out/pallas_call | solution.py:347
  (1 shorter events, 0.0 us)
Async XLA Ops:
  0.9 16.1 %copy-start = (f32[8192]{0:T(1024)S(1)}, f32[8192]{0:T(1024)}, u32[]{:S(2)}) copy-start(f32[8192]{0:T(1024)} %param.6) | copy-start | bytes 98308
  0.9 16.1 %copy-start.1 = (s32[8192]{0:T(1024)S(1)}, s32[8192]{0:T(1024)}, u32[]{:S(2)}) copy-start(s32[8192]{0:T(1024)} %param.7) | copy-start | bytes 98308
  17.1 4.1 %collective-permute-start = (f32[24,128]{1,0:T(8,128)S(1)}, f32[24,128]{1,0:T(8,128)S(1)}, u32[]{:S(2)}, u32[]{:S(2)}) collective-permute-start(f32[24,128]{1,0:T(8,128)S(1)} %edge_rows.1), channel_id=1, source_target_pairs={{136,137},{137,136},{138,139},{139,138},{140,141},{141,140},{142,1... | collective-permute-start | bytes 36872 | tf_op jit(solution)/shard_map/ppermute | solution.py:516
  21.4 11.3 %collective-permute-start.1 = (f32[64,128]{1,0:T(8,128)S(1)}, f32[64,128]{1,0:T(8,128)S(1)}, u32[]{:S(2)}, u32[]{:S(2)}) collective-permute-start(f32[64,128]{1,0:T(8,128)S(1)} %quad_carry.1.carry_ref), channel_id=1, source_target_pairs={{0,32},{8,40},{16,48},{24,56},{32,0},{40,8},{48,16},{56,24},{64,96... | collective-permute-start | bytes 98312 | tf_op jit(solution)/shard_map/ppermute | solution.py:522
  32.8 10.3 %collective-permute-start.2 = (f32[64,128]{1,0:T(8,128)S(1)}, f32[64,128]{1,0:T(8,128)S(1)}, u32[]{:S(2)}, u32[]{:S(2)}) collective-permute-start(f32[64,128]{1,0:T(8,128)S(1)} %pair_carry.1), channel_id=1, source_target_pairs={{0,96},{8,104},{16,112},{24,120},{32,64},{40,72},{48,80},{56,88},{... | collective-permute-start | bytes 98312 | tf_op jit(solution)/shard_map/ppermute | solution.py:524

commit v10 on v9

--- a/solution.py
+++ b/solution.py
@@ -24,6 +24,8 @@
 
 def shifted(xs, step):
     rolled = [pltpu.roll(x, step % LANES, 1) for x in xs]
+    if len(xs) == 1:
+        return rolled
     lane = lax.broadcasted_iota(jnp.int32, xs[0].shape, 1)
     edge = lane == (0 if step == 1 else LANES - 1)
     return [jnp.where(edge, rolled[(v - step) % len(xs)], x) for v, x in enumerate(rolled)]
@@ -202,20 +204,13 @@
     out_ref[pl.ds(COEFS + 2, ROWS - 2), :] = jnp.zeros((ROWS - 2, LANES), jnp.float32)
 
 
-def coarse_kernel(window_ref, speed_ref, out_ref):
-    quad, chunk = place()
-    shape = (ROWS, LANES)
-    last = jnp.logical_and(quad == QUAD - 1, lax.broadcasted_iota(jnp.int32, shape, 0) == ROWS - 1)
-    for r in range(CHUNK):
-        speed = jnp.broadcast_to(speed_ref[pl.ds(chunk * CHUNK + r, 1), :], shape)
-        speed2 = 2.0 * speed
-        for half in range(HALVES):
-            start = [window_ref[window_rows(half, r, k), :] for k in range(MODES)]
-            coarse = three_sections(start, lambda u: local_rhs(u, speed, speed2), STEPS * STEP)
-            if half == HALVES - 1:
-                coarse = [jnp.where(last, 0.0, x) for x in coarse]
-            for k in range(MODES):
-                out_ref[slab_rows(half, r, k), :] = coarse[k]
+def coarse_step(start, speed, half, quad):
+    speed2 = 2.0 * speed
+    coarse = three_sections(start, lambda u: local_rhs(u, speed, speed2), STEPS * STEP)
+    if half < HALVES - 1:
+        return coarse
+    last = jnp.logical_and(quad == QUAD - 1, lax.broadcasted_iota(jnp.int32, speed.shape, 0) == ROWS - 1)
+    return [jnp.where(last, 0.0, x) for x in coarse]
 
 
 def by_place(half, x):
@@ -244,8 +239,8 @@
     return lax.fori_loop(0, STEPS, advance, starts, unroll=True)
 
 
-def fine_kernel(window_ref, coarse_ref, speed_ref, flag_ref, out_ref):
-    _, chunk = place()
+def fine_kernel(window_ref, speed_ref, flag_ref, out_ref):
+    quad, chunk = place()
     first, final = chunk == 0, chunk == CHUNKS - 1
     shape = (ROWS, LANES)
     lane = lax.broadcasted_iota(jnp.int32, shape, 1)
@@ -273,13 +268,13 @@
     finals = fine_steps(starts, coefs)
     for half in range(HALVES):
         for r in range(CHUNK):
+            coarse = coarse_step(starts[half][r], speed[r], half, quad)
             for k in range(MODES):
-                rows = slab_rows(half, r, k)
-                out_ref[rows, :] = by_place(half, finals[half][r][k] - coarse_ref[rows, :])
-
-
-def end_kernel(term_ref, window_ref, coarse_ref, message_ref, speed_ref, flag_ref, out_ref):
-    _, chunk = place()
+                out_ref[slab_rows(half, r, k), :] = by_place(half, finals[half][r][k] - coarse[k])
+
+
+def end_kernel(term_ref, window_ref, message_ref, speed_ref, flag_ref, out_ref):
+    quad, chunk = place()
     first, final = chunk == 0, chunk == CHUNKS - 1
     out_ref[...] = term_ref[...]
 
@@ -298,16 +293,18 @@
         wall = jnp.logical_and(jnp.logical_and(first, lax.axis_index("space") == 0), lane == 0)
         opened = jnp.where(wall, 0.0, jnp.broadcast_to(opened, shape))
         beyond = [jnp.broadcast_to(message_ref[pl.ds(COEFS + i, 1), :], shape) for i in range(2)]
-        speed = joined_row(jnp.broadcast_to(speed_ref[pl.ds(at, 1), :], shape), beyond[0])
-        coefs = derived([speed], [joined_row(opened, beyond[1])])
-        starts = []
+        own_speed = jnp.broadcast_to(speed_ref[pl.ds(at, 1), :], shape)
+        coefs = derived([joined_row(own_speed, beyond[0])], [joined_row(opened, beyond[1])])
+        starts, coarse = [], []
         for half in range(HALVES):
             packed = message_ref[pl.ds(half * ROWS, ROWS), :]
-            start = []
+            start, owns = [], []
             for k in range(MODES):
                 own = jnp.where(first, window_ref[window_rows(half, 0, k), :], window_ref[window_rows(half, CHUNK - 1, k), :])
+                owns.append(own)
                 start.append(joined_row(own, unpacked(packed, packed, k, low)))
             starts.append([start])
+            coarse.append(coarse_step(owns, own_speed, half, quad))
         finals = fine_steps(starts, coefs)
         near_end = jnp.logical_or(jnp.logical_and(first, lane < SHARE), jnp.logical_and(final, lane >= LANES - SHARE))
         for r, here in ((0, first), (CHUNK - 1, final)):
@@ -317,7 +314,7 @@
                 for half in range(HALVES):
                     for k in range(MODES):
                         rows = slab_rows(half, r, k)
-                        made = pltpu.roll(finals[half][0][k], LANES // 2, 1) - coarse_ref[rows, :]
+                        made = pltpu.roll(finals[half][0][k], LANES // 2, 1) - coarse[half][k]
                         out_ref[rows, :] = jnp.where(near_end, by_place(half, made), term_ref[rows, :])
 
 
@@ -514,9 +511,8 @@
                 pairs += [ends, ends[::-1]]
     edge = on_device(edge_kernel, "edge_rows", COEFS + ROWS, windows, speed_rows, flag_rows)
     message = lax.ppermute(edge, ("tm", "space"), pairs)
-    coarse = on_device(coarse_kernel, "coarse_steps", rows * MODES, windows, speed_rows)
-    terms = on_device(fine_kernel, "fine_steps", rows * MODES, windows, coarse, speed_rows, flag_rows)
-    terms = on_device(end_kernel, "block_ends", rows * MODES, terms, windows, coarse, message, speed_rows, flag_rows)
+    terms = on_device(fine_kernel, "fine_steps", rows * MODES, windows, speed_rows, flag_rows)
+    terms = on_device(end_kernel, "block_ends", rows * MODES, terms, windows, message, speed_rows, flag_rows)
     size = MODES * HALVES * ROWS
     carry = on_device(quad_kernel, "quad_carry", size, terms, speed_rows)
     partner = lax.ppermute(carry, "tm", [(c, c ^ QUAD) for c in range(slabs)])

time: 58.5 us -> 58.3 us (level)
    pallas_call x7 -> x6, Pallas kernels: 3.96 us -> 3.8 us  [on_device(): pl.pallas_call(kernel, out_shape=jax.ShapeDtypeStruct((rows, LANES), jnp....]
where the time goes in v10:
time: 58.3 us; the launch traced here: 58 us
  blocking collectives  30.1 us (52%)
  starting transfers between devices  18.2 us (31%)
  Pallas kernels  5.52 us (9%)
  waiting for transfers between devices  4.11 us (7%)
    all_to_all x2, blocking collectives, swap_blocks(): lax.all_to_all(x.reshape(-1, rows, LANES), 'tm', 0, 0, axis_index_groups=...  30.1 us
    ppermute x1, starting transfers between devices, body(): partner = lax.ppermute(carry, 'tm', [(c, c ^ QUAD) for c in range(slabs)])  9.1 us
    ppermute x1, starting transfers between devices, body(): far = lax.ppermute(joint, 'tm', [(c, c ^ 3 * QUAD) for c in range(slabs)])  8.42 us
    pallas_call x6, Pallas kernels, on_device(): pl.pallas_call(kernel, out_shape=jax.ShapeDtypeStruct((rows, LANES), jnp....  3.8 us
    ppermute x1, waiting for transfers between devices, body(): partner = lax.ppermute(carry, 'tm', [(c, c ^ QUAD) for c in range(slabs)])  2.23 us
    ppermute x1, waiting for transfers between devices, body(): far = lax.ppermute(joint, 'tm', [(c, c ^ 3 * QUAD) for c in range(slabs)])  1.88 us
  transfers between devices with their start and end apart: 3, of which 2 were waited for; matrix products, arithmetic and copies ran while one was open for 0% of the time, Pallas kernels for 6%

profile of v10, /device:TPU:2, one launch (start us, length us, event | category | flops | bytes accessed | tf_op | source)
XLA Modules:
  0.0 58.0 jit_solution(17639575863837673138)
XLA Ops:
  0.0 0.9 %windows.1 = f32[288,128]{1,0:T(8,128)S(1)} custom-call(f32[256,128]{1,0:T(8,128)} %bitcast.36, f32[256,128]{1,0:T(8,128)} %bitcast.37), custom_call_target="tpu_custom_call" | custom-call | tf_op jit(solution)/shard_map/windows/pallas_call | solution.py:167
  0.9 0.0 copy-start
  0.9 0.0 copy-start.1
  1.0 16.1 %all_to_all.10 = f32[144,2,128]{2,1,0:T(2,128)S(1)} all-to-all(f32[144,2,128]{2,1,0:T(2,128)S(1)} %bitcast.30), channel_id=1, replica_groups={{8,136,256,384,0,128,264,392,16,144,272,400,24,152,280,408},{40,168,288..., dimensions={0} | all-to-all | bytes 294912 | tf_op jit(solution)/shard_map/all_to_all | solution.py:490
  17.0 0.0 copy-done
  17.0 0.0 copy-done.1
  17.0 0.1 edge_rows.1
  17.1 0.7 %collective-permute-start = (f32[24,128]{1,0:T(8,128)S(1)}, f32[24,128]{1,0:T(8,128)S(1)}, u32[]{:S(2)}, u32[]{:S(2)}) collective-permute-start(f32[24,128]{1,0:T(8,128)S(1)} %edge_rows.1), channel_id=1, source_target_pairs={{136,137},{137,136},{138,139},{139,138},{140,141},{141,140},{142,1... | collective-permute-start | bytes 36872 | tf_op jit(solution)/shard_map/ppermute | solution.py:513
  17.8 3.3 %fine_steps.1.term_ref = f32[256,128]{1,0:T(8,128)S(1)} custom-call(f32[288,128]{1,0:T(8,128)S(1)} %bitcast.22, f32[64,128]{1,0:T(8,128)S(1)} %bitcast.25, s32[64,128]{1,0:T(8,128)S(1)} %bitcast.34), custom_call_target="tpu_custom_call" | custom-call | tf_op jit(solution)/shard_map/fine_steps/pallas_call | solution.py:479
  21.1 0.0 collective-permute-done.message_ref
  21.2 0.1 quad_carry.1.carry_ref
  21.3 9.1 %collective-permute-start.1 = (f32[64,128]{1,0:T(8,128)S(1)}, f32[64,128]{1,0:T(8,128)S(1)}, u32[]{:S(2)}, u32[]{:S(2)}) collective-permute-start(f32[64,128]{1,0:T(8,128)S(1)} %quad_carry.1.carry_ref), channel_id=1, source_target_pairs={{0,32},{8,40},{16,48},{24,56},{32,0},{40,8},{48,16},{56,24},{64,96... | collective-permute-start | bytes 98312 | tf_op jit(solution)/shard_map/ppermute | solution.py:518
  30.4 2.2 %collective-permute-done.1.partner_ref = f32[64,128]{1,0:T(8,128)S(1)} collective-permute-done((f32[64,128]{1,0:T(8,128)S(1)}, f32[64,128]{1,0:T(8,128)S(1)}, u32[]{:S(2)}, u32[]{:S(2)}) %collective-permute-start.1) | collective-permute-done | bytes 32800 | tf_op jit(solution)/shard_map/ppermute | solution.py:518
  32.6 0.1 pair_carry.1
  32.7 8.4 %collective-permute-start.2 = (f32[64,128]{1,0:T(8,128)S(1)}, f32[64,128]{1,0:T(8,128)S(1)}, u32[]{:S(2)}, u32[]{:S(2)}) collective-permute-start(f32[64,128]{1,0:T(8,128)S(1)} %pair_carry.1), channel_id=1, source_target_pairs={{0,96},{8,104},{16,112},{24,120},{32,64},{40,72},{48,80},{56,88},{... | collective-permute-start | bytes 98312 | tf_op jit(solution)/shard_map/ppermute | solution.py:520
  41.1 1.9 %collective-permute-done.2.far_ref = f32[64,128]{1,0:T(8,128)S(1)} collective-permute-done((f32[64,128]{1,0:T(8,128)S(1)}, f32[64,128]{1,0:T(8,128)S(1)}, u32[]{:S(2)}, u32[]{:S(2)}) %collective-permute-start.2) | collective-permute-done | bytes 32800 | tf_op jit(solution)/shard_map/ppermute | solution.py:520
  43.0 0.2 slab_sums.1
  43.2 14.0 %all_to_all.11 = f32[64,4,128]{2,1,0:T(4,128)S(1)} all-to-all(f32[64,4,128]{2,1,0:T(4,128)S(1)} %bitcast.31), channel_id=1, replica_groups={{8,0,128,256,384,264,392,16,144,272,400,24,152,280,408,136},{40,32,160,..., dimensions={0} | all-to-all | bytes 262144 | tf_op jit(solution)/shard_map/all_to_all | solution.py:490
  57.2 0.8 %write_out.1 = f32[256,128]{1,0:T(8,128)} custom-call(f32[256,128]{1,0:T(8,128)S(1)} %bitcast.32), custom_call_target="tpu_custom_call" | custom-call | tf_op jit(solution)/shard_map/write_out/pallas_call | solution.py:344
  (1 shorter events, 0.0 us)
Async XLA Ops:
  0.9 16.1 %copy-start = (f32[8192]{0:T(1024)S(1)}, f32[8192]{0:T(1024)}, u32[]{:S(2)}) copy-start(f32[8192]{0:T(1024)} %param.6) | copy-start | bytes 98308
  0.9 16.1 %copy-start.1 = (s32[8192]{0:T(1024)S(1)}, s32[8192]{0:T(1024)}, u32[]{:S(2)}) copy-start(s32[8192]{0:T(1024)} %param.7) | copy-start | bytes 98308
  17.1 4.0 %collective-permute-start = (f32[24,128]{1,0:T(8,128)S(1)}, f32[24,128]{1,0:T(8,128)S(1)}, u32[]{:S(2)}, u32[]{:S(2)}) collective-permute-start(f32[24,128]{1,0:T(8,128)S(1)} %edge_rows.1), channel_id=1, source_target_pairs={{136,137},{137,136},{138,139},{139,138},{140,141},{141,140},{142,1... | collective-permute-start | bytes 36872 | tf_op jit(solution)/shard_map/ppermute | solution.py:513
  21.3 11.3 %collective-permute-start.1 = (f32[64,128]{1,0:T(8,128)S(1)}, f32[64,128]{1,0:T(8,128)S(1)}, u32[]{:S(2)}, u32[]{:S(2)}) collective-permute-start(f32[64,128]{1,0:T(8,128)S(1)} %quad_carry.1.carry_ref), channel_id=1, source_target_pairs={{0,32},{8,40},{16,48},{24,56},{32,0},{40,8},{48,16},{56,24},{64,96... | collective-permute-start | bytes 98312 | tf_op jit(solution)/shard_map/ppermute | solution.py:518
  32.7 10.3 %collective-permute-start.2 = (f32[64,128]{1,0:T(8,128)S(1)}, f32[64,128]{1,0:T(8,128)S(1)}, u32[]{:S(2)}, u32[]{:S(2)}) collective-permute-start(f32[64,128]{1,0:T(8,128)S(1)} %pair_carry.1), channel_id=1, source_target_pairs={{0,96},{8,104},{16,112},{24,120},{32,64},{40,72},{48,80},{56,88},{... | collective-permute-start | bytes 98312 | tf_op jit(solution)/shard_map/ppermute | solution.py:520

commit v11 on v10

--- a/solution.py
+++ b/solution.py
@@ -273,7 +273,7 @@
                 out_ref[slab_rows(half, r, k), :] = by_place(half, finals[half][r][k] - coarse[k])
 
 
-def end_kernel(term_ref, window_ref, message_ref, speed_ref, flag_ref, out_ref):
+def end_kernel(term_ref, window_ref, message_ref, speed_ref, flag_ref, out_ref, carry_ref):
     quad, chunk = place()
     first, final = chunk == 0, chunk == CHUNKS - 1
     out_ref[...] = term_ref[...]
@@ -317,6 +317,8 @@
                         made = pltpu.roll(finals[half][0][k], LANES // 2, 1) - coarse[half][k]
                         out_ref[rows, :] = jnp.where(near_end, by_place(half, made), term_ref[rows, :])
 
+    quad_carry(out_ref, speed_ref, carry_ref)
+
 
 def write_kernel(sums_ref, out_ref, sems):
     size = CHUNK * MODES
@@ -395,7 +397,7 @@
     return pl.ds((k * HALVES + half) * ROWS, ROWS)
 
 
-def quad_kernel(term_ref, speed_ref, carry_ref):
+def quad_carry(term_ref, speed_ref, carry_ref):
     quad, chunk = place()
     matrix = coarse_matrix(speed_ref, chunk)
     row = lax.broadcasted_iota(jnp.int32, (ROWS, LANES), 0)
@@ -476,11 +478,13 @@
 
 
 def on_device(kernel, name, rows, *operands):
+    whole = pl.BlockSpec(memory_space=pltpu.VMEM)
+    outs = [jax.ShapeDtypeStruct((n, LANES), jnp.float32) for n in (rows if isinstance(rows, tuple) else (rows,))]
     return pl.pallas_call(
         kernel,
-        out_shape=jax.ShapeDtypeStruct((rows, LANES), jnp.float32),
-        in_specs=[pl.BlockSpec(memory_space=pltpu.VMEM)] * len(operands),
-        out_specs=pl.BlockSpec(memory_space=pltpu.VMEM),
+        out_shape=outs if isinstance(rows, tuple) else outs[0],
+        in_specs=[whole] * len(operands),
+        out_specs=[whole] * len(outs) if isinstance(rows, tuple) else whole,
         compiler_params=pltpu.CompilerParams(vmem_limit_bytes=16 * 1024 * 1024),
         name=name,
     )(*operands)
@@ -512,9 +516,8 @@
     edge = on_device(edge_kernel, "edge_rows", COEFS + ROWS, windows, speed_rows, flag_rows)
     message = lax.ppermute(edge, ("tm", "space"), pairs)
     terms = on_device(fine_kernel, "fine_steps", rows * MODES, windows, speed_rows, flag_rows)
-    terms = on_device(end_kernel, "block_ends", rows * MODES, terms, windows, message, speed_rows, flag_rows)
     size = MODES * HALVES * ROWS
-    carry = on_device(quad_kernel, "quad_carry", size, terms, speed_rows)
+    terms, carry = on_device(end_kernel, "block_ends", (rows * MODES, size), terms, windows, message, speed_rows, flag_rows)
     partner = lax.ppermute(carry, "tm", [(c, c ^ QUAD) for c in range(slabs)])
     joint = on_device(pair_kernel, "pair_carry", size, carry, partner, speed_rows)
     far = lax.ppermute(joint, "tm", [(c, c ^ (3 * QUAD)) for c in range(slabs)])

time: 58.3 us -> 58.3 us (level)
    pallas_call x6 -> x5, Pallas kernels: 3.8 us -> 3.78 us  [on_device(): pl.pallas_call(kernel, out_shape=outs if isinstance(rows, tuple) else out...]
where the time goes in v11:
time: 58.3 us; the launch traced here: 58 us
  blocking collectives  30.1 us (52%)
  starting transfers between devices  18.2 us (31%)
  Pallas kernels  5.49 us (9%)
  waiting for transfers between devices  4.11 us (7%)
    all_to_all x2, blocking collectives, swap_blocks(): lax.all_to_all(x.reshape(-1, rows, LANES), 'tm', 0, 0, axis_index_groups=...  30.1 us
    ppermute x1, starting transfers between devices, body(): partner = lax.ppermute(carry, 'tm', [(c, c ^ QUAD) for c in range(slabs)])  9.1 us
    ppermute x1, starting transfers between devices, body(): far = lax.ppermute(joint, 'tm', [(c, c ^ 3 * QUAD) for c in range(slabs)])  8.42 us
    pallas_call x5, Pallas kernels, on_device(): pl.pallas_call(kernel, out_shape=outs if isinstance(rows, tuple) else out...  3.78 us
    ppermute x1, waiting for transfers between devices, body(): partner = lax.ppermute(carry, 'tm', [(c, c ^ QUAD) for c in range(slabs)])  2.23 us
    ppermute x1, waiting for transfers between devices, body(): far = lax.ppermute(joint, 'tm', [(c, c ^ 3 * QUAD) for c in range(slabs)])  1.88 us
  transfers between devices with their start and end apart: 3, of which 2 were waited for; matrix products, arithmetic and copies ran while one was open for 0% of the time, Pallas kernels for 6%

profile of v11, /device:TPU:2, one launch (start us, length us, event | category | flops | bytes accessed | tf_op | source)
XLA Modules:
  0.0 58.0 jit_solution(2565321957112866754)
XLA Ops:
  0.0 0.9 %windows.1 = f32[288,128]{1,0:T(8,128)S(1)} custom-call(f32[256,128]{1,0:T(8,128)} %bitcast.35, f32[256,128]{1,0:T(8,128)} %bitcast.36), custom_call_target="tpu_custom_call" | custom-call | tf_op jit(solution)/shard_map/windows/pallas_call | solution.py:167
  0.9 0.0 copy-start
  0.9 0.0 copy-start.1
  1.0 16.1 %all_to_all.10 = f32[144,2,128]{2,1,0:T(2,128)S(1)} all-to-all(f32[144,2,128]{2,1,0:T(2,128)S(1)} %bitcast.29), channel_id=1, replica_groups={{8,136,256,384,0,128,264,392,16,144,272,400,24,152,280,408},{40,168,288..., dimensions={0} | all-to-all | bytes 294912 | tf_op jit(solution)/shard_map/all_to_all | solution.py:494
  17.0 0.0 copy-done
  17.0 0.0 copy-done.1
  17.0 0.1 edge_rows.1
  17.1 0.7 %collective-permute-start = (f32[24,128]{1,0:T(8,128)S(1)}, f32[24,128]{1,0:T(8,128)S(1)}, u32[]{:S(2)}, u32[]{:S(2)}) collective-permute-start(f32[24,128]{1,0:T(8,128)S(1)} %edge_rows.1), channel_id=1, source_target_pairs={{136,137},{137,136},{138,139},{139,138},{140,141},{141,140},{142,1... | collective-permute-start | bytes 36872 | tf_op jit(solution)/shard_map/ppermute | solution.py:517
  17.8 3.3 %fine_steps.1.term_ref = f32[256,128]{1,0:T(8,128)S(1)} custom-call(f32[288,128]{1,0:T(8,128)S(1)} %bitcast.22, f32[64,128]{1,0:T(8,128)S(1)} %bitcast.25, s32[64,128]{1,0:T(8,128)S(1)} %bitcast.33), custom_call_target="tpu_custom_call" | custom-call | tf_op jit(solution)/shard_map/fine_steps/pallas_call | solution.py:483
  21.1 0.0 collective-permute-done.message_ref
  21.1 0.1 block_ends.1
  21.2 9.1 %collective-permute-start.1 = (f32[64,128]{1,0:T(8,128)S(1)}, f32[64,128]{1,0:T(8,128)S(1)}, u32[]{:S(2)}, u32[]{:S(2)}) collective-permute-start(f32[64,128]{1,0:T(8,128)S(1)} %get-tuple-element.8.carry_ref), channel_id=1, source_target_pairs={{0,32},{8,40},{16,48},{24,56},{32,0},{40,8},{48,16},{56,24},{64,96... | collective-permute-start | bytes 98312 | tf_op jit(solution)/shard_map/ppermute | solution.py:521
  30.3 2.2 %collective-permute-done.1.partner_ref = f32[64,128]{1,0:T(8,128)S(1)} collective-permute-done((f32[64,128]{1,0:T(8,128)S(1)}, f32[64,128]{1,0:T(8,128)S(1)}, u32[]{:S(2)}, u32[]{:S(2)}) %collective-permute-start.1) | collective-permute-done | bytes 32800 | tf_op jit(solution)/shard_map/ppermute | solution.py:521
  32.6 0.1 pair_carry.1
  32.7 8.4 %collective-permute-start.2 = (f32[64,128]{1,0:T(8,128)S(1)}, f32[64,128]{1,0:T(8,128)S(1)}, u32[]{:S(2)}, u32[]{:S(2)}) collective-permute-start(f32[64,128]{1,0:T(8,128)S(1)} %pair_carry.1), channel_id=1, source_target_pairs={{0,96},{8,104},{16,112},{24,120},{32,64},{40,72},{48,80},{56,88},{... | collective-permute-start | bytes 98312 | tf_op jit(solution)/shard_map/ppermute | solution.py:523
  41.1 1.9 %collective-permute-done.2.far_ref = f32[64,128]{1,0:T(8,128)S(1)} collective-permute-done((f32[64,128]{1,0:T(8,128)S(1)}, f32[64,128]{1,0:T(8,128)S(1)}, u32[]{:S(2)}, u32[]{:S(2)}) %collective-permute-start.2) | collective-permute-done | bytes 32800 | tf_op jit(solution)/shard_map/ppermute | solution.py:523
  43.0 0.2 slab_sums.1
  43.2 14.0 %all_to_all.11 = f32[64,4,128]{2,1,0:T(4,128)S(1)} all-to-all(f32[64,4,128]{2,1,0:T(4,128)S(1)} %bitcast.30), channel_id=1, replica_groups={{8,0,128,256,384,264,392,16,144,272,400,24,152,280,408,136},{40,32,160,..., dimensions={0} | all-to-all | bytes 262144 | tf_op jit(solution)/shard_map/all_to_all | solution.py:494
  57.2 0.8 %write_out.1 = f32[256,128]{1,0:T(8,128)} custom-call(f32[256,128]{1,0:T(8,128)S(1)} %bitcast.31), custom_call_target="tpu_custom_call" | custom-call | tf_op jit(solution)/shard_map/write_out/pallas_call | solution.py:346
Async XLA Ops:
  0.9 16.1 %copy-start = (f32[8192]{0:T(1024)S(1)}, f32[8192]{0:T(1024)}, u32[]{:S(2)}) copy-start(f32[8192]{0:T(1024)} %param.6) | copy-start | bytes 98308
  0.9 16.1 %copy-start.1 = (s32[8192]{0:T(1024)S(1)}, s32[8192]{0:T(1024)}, u32[]{:S(2)}) copy-start(s32[8192]{0:T(1024)} %param.7) | copy-start | bytes 98308
  17.1 4.0 %collective-permute-start = (f32[24,128]{1,0:T(8,128)S(1)}, f32[24,128]{1,0:T(8,128)S(1)}, u32[]{:S(2)}, u32[]{:S(2)}) collective-permute-start(f32[24,128]{1,0:T(8,128)S(1)} %edge_rows.1), channel_id=1, source_target_pairs={{136,137},{137,136},{138,139},{139,138},{140,141},{141,140},{142,1... | collective-permute-start | bytes 36872 | tf_op jit(solution)/shard_map/ppermute | solution.py:517
  21.2 11.3 %collective-permute-start.1 = (f32[64,128]{1,0:T(8,128)S(1)}, f32[64,128]{1,0:T(8,128)S(1)}, u32[]{:S(2)}, u32[]{:S(2)}) collective-permute-start(f32[64,128]{1,0:T(8,128)S(1)} %get-tuple-element.8.carry_ref), channel_id=1, source_target_pairs={{0,32},{8,40},{16,48},{24,56},{32,0},{40,8},{48,16},{56,24},{64,96... | collective-permute-start | bytes 98312 | tf_op jit(solution)/shard_map/ppermute | solution.py:521
  32.7 10.3 %collective-permute-start.2 = (f32[64,128]{1,0:T(8,128)S(1)}, f32[64,128]{1,0:T(8,128)S(1)}, u32[]{:S(2)}, u32[]{:S(2)}) collective-permute-start(f32[64,128]{1,0:T(8,128)S(1)} %pair_carry.1), channel_id=1, source_target_pairs={{0,96},{8,104},{16,112},{24,120},{32,64},{40,72},{48,80},{56,88},{... | collective-permute-start | bytes 98312 | tf_op jit(solution)/shard_map/ppermute | solution.py:523

commit v12 on v10

--- a/solution.py
+++ b/solution.py
@@ -108,7 +108,7 @@
     return z // QUAD, jnp.where(even_block(), chunk, CHUNKS - 1 - chunk)
 
 
-COPIES = 4
+COPIES = 8
 
 
 def window_kernel(slabs, guess_ref, initial_ref, out_ref, state, sems):

time: 58.3 us -> 58.5 us (level)
  no operation moved by 1% of the time
where the time goes in v12:
time: 58.5 us; the launch traced here: 58.1 us
  blocking collectives  30.1 us (51%)
  starting transfers between devices  18.2 us (31%)
  Pallas kernels  5.58 us (10%)
  waiting for transfers between devices  4.11 us (7%)
    all_to_all x2, blocking collectives, swap_blocks(): lax.all_to_all(x.reshape(-1, rows, LANES), 'tm', 0, 0, axis_index_groups=...  30.1 us
    ppermute x1, starting transfers between devices, body(): partner = lax.ppermute(carry, 'tm', [(c, c ^ QUAD) for c in range(slabs)])  9.1 us
    ppermute x1, starting transfers between devices, body(): far = lax.ppermute(joint, 'tm', [(c, c ^ 3 * QUAD) for c in range(slabs)])  8.42 us
    pallas_call x6, Pallas kernels, on_device(): pl.pallas_call(kernel, out_shape=jax.ShapeDtypeStruct((rows, LANES), jnp....  3.8 us
    ppermute x1, waiting for transfers between devices, body(): partner = lax.ppermute(carry, 'tm', [(c, c ^ QUAD) for c in range(slabs)])  2.23 us
    ppermute x1, waiting for transfers between devices, body(): far = lax.ppermute(joint, 'tm', [(c, c ^ 3 * QUAD) for c in range(slabs)])  1.88 us
  transfers between devices with their start and end apart: 3, of which 2 were waited for; matrix products, arithmetic and copies ran while one was open for 0% of the time, Pallas kernels for 6%

profile of v12, /device:TPU:2, one launch (start us, length us, event | category | flops | bytes accessed | tf_op | source)
XLA Modules:
  0.0 58.1 jit_solution(110251940105657432)
XLA Ops:
  0.0 1.0 %windows.1 = f32[288,128]{1,0:T(8,128)S(1)} custom-call(f32[256,128]{1,0:T(8,128)} %bitcast.36, f32[256,128]{1,0:T(8,128)} %bitcast.37), custom_call_target="tpu_custom_call" | custom-call | tf_op jit(solution)/shard_map/windows/pallas_call | solution.py:167
  1.0 0.0 copy-start
  1.0 0.0 copy-start.1
  1.0 16.1 %all_to_all.10 = f32[144,2,128]{2,1,0:T(2,128)S(1)} all-to-all(f32[144,2,128]{2,1,0:T(2,128)S(1)} %bitcast.30), channel_id=1, replica_groups={{8,136,256,384,0,128,264,392,16,144,272,400,24,152,280,408},{40,168,288..., dimensions={0} | all-to-all | bytes 294912 | tf_op jit(solution)/shard_map/all_to_all | solution.py:490
  17.1 0.0 copy-done
  17.1 0.0 copy-done.1
  17.1 0.1 edge_rows.1
  17.2 0.7 %collective-permute-start = (f32[24,128]{1,0:T(8,128)S(1)}, f32[24,128]{1,0:T(8,128)S(1)}, u32[]{:S(2)}, u32[]{:S(2)}) collective-permute-start(f32[24,128]{1,0:T(8,128)S(1)} %edge_rows.1), channel_id=1, source_target_pairs={{136,137},{137,136},{138,139},{139,138},{140,141},{141,140},{142,1... | collective-permute-start | bytes 36872 | tf_op jit(solution)/shard_map/ppermute | solution.py:513
  17.9 3.3 %fine_steps.1.term_ref = f32[256,128]{1,0:T(8,128)S(1)} custom-call(f32[288,128]{1,0:T(8,128)S(1)} %bitcast.22, f32[64,128]{1,0:T(8,128)S(1)} %bitcast.25, s32[64,128]{1,0:T(8,128)S(1)} %bitcast.34), custom_call_target="tpu_custom_call" | custom-call | tf_op jit(solution)/shard_map/fine_steps/pallas_call | solution.py:479
  21.2 0.0 collective-permute-done.message_ref
  21.2 0.1 quad_carry.1.carry_ref
  21.3 9.1 %collective-permute-start.1 = (f32[64,128]{1,0:T(8,128)S(1)}, f32[64,128]{1,0:T(8,128)S(1)}, u32[]{:S(2)}, u32[]{:S(2)}) collective-permute-start(f32[64,128]{1,0:T(8,128)S(1)} %quad_carry.1.carry_ref), channel_id=1, source_target_pairs={{0,32},{8,40},{16,48},{24,56},{32,0},{40,8},{48,16},{56,24},{64,96... | collective-permute-start | bytes 98312 | tf_op jit(solution)/shard_map/ppermute | solution.py:518
  30.4 2.2 %collective-permute-done.1.partner_ref = f32[64,128]{1,0:T(8,128)S(1)} collective-permute-done((f32[64,128]{1,0:T(8,128)S(1)}, f32[64,128]{1,0:T(8,128)S(1)}, u32[]{:S(2)}, u32[]{:S(2)}) %collective-permute-start.1) | collective-permute-done | bytes 32800 | tf_op jit(solution)/shard_map/ppermute | solution.py:518
  32.7 0.1 pair_carry.1
  32.8 8.4 %collective-permute-start.2 = (f32[64,128]{1,0:T(8,128)S(1)}, f32[64,128]{1,0:T(8,128)S(1)}, u32[]{:S(2)}, u32[]{:S(2)}) collective-permute-start(f32[64,128]{1,0:T(8,128)S(1)} %pair_carry.1), channel_id=1, source_target_pairs={{0,96},{8,104},{16,112},{24,120},{32,64},{40,72},{48,80},{56,88},{... | collective-permute-start | bytes 98312 | tf_op jit(solution)/shard_map/ppermute | solution.py:520
  41.2 1.9 %collective-permute-done.2.far_ref = f32[64,128]{1,0:T(8,128)S(1)} collective-permute-done((f32[64,128]{1,0:T(8,128)S(1)}, f32[64,128]{1,0:T(8,128)S(1)}, u32[]{:S(2)}, u32[]{:S(2)}) %collective-permute-start.2) | collective-permute-done | bytes 32800 | tf_op jit(solution)/shard_map/ppermute | solution.py:520
  43.1 0.2 slab_sums.1
  43.3 14.0 %all_to_all.11 = f32[64,4,128]{2,1,0:T(4,128)S(1)} all-to-all(f32[64,4,128]{2,1,0:T(4,128)S(1)} %bitcast.31), channel_id=1, replica_groups={{8,0,128,256,384,264,392,16,144,272,400,24,152,280,408,136},{40,32,160,..., dimensions={0} | all-to-all | bytes 262144 | tf_op jit(solution)/shard_map/all_to_all | solution.py:490
  57.3 0.8 %write_out.1 = f32[256,128]{1,0:T(8,128)} custom-call(f32[256,128]{1,0:T(8,128)S(1)} %bitcast.32), custom_call_target="tpu_custom_call" | custom-call | tf_op jit(solution)/shard_map/write_out/pallas_call | solution.py:344
  (1 shorter events, 0.0 us)
Async XLA Ops:
  1.0 16.1 %copy-start = (f32[8192]{0:T(1024)S(1)}, f32[8192]{0:T(1024)}, u32[]{:S(2)}) copy-start(f32[8192]{0:T(1024)} %param.6) | copy-start | bytes 98308
  1.0 16.1 %copy-start.1 = (s32[8192]{0:T(1024)S(1)}, s32[8192]{0:T(1024)}, u32[]{:S(2)}) copy-start(s32[8192]{0:T(1024)} %param.7) | copy-start | bytes 98308
  17.2 4.0 %collective-permute-start = (f32[24,128]{1,0:T(8,128)S(1)}, f32[24,128]{1,0:T(8,128)S(1)}, u32[]{:S(2)}, u32[]{:S(2)}) collective-permute-start(f32[24,128]{1,0:T(8,128)S(1)} %edge_rows.1), channel_id=1, source_target_pairs={{136,137},{137,136},{138,139},{139,138},{140,141},{141,140},{142,1... | collective-permute-start | bytes 36872 | tf_op jit(solution)/shard_map/ppermute | solution.py:513
  21.3 11.3 %collective-permute-start.1 = (f32[64,128]{1,0:T(8,128)S(1)}, f32[64,128]{1,0:T(8,128)S(1)}, u32[]{:S(2)}, u32[]{:S(2)}) collective-permute-start(f32[64,128]{1,0:T(8,128)S(1)} %quad_carry.1.carry_ref), channel_id=1, source_target_pairs={{0,32},{8,40},{16,48},{24,56},{32,0},{40,8},{48,16},{56,24},{64,96... | collective-permute-start | bytes 98312 | tf_op jit(solution)/shard_map/ppermute | solution.py:518
  32.8 10.3 %collective-permute-start.2 = (f32[64,128]{1,0:T(8,128)S(1)}, f32[64,128]{1,0:T(8,128)S(1)}, u32[]{:S(2)}, u32[]{:S(2)}) collective-permute-start(f32[64,128]{1,0:T(8,128)S(1)} %pair_carry.1), channel_id=1, source_target_pairs={{0,96},{8,104},{16,112},{24,120},{32,64},{40,72},{48,80},{56,88},{... | collective-permute-start | bytes 98312 | tf_op jit(solution)/shard_map/ppermute | solution.py:520
